TPU v7x, 32 devices: a whole 2x2x4 slice. The times are simulated.
32 devices in a mesh: dp: 8 (over z, core), seq: 4 (over y, x).
Axes of the slice: x: 2, y: 2, z: 4, core: 2. Of those that a mesh axis runs over, the one named last changes fastest.
Arguments:
- inputs: bfloat16 [16, 1024, 512], P('dp', 'seq'), may hold values from -3 to 3
- segment_ids: int32 [16, 1024], P('dp', 'seq'), may hold values from 0 to 3, never falling along the last dimension, each value on 1 to 800 neighbouring positions
- cotangent: bfloat16 [16, 1024, 512], P('dp', 'seq'), may hold values from -6 to 6
- norm_gain: bfloat16 [4, 512], P(None, 'seq'), may hold values from 0.5 to 1.5
- norm_bias: bfloat16 [4, 512], P(None, 'seq'), may hold values from -1.5 to 1.5
- glu_weight: bfloat16 [512, 1024], P('seq'), may hold values from -0.25 to 0.25
- left_weight: bfloat16 [512, 2048], P('seq'), may hold values from -0.25 to 0.25
- conv_weight: bfloat16 [3, 512, 256], P(None, 'seq'), may hold values from -0.75 to 0.75
- mid_gain: bfloat16 [2048], P('seq'), may hold values from 0.5 to 1.5
- mid_bias: bfloat16 [2048], P('seq'), may hold values from -1.5 to 1.5
- depth_weight: bfloat16 [9, 2048], P(None, 'seq'), may hold values from -2 to 2
- point_weight: bfloat16 [2048, 512], P('seq'), may hold values from -0.125 to 0.125
- qkv_weight: bfloat16 [512, 1536], P('seq'), may hold values from -0.25 to 0.25
- out_weight: bfloat16 [512, 512], P('seq'), may hold values from -1 to 1
- ffn_in: bfloat16 [512, 2048], P('seq'), may hold values from -0.25 to 0.25
- ffn_out: bfloat16 [2048, 512], P('seq'), may hold values from -0.1875 to 0.1875
Outputs:
- output: float32 [16, 1024, 512], P('dp', 'seq')
- input_grad: float32 [16, 1024, 512], P('dp', 'seq')
- grad_norm_gain: float32 [4, 512], P(None, 'seq')
- grad_norm_bias: float32 [4, 512], P(None, 'seq')
- grad_glu_weight: float32 [512, 1024], P('seq')
- grad_left_weight: float32 [512, 2048], P('seq')
- grad_conv_weight: float32 [3, 512, 256], P(None, 'seq')
- grad_mid_gain: float32 [2048], P('seq')
- grad_mid_bias: float32 [2048], P('seq')
- grad_depth_weight: float32 [9, 2048], P(None, 'seq')
- grad_point_weight: float32 [2048, 512], P('seq')
- grad_qkv_weight: float32 [512, 1536], P('seq')
- grad_out_weight: float32 [512, 512], P('seq')
- grad_ffn_in: float32 [512, 2048], P('seq')
- grad_ffn_out: float32 [2048, 512], P('seq')
Inputs may be any that keep to these rules, and one draw needn't show every extreme that they name: `segment_ids`: along each sequence of 1024 tokens the segment ids never fall and take every value from 0 to 3; each document has 1 to 800 tokens, and one document of every sequence has exactly 800.
All inputs are finite; a program needn't handle non-finite values.
Results may differ from a plain program's by a relative error of at most 0.02.
Values may be sent and summed in bfloat16 or wider, within the bound.
A program may use at most 192 MiB of HBM per device.

v0:
```python
import math

import jax
import jax.numpy as jnp
from jax import lax
from jax.sharding import PartitionSpec as P

HEADS = 8


EPS = 1e-06
NEG = -1000000000.0


def extended(cells, sides, width):
    for axis, dim in sides:
        count = lax.axis_size(axis)
        ends = count - 1
        head = lax.slice_in_dim(cells, 0, width, axis=dim)
        tail = lax.slice_in_dim(cells, cells.shape[dim] - width, cells.shape[dim], axis=dim)
        cells = jnp.concatenate(
            [
                lax.ppermute(tail, axis, [(i, (i + 1) % count) for i in range(ends)]),
                cells,
                lax.ppermute(head, axis, [((i + 1) % count, i) for i in range(ends)]),
            ],
            axis=dim,
        )
    return cells


def layer_norm(values, gain, bias):
    average = jnp.mean(values, axis=-1, keepdims=True)
    centred = values - average
    spread = jnp.mean(centred * centred, axis=-1, keepdims=True)
    return centred * lax.rsqrt(spread + EPS) * gain + bias


def gated(pre_act):
    split_at = pre_act.shape[-1] // 2
    return pre_act[..., :split_at] * jax.nn.sigmoid(pre_act[..., split_at:])


def smooth_act(values):
    return jax.nn.gelu(values)


def product(left, right):
    return jnp.dot(left, right, preferred_element_type=jnp.float32)


def product_rows(left, right):
    return jnp.einsum("ra,rb->ab", left, right, preferred_element_type=jnp.float32)


def product_back(left, right):
    return jnp.einsum("rb,ab->ra", left, right, preferred_element_type=jnp.float32)


def masked_scores(queries, keys_in, query_segs, key_segs):
    scores = jnp.einsum("bqhd,bkhd->bhqk", queries, keys_in, preferred_element_type=jnp.float32)
    same_doc = (query_segs[:, :, None] == key_segs[:, None, :])[:, None]
    return jnp.where(same_doc, scores, NEG)


def local(
    inputs,
    segment_ids,
    cotangent,
    norm_gain,
    norm_bias,
    glu_weight,
    left_weight,
    conv_weight,
    mid_gain,
    mid_bias,
    depth_weight,
    point_weight,
    qkv_weight,
    out_weight,
    ffn_in,
    ffn_out,
):
    seq_count, span_len, model_width = inputs.shape
    row_count = seq_count * span_len
    head_dim = model_width // HEADS
    score_scale = 1.0 / math.sqrt(head_dim)
    gathered = (
        lax.all_gather(norm_gain, "seq", axis=1, tiled=True),
        lax.all_gather(norm_bias, "seq", axis=1, tiled=True),
        lax.all_gather(glu_weight, "seq", axis=0, tiled=True),
        lax.all_gather(left_weight, "seq", axis=0, tiled=True),
        lax.all_gather(conv_weight, "seq", axis=1, tiled=True),
        lax.all_gather(mid_gain, "seq", axis=0, tiled=True),
        lax.all_gather(mid_bias, "seq", axis=0, tiled=True),
        lax.all_gather(depth_weight, "seq", axis=1, tiled=True),
        lax.all_gather(point_weight, "seq", axis=0, tiled=True),
        lax.all_gather(qkv_weight, "seq", axis=0, tiled=True),
        lax.all_gather(out_weight, "seq", axis=0, tiled=True),
        lax.all_gather(ffn_in, "seq", axis=0, tiled=True),
        lax.all_gather(ffn_out, "seq", axis=0, tiled=True),
    )
    (
        gains_all,
        biases_all,
        w_glu,
        w_left,
        w_conv,
        gain_mid,
        bias_mid,
        w_depth,
        w_point,
        w_qkv,
        w_out,
        w_inner,
        w_outer,
    ) = gathered
    hidden_width = w_inner.shape[1]
    half_width = w_conv.shape[2]
    gains = gains_all.astype(jnp.float32)
    biases = biases_all.astype(jnp.float32)
    depth = w_depth.astype(jnp.float32)
    full_segs = lax.all_gather(segment_ids, "seq", axis=1, tiled=True)
    length = full_segs.shape[1]
    padded_segs = jnp.pad(full_segs, ((0, 0), (4, 4)), constant_values=-1)
    own_start = lax.axis_index("seq") * span_len
    nearby = lax.dynamic_slice_in_dim(padded_segs, own_start, span_len + 8, 1)

    def tap_masks(radius):
        return jnp.stack(
            [
                nearby[:, 4 + offset : 4 + offset + span_len] == segment_ids
                for offset in range(-radius, radius + 1)
            ],
            0,
        )[..., None]

    narrow_masks = tap_masks(1).astype(jnp.bfloat16)
    wide_masks = tap_masks(4).astype(jnp.float32)
    stream = inputs.astype(jnp.float32).reshape(row_count, model_width)
    normed_glu, norm_glu_back = jax.vjp(layer_norm, stream, gains[0], biases[0])
    act1 = normed_glu.astype(jnp.bfloat16)
    pre1 = product(act1, w_glu)
    glu_out, glu_back = jax.vjp(gated, pre1)
    stream1 = stream + glu_out
    normed_branch, norm_branch_back = jax.vjp(layer_norm, stream1, gains[1], biases[1])
    act2 = normed_branch.astype(jnp.bfloat16)
    left_pre = product(act2, w_left)
    act2_rim = extended(act2.reshape(seq_count, span_len, model_width), (("seq", 1),), 1)
    taps_narrow = [
        (act2_rim[:, tap : tap + span_len] * narrow_masks[tap]).reshape(row_count, model_width)
        for tap in range(3)
    ]
    right_pre = (
        product(taps_narrow[0], w_conv[0])
        + product(taps_narrow[1], w_conv[1])
        + product(taps_narrow[2], w_conv[2])
    )
    left_act, left_act_back = jax.vjp(smooth_act, left_pre)
    right_act, right_act_back = jax.vjp(smooth_act, right_pre)
    middle = left_act + jnp.pad(right_act, ((0, 0), (0, hidden_width - half_width)))
    normed_mid, norm_mid_back = jax.vjp(
        layer_norm, middle, gain_mid.astype(jnp.float32), bias_mid.astype(jnp.float32)
    )
    act3_rim = extended(
        normed_mid.astype(jnp.bfloat16).reshape(seq_count, span_len, hidden_width), (("seq", 1),), 4
    )
    separable = sum(
        (act3_rim[:, tap : tap + span_len] * wide_masks[tap] * depth[tap] for tap in range(9))
    )
    sep_hidden = separable.astype(jnp.bfloat16).reshape(row_count, hidden_width)
    sep_out = product(sep_hidden, w_point)
    stream2 = stream1 + sep_out
    normed_attn, norm_attn_back = jax.vjp(layer_norm, stream2, gains[2], biases[2])
    act4 = normed_attn.astype(jnp.bfloat16)
    qkv = product(act4, w_qkv)
    queries = (qkv[:, :model_width] * score_scale).astype(jnp.bfloat16)
    keys_values = qkv[:, model_width:].astype(jnp.bfloat16)
    att_seqs = min(seq_count, max(1, 512 // span_len))
    blocks = seq_count // att_seqs
    query_blocks = queries.reshape(blocks, att_seqs, span_len, HEADS, head_dim)
    local_kv = keys_values.reshape(blocks, att_seqs, span_len, 2 * model_width)
    qseg_blocks = segment_ids.reshape(blocks, att_seqs, span_len)
    kseg_blocks = full_segs.reshape(blocks, att_seqs, length)

    def split_kv(whole_kv):
        keys_in = whole_kv[..., :model_width].reshape(att_seqs, length, HEADS, head_dim)
        values_in = whole_kv[..., model_width:].reshape(att_seqs, length, HEADS, head_dim)
        return (keys_in, values_in)

    def attend(entry):
        query_part, kv_part, query_segs, key_segs = entry
        whole_kv = lax.all_gather(kv_part, "seq", axis=1, tiled=True)
        keys_in, values_in = split_kv(whole_kv)
        scores = masked_scores(query_part, keys_in, query_segs, key_segs)
        row_max = jnp.max(scores, axis=-1, keepdims=True)
        exponent = jnp.exp(scores - row_max)
        totals = jnp.sum(exponent, axis=-1, keepdims=True)
        probabilities = (exponent / totals).astype(jnp.bfloat16)
        context = jnp.einsum(
            "bhqk,bkhd->bqhd", probabilities, values_in, preferred_element_type=jnp.float32
        )
        return (context.astype(jnp.bfloat16), row_max[..., 0] + jnp.log(totals[..., 0]), whole_kv)

    contexts, log_totals, kept_kv = lax.map(
        attend, (query_blocks, local_kv, qseg_blocks, kseg_blocks)
    )
    context_rows = contexts.reshape(row_count, model_width)
    attn_out = product(context_rows, w_out)
    stream3 = stream2 + attn_out
    normed_ffn, norm_ffn_back = jax.vjp(layer_norm, stream3, gains[3], biases[3])
    act5 = normed_ffn.astype(jnp.bfloat16)
    inner_pre = product(act5, w_inner)
    inner_act, inner_act_back = jax.vjp(smooth_act, inner_pre)
    hidden = inner_act.astype(jnp.bfloat16)
    feed_out = product(hidden, w_outer)
    stream4 = stream3 + feed_out
    output = stream4.reshape(seq_count, span_len, model_width)
    grad4 = cotangent.astype(jnp.float32).reshape(row_count, model_width)
    grad_feed = grad4.astype(jnp.bfloat16)
    g_outer = product_rows(hidden, grad_feed)
    d_inner = inner_act_back(product_back(grad_feed, w_outer))[0].astype(jnp.bfloat16)
    g_inner = product_rows(act5, d_inner)
    d_act5, g_gain_ffn, g_bias_ffn = norm_ffn_back(product_back(d_inner, w_inner))
    grad3 = grad4 + d_act5
    grad_attn = grad3.astype(jnp.bfloat16)
    g_out = product_rows(context_rows, grad_attn)
    d_context = (
        product_back(grad_attn, w_out)
        .astype(jnp.bfloat16)
        .reshape(blocks, att_seqs, span_len, HEADS, head_dim)
    )

    def attend_back(entry):
        query_part, whole_kv, query_segs, key_segs, log_total, d_part = entry
        keys_in, values_in = split_kv(whole_kv)
        scores = masked_scores(query_part, keys_in, query_segs, key_segs)
        probabilities = jnp.exp(scores - log_total[..., None])
        d_probs = jnp.einsum(
            "bqhd,bkhd->bhqk", d_part, values_in, preferred_element_type=jnp.float32
        )
        row_delta = jnp.sum(probabilities * d_probs, axis=-1)
        d_scores = (probabilities * (d_probs - row_delta[..., None])).astype(jnp.bfloat16)
        d_queries = jnp.einsum(
            "bhqk,bkhd->bqhd", d_scores, keys_in, preferred_element_type=jnp.float32
        )
        d_keys = jnp.einsum(
            "bhqk,bqhd->bkhd", d_scores, query_part, preferred_element_type=jnp.float32
        )
        d_values = jnp.einsum(
            "bhqk,bqhd->bkhd",
            probabilities.astype(jnp.bfloat16),
            d_part,
            preferred_element_type=jnp.float32,
        )
        owned_keys, owned_values = (
            lax.psum_scatter(
                d_keys.reshape(att_seqs, length, model_width).astype(jnp.bfloat16),
                "seq",
                scatter_dimension=1,
                tiled=True,
            ).astype(jnp.float32),
            lax.psum_scatter(
                d_values.reshape(att_seqs, length, model_width).astype(jnp.bfloat16),
                "seq",
                scatter_dimension=1,
                tiled=True,
            ).astype(jnp.float32),
        )
        return (d_queries, owned_keys, owned_values)

    d_query_all, d_key_all, d_value_all = lax.map(
        attend_back, (query_blocks, kept_kv, qseg_blocks, kseg_blocks, log_totals, d_context)
    )
    d_qkv = jnp.concatenate(
        [
            d_query_all.reshape(row_count, model_width) * score_scale,
            d_key_all.reshape(row_count, model_width),
            d_value_all.reshape(row_count, model_width),
        ],
        1,
    ).astype(jnp.bfloat16)
    g_qkv = product_rows(act4, d_qkv)
    d_act4, g_gain_attn, g_bias_attn = norm_attn_back(product_back(d_qkv, w_qkv))
    grad2 = grad3 + d_act4
    grad_sep = grad2.astype(jnp.bfloat16)
    g_point = product_rows(sep_hidden, grad_sep)
    d_sep = (
        product_back(grad_sep, w_point)
        .astype(jnp.bfloat16)
        .reshape(seq_count, span_len, hidden_width)
    )
    g_depth = jnp.stack(
        [
            jnp.sum(act3_rim[:, tap : tap + span_len] * wide_masks[tap] * d_sep, axis=(0, 1))
            for tap in range(9)
        ],
        0,
    )
    d_sep_rim = extended(d_sep, (("seq", 1),), 4)
    d_act3 = sum(
        (
            d_sep_rim[:, 8 - tap : 8 - tap + span_len] * wide_masks[8 - tap] * depth[tap]
            for tap in range(9)
        )
    )
    d_middle, g_gain_mid, g_bias_mid = norm_mid_back(d_act3.reshape(row_count, hidden_width))
    d_left = left_act_back(d_middle)[0].astype(jnp.bfloat16)
    d_right = right_act_back(d_middle[:, :half_width])[0].astype(jnp.bfloat16)
    g_left = product_rows(act2, d_left)
    g_conv = jnp.stack([product_rows(taps_narrow[tap], d_right) for tap in range(3)], 0)
    d_right_rim = extended(d_right.reshape(seq_count, span_len, half_width), (("seq", 1),), 1)
    d_act2 = product_back(d_left, w_left)
    for tap in range(3):
        moved = (d_right_rim[:, 2 - tap : 2 - tap + span_len] * narrow_masks[2 - tap]).reshape(
            row_count, half_width
        )
        d_act2 = d_act2 + product_back(moved, w_conv[tap])
    d_branch_in, g_gain_branch, g_bias_branch = norm_branch_back(d_act2)
    grad1 = grad2 + d_branch_in
    d_pre1 = glu_back(grad1)[0].astype(jnp.bfloat16)
    g_glu = product_rows(act1, d_pre1)
    d_glu_in, g_gain_glu, g_bias_glu = norm_glu_back(product_back(d_pre1, w_glu))
    input_grad = (grad1 + d_glu_in).reshape(seq_count, span_len, model_width)
    g_norm_gain = jnp.stack([g_gain_glu, g_gain_branch, g_gain_attn, g_gain_ffn], 0)
    g_norm_bias = jnp.stack([g_bias_glu, g_bias_branch, g_bias_attn, g_bias_ffn], 0)
    owned = (
        lax.psum_scatter(
            g_norm_gain.astype(jnp.bfloat16), "seq", scatter_dimension=1, tiled=True
        ).astype(jnp.float32),
        lax.psum_scatter(
            g_norm_bias.astype(jnp.bfloat16), "seq", scatter_dimension=1, tiled=True
        ).astype(jnp.float32),
        lax.psum_scatter(g_glu.astype(jnp.bfloat16), "seq", scatter_dimension=0, tiled=True).astype(
            jnp.float32
        ),
        lax.psum_scatter(
            g_left.astype(jnp.bfloat16), "seq", scatter_dimension=0, tiled=True
        ).astype(jnp.float32),
        lax.psum_scatter(
            g_conv.astype(jnp.bfloat16), "seq", scatter_dimension=1, tiled=True
        ).astype(jnp.float32),
        lax.psum_scatter(
            g_gain_mid.astype(jnp.bfloat16), "seq", scatter_dimension=0, tiled=True
        ).astype(jnp.float32),
        lax.psum_scatter(
            g_bias_mid.astype(jnp.bfloat16), "seq", scatter_dimension=0, tiled=True
        ).astype(jnp.float32),
        lax.psum_scatter(
            g_depth.astype(jnp.bfloat16), "seq", scatter_dimension=1, tiled=True
        ).astype(jnp.float32),
        lax.psum_scatter(
            g_point.astype(jnp.bfloat16), "seq", scatter_dimension=0, tiled=True
        ).astype(jnp.float32),
        lax.psum_scatter(g_qkv.astype(jnp.bfloat16), "seq", scatter_dimension=0, tiled=True).astype(
            jnp.float32
        ),
        lax.psum_scatter(g_out.astype(jnp.bfloat16), "seq", scatter_dimension=0, tiled=True).astype(
            jnp.float32
        ),
        lax.psum_scatter(
            g_inner.astype(jnp.bfloat16), "seq", scatter_dimension=0, tiled=True
        ).astype(jnp.float32),
        lax.psum_scatter(
            g_outer.astype(jnp.bfloat16), "seq", scatter_dimension=0, tiled=True
        ).astype(jnp.float32),
    )
    summed = (
        lax.psum(owned[0].astype(jnp.bfloat16), "dp").astype(jnp.float32),
        lax.psum(owned[1].astype(jnp.bfloat16), "dp").astype(jnp.float32),
        lax.psum(owned[2].astype(jnp.bfloat16), "dp").astype(jnp.float32),
        lax.psum(owned[3].astype(jnp.bfloat16), "dp").astype(jnp.float32),
        lax.psum(owned[4].astype(jnp.bfloat16), "dp").astype(jnp.float32),
        lax.psum(owned[5].astype(jnp.bfloat16), "dp").astype(jnp.float32),
        lax.psum(owned[6].astype(jnp.bfloat16), "dp").astype(jnp.float32),
        lax.psum(owned[7].astype(jnp.bfloat16), "dp").astype(jnp.float32),
        lax.psum(owned[8].astype(jnp.bfloat16), "dp").astype(jnp.float32),
        lax.psum(owned[9].astype(jnp.bfloat16), "dp").astype(jnp.float32),
        lax.psum(owned[10].astype(jnp.bfloat16), "dp").astype(jnp.float32),
        lax.psum(owned[11].astype(jnp.bfloat16), "dp").astype(jnp.float32),
        lax.psum(owned[12].astype(jnp.bfloat16), "dp").astype(jnp.float32),
    )
    return (
        output,
        input_grad,
        summed[0],
        summed[1],
        summed[2],
        summed[3],
        summed[4],
        summed[5],
        summed[6],
        summed[7],
        summed[8],
        summed[9],
        summed[10],
        summed[11],
        summed[12],
    )


def solution(mesh):
    in_specs = (
        P("dp", "seq", None),
        P("dp", "seq"),
        P("dp", "seq", None),
        P(None, "seq"),
        P(None, "seq"),
        P("seq", None),
        P("seq", None),
        P(None, "seq", None),
        P("seq"),
        P("seq"),
        P(None, "seq"),
        P("seq", None),
        P("seq", None),
        P("seq", None),
        P("seq", None),
        P("seq", None),
    )
    out_specs = (
        P("dp", "seq", None),
        P("dp", "seq", None),
        P(None, "seq"),
        P(None, "seq"),
        P("seq", None),
        P("seq", None),
        P(None, "seq", None),
        P("seq"),
        P("seq"),
        P(None, "seq"),
        P("seq", None),
        P("seq", None),
        P("seq", None),
        P("seq", None),
        P("seq", None),
    )
    return jax.shard_map(local, mesh=mesh, in_specs=in_specs, out_specs=out_specs, check_vma=False)
```

profile of v0, /device:TPU:0, one launch (start us, length us, event | category | flops | bytes accessed | tf_op | source)
XLA Modules:
  0.0 849.6 jit_solution(7836343206225718226)
XLA Ops:
  15.1 9.6 %all_gather.46 = bf16[4,512]{1,0:T(4,128)(2,1)S(1)} all-gather(bf16[4,128]{1,0:T(4,128)(2,1)} %param.19), channel_id=1, replica_groups=mesh['dp'=8,'seq'=4] {'seq'}, dimensions={1}, use_global_device_ids=true | all-gather | bytes 5120 | tf_op jit(solution)/shard_map/all_gather | solution.py:89
  24.8 7.9 all_gather.47
  32.7 7.2 all-gather.1
  40.0 7.9 all-gather
  47.9 7.2 all_gather.50
  62.1 8.8 %all_gather.54 = bf16[9,2048]{1,0:T(8,128)(2,1)S(1)} all-gather(bf16[9,512]{1,0:T(8,128)(2,1)} %param.26), channel_id=1, replica_groups=mesh['dp'=8,'seq'=4] {'seq'}, dimensions={1}, use_global_device_ids=true | all-gather | bytes 46080 | tf_op jit(solution)/shard_map/all_gather | solution.py:96
  70.9 13.9 %all_gather.51 = bf16[3,512,256]{2,1,0:T(8,128)(2,1)} all-gather(bf16[3,128,256]{2,1,0:T(8,128)(2,1)} %param.23), channel_id=1, replica_groups=mesh['dp'=8,'seq'=4] {'seq'}, dimensions={1}, use_global_device_ids=true | all-gather | bytes 983040 | tf_op jit(solution)/shard_map/all_gather | solution.py:93
  91.7 4.5 collective-permute-start
  109.5 4.2 collective-permute-start.2
  115.8 4.1 collective-permute-done.3
  120.5 10.3 %add_convert_fusion = bf16[2,256,2048]{2,1,0:T(8,128)(2,1)} fusion(bf16[2,256,2048]{2,1,0:T(8,128)(2,1)S(1)} %bitcast.238, bf16[2,4,2048]{2,1,0:T(4,128)(2,1)S(1)} %collective-permute-done.3, bf16[2,4,2048]{2,1,0:T(4,128)(2,1)S(1)} %collective-permute-done.2, f32[2048]{0:T(1024)S(1)} %bitcast.294, f32[2,256]{1,0:T(2,128)S(1)} %get-tuple-element.153, ...), kind=kLoop, calls=%fused_computation.61 | loop fusion | flops 62914560 | bytes 4352000 | tf_op jit(solution)/shard_map/convert_element_type | solution.py:171
  135.6 15.6 %all-gather.16.cloned.1.call-done = bf16[512,1536]{1,0:T(8,128)(2,1)} async-done(((bf16[128,1536]{1,0:T(8,128)(2,1)}), bf16[512,1536]{1,0:T(8,128)(2,1)}) %all-gather.16.cloned.1.call-update) | async-done | bytes 1572880 | tf_op jit(solution)/shard_map/all_gather | solution.py:98
  158.8 14.2 %all_gather.58 = bf16[512,512]{1,0:T(8,128)(2,1)} all-gather(bf16[128,512]{1,0:T(8,128)(2,1)S(1)} %copy-done.59), channel_id=1, replica_groups=mesh['dp'=8,'seq'=4] {'seq'}, dimensions={0}, use_global_device_ids=true | all-gather | bytes 655360 | tf_op jit(solution)/shard_map/all_gather | solution.py:99
  173.0 18.3 %all-gather.22.cloned.1.call-done = bf16[2048,512]{1,0:T(8,128)(2,1)} async-done(((bf16[512,512]{1,0:T(8,128)(2,1)}), bf16[2048,512]{1,0:T(8,128)(2,1)}) %all-gather.22.cloned.1.call-update) | async-done | bytes 2097168 | tf_op jit(solution)/shard_map/all_gather | solution.py:101
  191.3 5.0 fusion.134
  203.4 42.8 %all-gather.18.cloned.1.call-done = bf16[2,1024,1024]{2,1,0:T(8,128)(2,1)} async-done(((bf16[2,256,1024]{2,1,0:T(8,128)(2,1)}), bf16[2,1024,1024]{2,1,0:T(8,128)(2,1)}) %all-gather.18.cloned.1.call-update) | async-done | bytes 4194320 | tf_op jit(solution)/shard_map/while/body/eval_jaxpr/all_gather | solution.py:193
  246.3 4.4 fusion.123
  258.7 4.6 select_reduce_fusion
  269.1 7.2 fusion.55
  283.5 8.9 %fusion.21 = (bf16[512,2048]{1,0:T(8,128)(2,1)S(1)}, f32[512,2048]{1,0:T(8,128)}) fusion(f32[512,2048]{1,0:T(8,128)} %fusion.134, bf16[512,2048]{1,0:T(8,128)(2,1)} %all-gather.20.cloned.1.call-done, f32[512,512]{1,0:T(8,128)} %copy-done.17, f32[512]{0:T(512)S(1)} %bitcast.328, f32[512]{0:T(512)S(1)} %bitcast.319, f32[512]{0:T(512)S(1)} %fusion.102, ...), kind=kOutput, calls=%fused_computation.40 | convolution fusion | flops 1096024064 | bytes 13639680 | tf_op jit(solution)/shard_map/dot_general | solution.py:49
  302.6 11.0 %fusion.49 = bf16[2,8,64,1024]{3,2,1,0:T(8,128)(2,1)} fusion(bf16[2,256,8,64]{1,3,2,0:T(8,128)(2,1)} %copy.57, f32[2,8,256,1024]{3,2,1,0:T(8,128)} %copy-done, f32[2,8,256]{2,1,0:T(8,128)S(1)} %log_add_fusion, pred[2,256,1024]{2,1,0:T(8,128)(4,1)} %broadcast_compare_fusion), kind=kOutput, calls=%fused_computation.113 | convolution fusion | flops 550502400 | bytes 19939328 | tf_op jit(solution)/shard_map/while/body/eval_jaxpr/bhqk,bqhd->bkhd/dot_general | solution.py:250
  313.7 4.3 copy.62
  318.1 13.3 %multiply_reduce_fusion = (f32[2,8,256]{2,1,0:T(8,128)S(1)}, f32[2,8,256,1024]{3,2,1,0:T(8,128)}) fusion(f32[2,8,256,1024]{3,2,1,0:T(8,128)} %copy-done, f32[2,8,256]{2,1,0:T(8,128)S(1)} %log_add_fusion, pred[2,256,1024]{2,1,0:T(8,128)(4,1)} %broadcast_compare_fusion, bf16[2,256,8,64]{1,3,2,0:T(8,128)(2,1)} %copy.57, bf16[2,1024,8,64]{1,3,2,0:T(8,128)(2,1)} %bitcast.248), kind=kOutput, calls=%fused_computation.1 | convolution fusion | flops 553644032 | bytes 36732928 | tf_op jit(solution)/shard_map/while/body/eval_jaxpr/bqhd,bkhd->bhqk/dot_general | solution.py:239
  331.4 12.4 %multiply_convert_fusion = bf16[2,8,256,1024]{3,2,1,0:T(8,128)(2,1)S(1)} fusion(f32[2,8,256,1024]{3,2,1,0:T(8,128)} %get-tuple-element.189, f32[2,8,256,1024]{3,2,1,0:T(8,128)} %copy-done, f32[2,8,256]{2,1,0:T(8,128)S(1)} %get-tuple-element.188, f32[2,8,256]{2,1,0:T(8,128)S(1)} %log_add_fusion, pred[2,256,1024]{2,1,0:T(8,128)(4,1)S(1)} %copy-done.8), kind=kLoop, calls=%fused_computation | loop fusion | flops 20971520 | bytes 42500096 | tf_op jit(solution)/shard_map/while/body/eval_jaxpr/convert_element_type | solution.py:243
  354.4 4.7 convolution_convert_fusion.2
  359.4 6.8 fusion.54
  369.7 22.1 %reduce-scatter.18.cloned.1.call-done = bf16[2,256,512]{2,1,0:T(8,128)(2,1)} async-done(((bf16[2,1024,512]{2,1,0:T(8,128)(2,1)}), bf16[2,256,512]{2,1,0:T(8,128)(2,1)}) %reduce-scatter.18.cloned.1.call-update) | async-done | bytes 524304 | tf_op jit(solution)/shard_map/while/body/eval_jaxpr/reduce_scatter | solution.py:257
  399.1 4.7 fusion.31
  406.5 4.5 collective-permute-start.5
  414.6 18.1 %fusion.116 = (bf16[2048]{0:T(1024)(128)(2,1)S(1)}, f32[2,256,2048]{2,1,0:T(8,128)S(1)}) fusion(f32[2048]{0:T(1024)S(1)} %bitcast.295, f32[2,256]{1,0:T(2,128)S(1)} %get-tuple-element.161, bf16[2,256,2048]{2,1,0:T(8,128)(2,1)} %bitcast.242, bf16[2,4,2048]{2,1,0:T(4,128)(2,1)S(1)} %collective-permute-done.5, f32[2048]{0:T(1024)S(1)} %bitcast.293, ...), kind=kLoop, calls=%fused_computation.290 | loop fusion | flops 62912512 | bytes 6453248 | tf_op jit(solution)/shard_map/transpose(jvp())/reduce_sum | solution.py:36
  438.8 4.2 fusion.14
  443.3 4.2 collective-permute-start.7
  465.9 4.9 convolution_convert_fusion.3
  470.9 4.3 convolution_convert_fusion.4
  475.4 7.0 fusion.35
  491.0 4.8 reduce-scatter.38.cloned.1.call-done
  495.8 29.8 %reduce-scatter.26.cloned.1.call-done = bf16[3,128,256]{2,1,0:T(8,128)(2,1)} async-done(((bf16[3,512,256]{2,1,0:T(8,128)(2,1)}), bf16[3,128,256]{2,1,0:T(8,128)(2,1)}) %reduce-scatter.26.cloned.1.call-update) | async-done | bytes 196624 | tf_op jit(solution)/shard_map/reduce_scatter | solution.py:340
  525.6 30.8 %reduce-scatter.22.cloned.1.call-done = bf16[128,1024]{1,0:T(8,128)(2,1)} async-done(((bf16[512,1024]{1,0:T(8,128)(2,1)}), bf16[128,1024]{1,0:T(8,128)(2,1)}) %reduce-scatter.22.cloned.1.call-update) | async-done | bytes 262160 | tf_op jit(solution)/shard_map/reduce_scatter | solution.py:334
  556.4 33.8 %reduce-scatter.32.cloned.1.call-done = bf16[128,1536]{1,0:T(8,128)(2,1)} async-done(((bf16[512,1536]{1,0:T(8,128)(2,1)}), bf16[128,1536]{1,0:T(8,128)(2,1)}) %reduce-scatter.32.cloned.1.call-update) | async-done | bytes 393232 | tf_op jit(solution)/shard_map/reduce_scatter | solution.py:355
  590.2 38.1 %reduce-scatter.30.cloned.1.call-done = bf16[512,512]{1,0:T(8,128)(2,1)} async-done(((bf16[2048,512]{1,0:T(8,128)(2,1)}), bf16[512,512]{1,0:T(8,128)(2,1)}) %reduce-scatter.30.cloned.1.call-update) | async-done | bytes 524304 | tf_op jit(solution)/shard_map/reduce_scatter | solution.py:352
  628.2 38.3 %reduce-scatter.24.cloned.1.call-done = bf16[128,2048]{1,0:T(8,128)(2,1)} async-done(((bf16[512,2048]{1,0:T(8,128)(2,1)}), bf16[128,2048]{1,0:T(8,128)(2,1)}) %reduce-scatter.24.cloned.1.call-update) | async-done | bytes 524304 | tf_op jit(solution)/shard_map/reduce_scatter | solution.py:337
  667.9 5.7 convolution_add_fusion.3
  673.5 9.1 %all-reduce.8 = (bf16[2048]{0:T(1024)(128)(2,1)S(1)}, bf16[2048]{0:T(1024)(128)(2,1)S(1)}) all-reduce(bf16[2048]{0:T(1024)(128)(2,1)S(1)} %get-tuple-element.59, bf16[2048]{0:T(1024)(128)(2,1)S(1)} %get-tuple-element.107), channel_id=9, replica_groups=mesh['dp'=8,'seq'=4] {'seq'}, use_global_device_ids=true, to_apply=%region_44.45.clone | all-reduce | flops 4096 | bytes 16384
  684.1 9.5 %reduce-scatter.40.cloned.1.call-done = bf16[128,4]{1,0:T(8,128)(2,1)} async-done(((bf16[512,4]{1,0:T(8,128)(2,1)}), bf16[128,4]{1,0:T(8,128)(2,1)}) %reduce-scatter.40.cloned.1.call-update) | async-done | bytes 1040
  694.4 26.6 %reduce-scatter.42.cloned.1.call-done = bf16[128,4]{1,0:T(8,128)(2,1)} async-done(((bf16[512,4]{1,0:T(8,128)(2,1)}), bf16[128,4]{1,0:T(8,128)(2,1)}) %reduce-scatter.42.cloned.1.call-update) | async-done | bytes 1040
  721.8 26.0 %reduce-scatter.28.cloned.1.call-done = bf16[9,512]{1,0:T(8,128)(2,1)} async-done(((bf16[9,2048]{1,0:T(8,128)(2,1)}), bf16[9,512]{1,0:T(8,128)(2,1)}) %reduce-scatter.28.cloned.1.call-update) | async-done | bytes 9232 | tf_op jit(solution)/shard_map/reduce_scatter | solution.py:349
  747.8 29.0 %all-reduce.6 = (bf16[4,128]{1,0:T(4,128)(2,1)S(1)}, bf16[4,128]{1,0:T(4,128)(2,1)S(1)}, bf16[512]{0:T(512)(128)(2,1)S(1)}, bf16[512]{0:T(512)(128)(2,1)S(1)}, bf16[9,512]{1,0:T(8,128)(2,1)S(1)}) all-reduce(bf16[4,128]{1,0:T(4,128)(2,1)S(1)} %copy.66, bf16[4,128]{1,0:T(4,128)(2,1)S(1)} %copy.68, ...), channel_id=1, replica_groups=mesh['dp'=8,'seq'=4] {'dp'}, use_global_device_ids=true, to_apply=%region_30.31 | all-reduce | flops 6656 | bytes 26624 | tf_op jit(solution)/shard_map/psum | solution.py:369
  779.8 49.8 %all-reduce.11.cloned.1.call-done = (bf16[128,1024]{1,0:T(8,128)(2,1)}, bf16[128,2048]{1,0:T(8,128)(2,1)}, bf16[3,128,256]{2,1,0:T(8,128)(2,1)}, bf16[512,512]{1...) async-done(((bf16[128,1024]{1,0:T(8,128)(2,1)}, bf16[128,2048]{1,0:T(8,128)(2,1)}, ...) | async-done | bytes 3080208 | tf_op jit(solution)/shard_map/psum | solution.py:371
  (379 shorter events, 168.0 us)
Async XLA Ops:
  7.2 77.6 %copy-start.9 = (bf16[2,256,512]{2,1,0:T(8,128)(2,1)S(1)}, bf16[2,256,512]{2,1,0:T(8,128)(2,1)}, u32[]{:S(2)}) copy-start(bf16[2,256,512]{2,1,0:T(8,128)(2,1)} %param.16) | copy-start | bytes 1572868
  7.2 77.9 %all-gather.10.cloned.1.call-start = ((), (), s32[]{:S(2)}) async-start(), calls=%async_computation.13 | async-start | bytes 1310720 | tf_op jit(solution)/shard_map/all_gather | solution.py:91
  7.9 92.1 %all-gather.12.cloned.1.call-start = ((), (), s32[]{:S(2)}) async-start(), calls=%async_computation.14 | async-start | bytes 2621440 | tf_op jit(solution)/shard_map/all_gather | solution.py:92
  8.7 122.1 %all-gather.14.cloned.1.call-start = ((), (), s32[]{:S(2)}) async-start(), calls=%async_computation.15 | async-start | bytes 2621440 | tf_op jit(solution)/shard_map/all_gather | solution.py:97
  9.4 141.8 %all-gather.16.cloned.1.call-start = ((), (), s32[]{:S(2)}) async-start(), calls=%async_computation.16 | async-start | bytes 1966080 | tf_op jit(solution)/shard_map/all_gather | solution.py:98
  10.0 181.3 %all-gather.22.cloned.1.call-start = ((), (), s32[]{:S(2)}) async-start(), calls=%async_computation.19 | async-start | bytes 2621440 | tf_op jit(solution)/shard_map/all_gather | solution.py:101
  10.6 235.7 %all-gather.18.cloned.1.call-start = ((), (), s32[]{:S(2)}) async-start(), calls=%async_computation.17 | async-start | bytes 5242880 | tf_op jit(solution)/shard_map/while/body/eval_jaxpr/all_gather | solution.py:193
  13.2 76.5 %copy-start.62 = (f32[1,2,2,128]{3,1,2,0:T(2,128)}, f32[1,2,2,128]{3,1,2,0:T(2,128)S(1)}, u32[]{:S(2)}) copy-start(f32[1,2,2,128]{3,1,2,0:T(2,128)S(1)} %copy.73) | copy-start | bytes 6148
  15.1 74.6 %copy-start.64 = (f32[512]{0:T(512)}, f32[512]{0:T(512)S(1)}, u32[]{:S(2)}) copy-start(f32[512]{0:T(512)S(1)} %rsqrt.50) | copy-start | bytes 6148
  32.7 57.1 %copy-start.66 = (f32[1,512]{1,0:T(1,128)}, f32[1,512]{1,0:T(1,128)S(1)}, u32[]{:S(2)}) copy-start(f32[1,512]{1,0:T(1,128)S(1)} %get-tuple-element.165) | copy-start | bytes 6148
  32.7 57.4 %copy-start.70 = (f32[1,512]{1,0:T(1,128)}, f32[1,512]{1,0:T(1,128)S(1)}, u32[]{:S(2)}) copy-start(f32[1,512]{1,0:T(1,128)S(1)} %get-tuple-element.164) | copy-start | bytes 6148
  85.9 10.3 %copy-start.28 = (bf16[3,512,256]{2,1,0:T(8,128)(2,1)S(1)}, bf16[3,512,256]{2,1,0:T(8,128)(2,1)}, u32[]{:S(2)}) copy-start(bf16[3,512,256]{2,1,0:T(8,128)(2,1)} %all_gather.51) | copy-start | bytes 2359300
  89.8 10.2 %copy-start.60 = (f32[512]{0:T(512)}, f32[512]{0:T(512)S(1)}, u32[]{:S(2)}) copy-start(f32[512]{0:T(512)S(1)} %broadcast_multiply_fusion.3) | copy-start | bytes 6148
  90.4 6.2 collective-permute-start.1
  91.7 5.9 collective-permute-start
  109.5 6.3 collective-permute-start.2
  113.7 6.2 collective-permute-start.3
  156.8 126.7 %all-gather.20.cloned.1.call-start = ((), (), s32[]{:S(2)}) async-start(), calls=%async_computation.18 | async-start | bytes 2621440 | tf_op jit(solution)/shard_map/all_gather | solution.py:100
  157.6 210.0 %reduce-scatter.20.cloned.1.call-start = ((), (), s32[]{:S(2)}) async-start(), calls=%async_computation.21 | async-start | bytes 2621440 | tf_op jit(solution)/shard_map/while/body/eval_jaxpr/reduce_scatter | solution.py:263
  318.0 73.8 %reduce-scatter.18.cloned.1.call-start = ((), (), s32[]{:S(2)}) async-start(), calls=%async_computation.20 | async-start | bytes 2621440 | tf_op jit(solution)/shard_map/while/body/eval_jaxpr/reduce_scatter | solution.py:257
  318.1 13.3 %copy-start.8 = (pred[2,256,1024]{2,1,0:T(8,128)(4,1)S(1)}, pred[2,256,1024]{2,1,0:T(8,128)(4,1)}, u32[]{:S(2)}) copy-start(pred[2,256,1024]{2,1,0:T(8,128)(4,1)} %broadcast_compare_fusion) | copy-start | bytes 1572868
  331.4 12.5 %copy-start.25 = (bf16[2,256,8,64]{1,3,2,0:T(8,128)(2,1)S(1)}, bf16[2,256,8,64]{1,3,2,0:T(8,128)(2,1)}, u32[]{:S(2)}) copy-start(bf16[2,256,8,64]{1,3,2,0:T(8,128)(2,1)} %copy.54) | copy-start | bytes 1572868
  351.8 139.2 %reduce-scatter.34.cloned.1.call-start = ((), (), s32[]{:S(2)}) async-start(), calls=%async_computation.28 | async-start | bytes 655360 | tf_op jit(solution)/shard_map/reduce_scatter | solution.py:358
  354.3 136.7 %reduce-scatter.36.cloned.1.call-start = ((), (), s32[]{:S(2)}) async-start(), calls=%async_computation.29 | async-start | bytes 2621440 | tf_op jit(solution)/shard_map/reduce_scatter | solution.py:361
  359.1 136.7 %reduce-scatter.38.cloned.1.call-start = ((), (), s32[]{:S(2)}) async-start(), calls=%async_computation.30 | async-start | bytes 2621440 | tf_op jit(solution)/shard_map/reduce_scatter | solution.py:364
  399.1 11.9 %copy-start.80 = (f32[512,2048]{1,0:T(8,128)S(1)}, f32[512,2048]{1,0:T(8,128)}, u32[]{:S(2)}) copy-start(f32[512,2048]{1,0:T(8,128)} %get-tuple-element.186) | copy-start | bytes 12582916
  405.2 9.4 %collective-permute-start.4 = (bf16[2,4,2048]{2,1,0:T(4,128)(2,1)S(1)}, bf16[2,4,2048]{2,1,0:T(4,128)(2,1)S(1)}, u32[]{:S(2)}, u32[]{:S(2)}) collective-permute-start(bf16[2,4,2048]{2,1,0:T(4,128)(2,1)S(1)} %get-tuple-element.131), channel_id=1, source_target_pairs={{1,0},{2,1},{3,2},{5,4},{6,5},{7,6},{9,8},{10,9},{11,10},{13,12},{... | collective-permute-start | bytes 98312 | tf_op jit(solution)/shard_map/ppermute | solution.py:25
  406.5 8.1 collective-permute-start.5
  414.3 111.4 %reduce-scatter.26.cloned.1.call-start = ((), (), s32[]{:S(2)}) async-start(), calls=%async_computation.24 | async-start | bytes 983040 | tf_op jit(solution)/shard_map/reduce_scatter | solution.py:340
  414.5 18.1 %copy-start.3 = (f32[512,2048]{1,0:T(8,128)S(1)}, f32[512,2048]{1,0:T(8,128)}, u32[]{:S(2)}) copy-start(f32[512,2048]{1,0:T(8,128)} %copy-done.2) | copy-start | bytes 12582916
  414.5 18.1 %copy-start.12 = (f32[512,256]{1,0:T(8,128)S(1)}, f32[512,256]{1,0:T(8,128)}, u32[]{:S(2)}) copy-start(f32[512,256]{1,0:T(8,128)} %copy-done.11) | copy-start | bytes 1572868
  438.7 10.5 %copy-start.43 = (bf16[2,256,512]{2,1,0:T(8,128)(2,1)S(1)}, bf16[2,256,512]{2,1,0:T(8,128)(2,1)}, u32[]{:S(2)}) copy-start(bf16[2,256,512]{2,1,0:T(8,128)(2,1)} %copy-done.42) | copy-start | bytes 1572868
  438.8 10.8 %copy-start.37 = (bf16[512,512]{1,0:T(8,128)(2,1)S(1)}, bf16[512,512]{1,0:T(8,128)(2,1)}, u32[]{:S(2)}) copy-start(bf16[512,512]{1,0:T(8,128)(2,1)} %copy-done.36) | copy-start | bytes 1572868
  443.3 11.7 %collective-permute-start.7 = (bf16[2,1,256]{2,1,0:T(2,128)(2,1)S(1)}, bf16[2,1,256]{2,1,0:T(2,128)(2,1)S(1)}, u32[]{:S(2)}, u32[]{:S(2)}) collective-permute-start(bf16[2,1,256]{2,1,0:T(2,128)(2,1)S(1)} %get-tuple-element.141), channel_id=1, source_target_pairs={{0,1},{1,2},{2,3},{4,5},{5,6},{6,7},{8,9},{9,10},{10,11},{12,13},{... | collective-permute-start | bytes 3080 | tf_op jit(solution)/shard_map/ppermute | solution.py:23
  447.6 7.4 collective-permute-start.6
  451.1 105.3 %reduce-scatter.22.cloned.1.call-start = ((), (), s32[]{:S(2)}) async-start(), calls=%async_computation.22 | async-start | bytes 1310720 | tf_op jit(solution)/shard_map/reduce_scatter | solution.py:334
  461.9 128.2 %reduce-scatter.32.cloned.1.call-start = ((), (), s32[]{:S(2)}) async-start(), calls=%async_computation.27 | async-start | bytes 1966080 | tf_op jit(solution)/shard_map/reduce_scatter | solution.py:355
  465.8 162.4 %reduce-scatter.30.cloned.1.call-start = ((), (), s32[]{:S(2)}) async-start(), calls=%async_computation.26 | async-start | bytes 2621440 | tf_op jit(solution)/shard_map/reduce_scatter | solution.py:352
  470.8 195.7 %reduce-scatter.24.cloned.1.call-start = ((), (), s32[]{:S(2)}) async-start(), calls=%async_computation.23 | async-start | bytes 2621440 | tf_op jit(solution)/shard_map/reduce_scatter | solution.py:337
  475.2 218.4 %reduce-scatter.40.cloned.1.call-start = ((), (), s32[]{:S(2)}) async-start(), calls=%async_computation.31 | async-start | bytes 163840
  484.9 181.7 %copy-start.78 = (u32[32]{0:T(128)S(1)}, u32[32]{0:T(128)}, u32[]{:S(2)}) copy-start(u32[32]{0:T(128)} %constant.130) | copy-start | bytes 388
  485.8 235.2 %reduce-scatter.42.cloned.1.call-start = ((), (), s32[]{:S(2)}) async-start(), calls=%async_computation.32 | async-start | bytes 163840
  486.7 261.1 %reduce-scatter.28.cloned.1.call-start = ((), (), s32[]{:S(2)}) async-start(), calls=%async_computation.25 | async-start | bytes 81920 | tf_op jit(solution)/shard_map/reduce_scatter | solution.py:349
  490.9 338.7 %all-reduce.11.cloned.1.call-start = ((), (), s32[]{:S(2)}) async-start(), calls=%async_computation.33 | async-start | bytes 6160384 | tf_op jit(solution)/shard_map/psum | solution.py:371
  667.8 14.9 %copy-start.14 = (f32[512,512]{1,0:T(8,128)S(1)}, f32[512,512]{1,0:T(8,128)}, u32[]{:S(2)}) copy-start(f32[512,512]{1,0:T(8,128)} %copy-done.13) | copy-start | bytes 3145732
  667.8 14.9 %copy-start.35 = (f32[512,512]{1,0:T(8,128)S(1)}, f32[512,512]{1,0:T(8,128)}, u32[]{:S(2)}) copy-start(f32[512,512]{1,0:T(8,128)} %copy-done.34) | copy-start | bytes 3145732
  829.6 10.4 %copy-start.54 = (bf16[128,2048]{1,0:T(8,128)(2,1)S(1)}, bf16[128,2048]{1,0:T(8,128)(2,1)}, u32[]{:S(2)}) copy-start(bf16[128,2048]{1,0:T(8,128)(2,1)} %get-tuple-element.103) | copy-start | bytes 1572868
  829.6 11.5 %copy-start.53 = (bf16[512,512]{1,0:T(8,128)(2,1)S(1)}, bf16[512,512]{1,0:T(8,128)(2,1)}, u32[]{:S(2)}) copy-start(bf16[512,512]{1,0:T(8,128)(2,1)} %get-tuple-element.104) | copy-start | bytes 1572868
  (62 other events, 270.2 us)
Sparse Core Ops, SparseCore 0:
  9.9 29.3 all-gather.9
  41.1 39.2 all-gather.11
  82.3 36.0 all-gather.13
  120.1 31.0 all-gather.15
  152.9 38.3 all-gather.21
  193.5 52.6 all-gather.17
  248.1 35.3 all-gather.19
  318.1 35.1 reduce-scatter.19
  356.6 35.1 reduce-scatter.17
  394.5 24.7 reduce-scatter.33
  422.5 35.1 reduce-scatter.35
  460.6 35.1 reduce-scatter.37
  499.5 26.0 reduce-scatter.25
  528.6 27.7 reduce-scatter.21
  559.2 30.8 reduce-scatter.31
  593.0 35.1 reduce-scatter.29
  631.3 35.1 reduce-scatter.23
  669.7 23.8 reduce-scatter.39
  697.1 23.8 reduce-scatter.41
  724.1 23.6 reduce-scatter.27
  751.1 78.4 all-reduce.10
where the time goes:
time: 858 us; the launch traced here: 850 us
  waiting for transfers between devices  399 us (47%)
  matrix products  124 us (14%)
  blocking collectives  115 us (13%)
  other arithmetic  108 us (13%)
  local copies, waits for them, and re-layouts  62.3 us (7%)
  starting transfers between devices  24.6 us (3%)
  between operations  17.1 us (2%)
    psum x1, waiting for transfers between devices, local(): lax.psum(owned[2].astype(jnp.bfloat16), 'dp').astype(jnp.float32)  49.8 us
    all_gather x1, waiting for transfers between devices, attend(): whole_kv = lax.all_gather(kv_part, 'seq', axis=1, tiled=True)  42.8 us
    unnamed x23, waiting for transfers between devices  40.1 us
    reduce_scatter x1, waiting for transfers between devices, local(): lax.psum_scatter(g_left.astype(jnp.bfloat16), 'seq', scatter_dimension=0,...  38.3 us
    reduce_scatter x1, waiting for transfers between devices, local(): lax.psum_scatter(g_point.astype(jnp.bfloat16), 'seq', scatter_dimension=0...  38.1 us
    reduce_scatter x1, waiting for transfers between devices, local(): lax.psum_scatter(g_qkv.astype(jnp.bfloat16), 'seq', scatter_dimension=0,...  33.8 us
    reduce_scatter x1, waiting for transfers between devices, local(): lax.psum_scatter(g_glu.astype(jnp.bfloat16), 'seq', scatter_dimension=0,...  30.8 us
    reduce_scatter x1, waiting for transfers between devices, local(): lax.psum_scatter(g_conv.astype(jnp.bfloat16), 'seq', scatter_dimension=1,...  29.8 us
  transfers between devices with their start and end apart: 29, of which 17 were waited for; matrix products, arithmetic and copies ran while one was open for 27% of the time, Pallas kernels for 0%

commit v1 on v0

v1 whole, which is shorter than its diff:
```python
import math

import jax
import jax.numpy as jnp
from jax import lax
from jax.experimental import pallas as pl
from jax.experimental.pallas import tpu as pltpu
from jax.sharding import PartitionSpec as P

HEADS = 8
EPS = 1e-06
NEG = -1000000000.0
MESH = pl.DeviceIdType.MESH
F32 = jnp.float32
BF16 = jnp.bfloat16

GLU, CONV, LEFT, POINT, QKV, OUT, FIN, FOUT = range(8)
WEIGHTS = 8
SMALL = 8


def mm(a, b):
    return lax.dot_general(a, b, (((1,), (0,)), ((), ())), preferred_element_type=F32)


def mm_t(a, b):
    return lax.dot_general(a, b, (((1,), (1,)), ((), ())), preferred_element_type=F32)


def mm_tn(a, b):
    return lax.dot_general(a, b, (((0,), (0,)), ((), ())), preferred_element_type=F32)


def normed(v):
    centred = v - jnp.mean(v, axis=-1, keepdims=True)
    r = lax.rsqrt(jnp.mean(centred * centred, axis=-1, keepdims=True) + EPS)
    return centred * r, r


def gelu_both(v):
    c = math.sqrt(2.0 / math.pi)
    sq = v * v
    t = jnp.tanh(v * (c + (c * 0.044715) * sq))
    half = 0.5 * t + 0.5
    value = v * half
    slope = half + (0.5 * v) * (1.0 - t * t) * (c + (3.0 * c * 0.044715) * sq)
    return value, slope


def sigmoid(v):
    return 0.5 * jnp.tanh(0.5 * v) + 0.5


class Buffers:
    pass


class Plan:
    def __init__(self, dp, n, seqs, span, width, hidden, half):
        self.n, self.Z = n, dp // 2
        self.S, self.span = seqs, span
        self.D, self.FF, self.HALF = width, hidden, half
        self.LEN = span * n
        self.T = self.LEN // 2
        self.PH = n // 2
        self.B = math.isqrt(n)
        self.A = n // self.B
        assert self.A == self.B and n == 2 * seqs and dp % 2 == 0
        self.sw = max(span, 128)
        self.sr = self.sw // span
        dn = width // n
        self.nw = max(dn, 128)
        self.nr = self.nw // dn
        self.FFn = hidden // n
        self.dims = [
            (width, 2 * width),
            (width, half),
            (width, hidden),
            (hidden, width),
            (width, 3 * width),
            (width, width),
            (width, hidden),
            (hidden, width),
        ]

    def whole(self, w):
        k, cols = self.dims[w]
        return (3, k, cols) if w == CONV else (k, cols)

    def kr(self, w):
        return self.dims[w][0] // self.n

    def hr(self, w):
        return self.kr(w) // 2

    def piece(self, w, rows):
        cols = self.dims[w][1]
        return (3, rows, cols) if w == CONV else (rows, cols)

    def buffers(self, take):
        T, D, FF, H, n = self.T, self.D, self.FF, self.HALF, self.n
        r = Buffers()

        def vm(shape, dtype):
            return take(pltpu.VMEM(shape, dtype))

        def sem(*shape):
            return take(pltpu.SemaphoreType.DMA(shape))

        every = range(WEIGHTS)
        parts = [(self.piece(w, self.hr(w)), BF16) for w in every] + [((8, FF), F32)]
        r.w = [vm(self.whole(w), BF16) for w in every]
        r.g8 = vm((16, FF), F32)
        r.g = r.w + [r.g8]
        r.r = [vm(self.piece(w, n * self.hr(w)), BF16) for w in every] + [vm((8, FF), F32)]
        r.p = [vm((n - 1,) + shape, dtype) for shape, dtype in parts]
        if self.Z > 1:
            r.u = [vm(shape, dtype) for shape, dtype in parts]
            r.d = [vm(shape, dtype) for shape, dtype in parts]
        r.segbuf = vm((n, 8, self.sw), F32)
        r.segrow = vm((8, self.LEN), F32)
        r.segq = vm((8, T), F32)
        r.segcol = vm((self.LEN + 16, 128), F32)
        r.segloc = vm((T + 16, 128), F32)
        r.mext = vm((4, T + 16, 128), F32)
        r.smallbuf = vm((n, 32, self.FFn), BF16)
        r.nrm = vm((8, D), F32)
        r.midp = vm((16, FF), F32)
        r.xin = vm((T, D), BF16)
        r.cot = vm((T, D), BF16)
        r.a1 = vm((T, D), BF16)
        r.sg = vm((T, 2 * D), BF16)
        r.y1 = vm((T, D), F32)
        r.a2 = vm((T, D), BF16)
        r.pext = vm((3, T + 16, H), F32)
        r.dgl = vm((T, FF), BF16)
        r.dgr = vm((T, H), BF16)
        r.nm = vm((T, FF), BF16)
        r.rm = vm((T, 1), F32)
        r.big = vm((T + 16, FF), F32)
        r.sep = vm((T, FF), BF16)
        r.y2 = vm((T, D), F32)
        r.a4 = vm((T, D), BF16)
        r.qb = vm((T, D), BF16)
        r.kvb = vm((2, T, 2 * D), BF16)
        r.lse = vm((T, 128), F32)
        r.lset = vm((HEADS // 2, 8, T), F32)
        r.ctx = vm((T, D), BF16)
        r.y3 = vm((T, D), F32)
        r.a5 = vm((T, D), BF16)
        r.hid = vm((T, FF), BF16)
        r.dg = vm((T, FF), BF16)
        r.osend = vm((T, D), BF16)
        r.gs = vm((T, D), F32)
        r.dkvr = vm((T, 2 * D), BF16)
        r.acc = vm((2, self.LEN, 128), F32)
        r.tr = vm((D, T), BF16)
        r.col = vm((T, 128), F32)
        wides = (H, FF, FF, H)
        r.es = [vm((8, wide), F32) for wide in wides]
        r.er = [vm((8, wide), F32) for wide in wides]
        r.s_loc = sem(WEIGHTS)
        r.s_as = sem(WEIGHTS, self.B)
        r.s_ar = sem(WEIGHTS, self.B)
        r.s_bs = sem(WEIGHTS, self.A * self.B)
        r.s_br = sem(WEIGHTS, self.A * self.B)
        r.s_ds = sem(WEIGHTS, n)
        r.s_dr = sem(WEIGHTS, n)
        r.s_rs = sem(WEIGHTS + 1, n)
        r.s_rr = sem(WEIGHTS + 1, n)
        r.s_ps = sem(WEIGHTS + 1, n)
        r.s_pr = sem(WEIGHTS + 1, n)
        r.s_zs = sem(WEIGHTS + 1, 2)
        r.s_zr = sem(WEIGHTS + 1, 2)
        r.s_fs = sem(WEIGHTS + 1)
        r.s_fr = sem(WEIGHTS + 1)
        r.s_fl = sem(WEIGHTS + 1)
        r.s_xs = sem(4, self.S)
        r.s_xr = sem(4, max(self.PH, self.S))
        r.s_gs = sem(2 * self.S)
        r.s_gr = sem(n)
        r.s_ms = sem(n)
        r.s_mr = sem(n)
        r.s_es = sem(4)
        r.s_er = sem(4)
        r.s_ks = sem(2)
        r.s_kr = sem(2)
        return r


INPUTS = 4 + WEIGHTS
OUTPUTS = 2 + WEIGHTS + 1


def kernel(plan, *refs):
    ins, outs = refs[:INPUTS], refs[INPUTS : INPUTS + OUTPUTS]
    scratch = iter(refs[INPUTS + OUTPUTS :])
    r = plan.buffers(lambda shape: next(scratch))
    r.x, r.seg, r.ct, r.small = ins[:4]
    r.h = ins[4:]
    r.o_out, r.o_ig = outs[:2]
    r.o = outs[2:]
    n, Z, S, span = plan.n, plan.Z, plan.S, plan.span
    T, D, FF, H, PH = plan.T, plan.D, plan.FF, plan.HALF, plan.PH
    A, B = plan.A, plan.B
    dp, q = lax.axis_index("dp"), lax.axis_index("seq")
    z, c = dp // 2, dp % 2
    oc = 1 - c

    def aligned(v, m=16):
        return pl.multiple_of(v, m)

    def dev(core, chip, plane=None):
        return ((z if plane is None else plane) * 2 + core, chip)

    sibling = dev(oc, q)

    def remote(src, dst, ss, rs, to):
        return pltpu.make_async_remote_copy(
            src_ref=src, dst_ref=dst, send_sem=ss, recv_sem=rs, device_id=to, device_id_type=MESH
        )

    barrier = pltpu.get_barrier_semaphore()
    for core in range(2):

        def greet(t, _, core=core):
            chip = lax.rem(q + t, n)
            to = (z * 2 + (c + core) % 2, chip)
            pl.semaphore_signal(barrier, inc=1, device_id=to, device_id_type=MESH)
            return 0

        lax.fori_loop(1 - core, n, greet, 0)
    if Z > 1:

        @pl.when(z > 0)
        def _():
            pl.semaphore_signal(barrier, inc=1, device_id=dev(c, q, z - 1), device_id_type=MESH)

        @pl.when(z < Z - 1)
        def _():
            pl.semaphore_signal(barrier, inc=1, device_id=dev(c, q, z + 1), device_id_type=MESH)

    pl.semaphore_wait(barrier, 2 * n - 1 + (z + Z - 1) // Z + (2 * Z - 2 - z) // Z)

    def vrows(ref, w, row0, rows):
        ds = pl.ds(aligned(row0), rows)
        return ref.at[:, ds] if w == CONV else ref.at[ds]

    def wblock(w, shard, half):
        return vrows(r.w[w], w, shard * plan.kr(w) + half * plan.hr(w), plan.hr(w))

    def qof(core, f, g):
        f, g = f % B, g % B
        return core * (f * B + g) + (1 - core) * (g * B + f)

    b_, a_ = q % B, q // B
    f_, g_ = c * a_ + oc * b_, c * b_ + oc * a_
    of_, og_ = oc * a_ + c * b_, oc * b_ + c * a_

    def copy_a(w, t):
        src = vrows(r.h[w], w, c * plan.hr(w), plan.hr(w))
        return remote(
            src,
            wblock(w, q, c),
            r.s_as.at[w, t],
            r.s_ar.at[w, t],
            dev(c, qof(c, f_ + t, g_)),
        )

    def arrived_a(w, t):
        blk = wblock(w, qof(c, f_ + B - t, g_), c)
        return remote(blk, blk, r.s_as.at[w, t], r.s_ar.at[w, t], sibling)

    def copy_b(w, u, t):
        shard = qof(c, f_ + B - t, g_)
        if t == 0:
            src = vrows(r.h[w], w, c * plan.hr(w), plan.hr(w))
        else:
            src = wblock(w, shard, c)
        i = u * B + t
        return remote(
            src,
            wblock(w, shard, c),
            r.s_bs.at[w, i],
            r.s_br.at[w, i],
            dev(c, qof(c, f_, g_ + u)),
        )

    def arrived_b(w, u, t):
        blk = wblock(w, qof(c, f_ + B - t, g_ + B - u), c)
        i = u * B + t
        return remote(blk, blk, r.s_bs.at[w, i], r.s_br.at[w, i], sibling)

    def copy_d(w, u, t):
        blk = wblock(w, qof(c, f_ + B - t, g_ + B - u), c)
        i = u * B + t
        return remote(blk, blk, r.s_ds.at[w, i], r.s_dr.at[w, i], sibling)

    def arrived_d(w, u, t):
        blk = wblock(w, qof(oc, of_ + B - t, og_ + B - u), oc)
        i = u * B + t
        return remote(blk, blk, r.s_ds.at[w, i], r.s_dr.at[w, i], sibling)

    def local_shard(w):
        dst = vrows(r.w[w], w, q * plan.kr(w), plan.kr(w))
        return pltpu.make_async_copy(r.h[w], dst, r.s_loc.at[w])

    def g0(w):
        local_shard(w).start()
        for t in range(1, B):
            copy_a(w, t).start()
        for u in range(1, A):
            copy_b(w, u, 0).start()

    def g1(w):
        for t in range(1, B):
            arrived_a(w, t).wait_recv()
            for u in range(1, A):
                copy_b(w, u, t).start()
            copy_d(w, 0, t).start()

    def g2(w):
        for u in range(1, A):
            for t in range(B):
                arrived_b(w, u, t).wait_recv()
                copy_d(w, u, t).start()

    def g3(w):
        local_shard(w).wait()
        for u in range(A):
            for t in range(B):
                if (u, t) != (0, 0):
                    arrived_d(w, u, t).wait_recv()

    def gather_sent(w):
        for t in range(1, B):
            copy_a(w, t).wait_send()
        for u in range(A):
            for t in range(B):
                if u > 0:
                    copy_b(w, u, t).wait_send()
                if (u, t) != (0, 0):
                    copy_d(w, u, t).wait_send()

    def token_rows(ref, slot):
        return ref.at[pl.ds(aligned(slot * span), span)]

    def tokens_in(src, dst, k):
        for j in range(S):
            chip, core, slot = S * c + j, q // PH, q % PH
            here = jnp.logical_and(chip == q, core == c)
            there = token_rows(dst, slot)

            @pl.when(here)
            def _():
                pltpu.make_async_copy(src.at[j], there, r.s_xr.at[k, slot]).start()

            @pl.when(jnp.logical_not(here))
            def _():
                remote(
                    src.at[j], there, r.s_xs.at[k, j], r.s_xr.at[k, slot], dev(core, chip)
                ).start()

    def tokens_in_done(dst, k):
        for slot in range(PH):
            blk = token_rows(dst, slot)
            pltpu.make_async_copy(blk, blk, r.s_xr.at[k, slot]).wait()

    def tokens_in_sent(src, dst, k):
        for j in range(S):
            chip, core, slot = S * c + j, q // PH, q % PH
            here = jnp.logical_and(chip == q, core == c)

            @pl.when(jnp.logical_not(here))
            def _():
                remote(
                    src.at[j],
                    token_rows(dst, slot),
                    r.s_xs.at[k, j],
                    r.s_xr.at[k, slot],
                    dev(core, chip),
                ).wait_send()

    def tokens_out(src, dst, k):
        for p in range(PH):
            chip, core, slot = c * PH + p, q // S, q % S
            here = jnp.logical_and(chip == q, core == c)

            @pl.when(here)
            def _():
                pltpu.make_async_copy(token_rows(src, p), dst.at[slot], r.s_xr.at[k, slot]).start()

            @pl.when(jnp.logical_not(here))
            def _():
                remote(
                    token_rows(src, p),
                    dst.at[slot],
                    r.s_xs.at[k, p],
                    r.s_xr.at[k, slot],
                    dev(core, chip),
                ).start()

    def tokens_out_done(src, dst, k):
        for j in range(S):
            pltpu.make_async_copy(dst.at[j], dst.at[j], r.s_xr.at[k, j]).wait()
        for p in range(PH):
            chip, core, slot = c * PH + p, q // S, q % S
            here = jnp.logical_and(chip == q, core == c)

            @pl.when(jnp.logical_not(here))
            def _():
                remote(
                    token_rows(src, p),
                    dst.at[slot],
                    r.s_xs.at[k, p],
                    r.s_xr.at[k, slot],
                    dev(core, chip),
                ).wait_send()

    def seg_send():
        for j in range(S):
            for core in range(2):
                chip = S * c + j
                here = jnp.logical_and(chip == q, c == core)
                i = 2 * j + core

                @pl.when(here)
                def _():
                    pltpu.make_async_copy(r.seg.at[j], r.segbuf.at[q], r.s_gr.at[q]).start()

                @pl.when(jnp.logical_not(here))
                def _():
                    remote(
                        r.seg.at[j],
                        r.segbuf.at[q],
                        r.s_gs.at[i],
                        r.s_gr.at[q],
                        dev(core, chip),
                    ).start()

    def seg_sent():
        for j in range(S):
            for core in range(2):
                chip = S * c + j
                here = jnp.logical_and(chip == q, c == core)

                @pl.when(jnp.logical_not(here))
                def _():
                    remote(
                        r.seg.at[j],
                        r.segbuf.at[q],
                        r.s_gs.at[2 * j + core],
                        r.s_gr.at[q],
                        dev(core, chip),
                    ).wait_send()

    def small_copy(t):
        return remote(
            r.small,
            r.smallbuf.at[q],
            r.s_ms.at[t],
            r.s_mr.at[t],
            dev(c, (q + t) % n),
        )

    def small_arrived(t):
        blk = r.smallbuf.at[(q + n - t) % n]
        return remote(blk, blk, r.s_ms.at[t], r.s_mr.at[t], sibling)

    def edge_copy(i):
        return remote(r.es[i], r.er[i], r.s_es.at[i], r.s_er.at[i], sibling)

    def edge_send(i, last, first):
        r.es[i][...] = jnp.where(c == 0, last, first)
        edge_copy(i).start()

    def edge_take(i):
        edge_copy(i).wait()
        got = r.er[i][...]
        return jnp.where(c == 1, got, 0.0), jnp.where(c == 0, got, 0.0)

    def gpiece(w, shard, half):
        if w == SMALL:
            return r.g8.at[pl.ds(pl.multiple_of(half * 8, 8), 8)]
        return vrows(r.w[w], w, shard * plan.kr(w) + half * plan.hr(w), plan.hr(w))

    def rpiece(w, shard):
        if w == SMALL:
            return r.r[SMALL]
        return vrows(r.r[w], w, shard * plan.hr(w), plan.hr(w))

    def copy_r(w, s):
        return remote(
            gpiece(w, s, oc), rpiece(w, s), r.s_rs.at[w, s], r.s_rr.at[w, s], sibling
        )

    def copy_p(w, t):
        chip = lax.rem(q + t, n)
        return remote(
            gpiece(w, chip, c),
            r.p[w].at[t - 1],
            r.s_ps.at[w, t],
            r.s_pr.at[w, t],
            dev(c, chip),
        )

    def shards(w):
        return 1 if w == SMALL else n

    def red0(w):
        for s in range(shards(w)):
            copy_r(w, s).start()

    def add_core(w, s):
        copy_r(w, s).wait_recv()
        mine = gpiece(w, s, c)
        total = mine[...].astype(F32) + rpiece(w, s)[...].astype(F32)
        mine[...] = total.astype(mine.dtype)

    def red1(w):
        if w == SMALL:
            add_core(w, 0)

        def one(t, _):
            if w != SMALL:
                add_core(w, lax.rem(q + t, n))
            copy_p(w, t).start()
            return 0

        lax.fori_loop(1, n, one, 0)
        if w != SMALL:
            add_core(w, q)

    def red2(w):
        buf = r.p[w]
        mine = gpiece(w, q, c)
        total = mine[...].astype(F32)
        for t in range(1, n):
            copy_p(w, t).wait_recv()
            total = total + buf[t - 1].astype(F32)
        buf[0] = total.astype(buf.dtype)

    def copy_z(w, way):
        plane = z + 1 if way == 0 else z - 1
        return remote(
            r.p[w].at[1 + way],
            (r.u, r.d)[way][w],
            r.s_zs.at[w, way],
            r.s_zr.at[w, way],
            dev(c, q, plane),
        )

    def red_hop(w, h):
        buf = r.p[w]

        @pl.when(z == h)
        def _():
            if h == 0:
                buf[1] = buf[0]
            else:
                copy_z(w, 0).wait_recv()
                buf[1] = (buf[0].astype(F32) + r.u[w][...].astype(F32)).astype(buf.dtype)
            if h < Z - 1:
                copy_z(w, 0).start()

        @pl.when(z == Z - 1 - h)
        def _():
            if h == 0:
                buf[2] = buf[0]
            else:
                copy_z(w, 1).wait_recv()
                if h < Z - 1:
                    buf[2] = (buf[0].astype(F32) + r.d[w][...].astype(F32)).astype(buf.dtype)
            if h < Z - 1:
                copy_z(w, 1).start()

    def final_rows(w, ref):
        if w == SMALL:
            return ref.at[pl.ds(pl.multiple_of(c * 8, 8), 8)]
        return vrows(ref, w, c * plan.hr(w), plan.hr(w))

    def final_local(w):
        return pltpu.make_async_copy(
            r.p[w].at[0], final_rows(w, r.o[w]), r.s_fl.at[w]
        )

    def final_remote(w):
        return remote(
            r.p[w].at[0],
            final_rows(w, r.o[w]),
            r.s_fs.at[w],
            r.s_fr.at[w],
            sibling,
        )

    def red_final(w):
        buf = r.p[w]
        if Z > 1:

            @pl.when(z == Z - 1)
            def _():
                buf[0] = buf[1]

            @pl.when(z < Z - 1)
            def _():
                buf[0] = (buf[1].astype(F32) + r.d[w][...].astype(F32)).astype(buf.dtype)

        final_local(w).start()
        final_remote(w).start()

    def red_end(w):
        final_local(w).wait()
        final_remote(w).wait()
        for s in range(shards(w)):
            copy_r(w, s).wait_send()
        for t in range(1, n):
            copy_p(w, t).wait_send()
        if Z > 1:

            @pl.when(z < Z - 1)
            def _():
                copy_z(w, 0).wait_send()

            @pl.when(z > 0)
            def _():
                copy_z(w, 1).wait_send()

    active = []

    def reduce_start(w):
        red0(w)
        steps = [red1, red2]
        if Z > 1:
            steps += [lambda k, h=h: red_hop(k, h) for h in range(Z)]
        steps.append(red_final)
        active.append((w, steps))

    def pump(times=1):
        for _ in range(times):
            for w, steps in active:
                if steps:
                    steps.pop(0)(w)

    def loop(count, body):
        def step(i, _):
            body(i)
            return 0

        lax.fori_loop(0, count, step, 0)

    RB = 256
    NB = T // RB

    def rows_of(i, size=RB, base=0):
        return pl.ds(pl.multiple_of(i * size + base, 8 if base else size), size)

    small_local = pltpu.make_async_copy(r.small, r.smallbuf.at[q], r.s_mr.at[0])
    small_local.start()
    for t in range(1, n):
        small_copy(t).start()
    seg_send()
    tokens_in(r.x, r.xin, 0)
    g0(GLU)
    g0(CONV)
    r.g8[...] = jnp.zeros((16, FF), F32)

    for s in range(n):
        blk = r.segbuf.at[s]
        pltpu.make_async_copy(blk, blk, r.s_gr.at[s]).wait()
    for grp in range(n // plan.sr):
        got = r.segbuf[grp * plan.sr]
        for k in range(1, plan.sr):
            got = got + r.segbuf[grp * plan.sr + k]
        r.segrow[:, grp * plan.sw : (grp + 1) * plan.sw] = got
    r.segq[...] = r.segrow[:, pl.ds(pl.multiple_of(c * T, 128), T)]
    r.segcol[0:8] = jnp.full((8, 128), -1.0, F32)
    r.segcol[plan.LEN + 8 : plan.LEN + 16] = jnp.full((8, 128), -1.0, F32)
    for k in range(plan.LEN // 128):
        row = r.segrow[0:1, k * 128 : (k + 1) * 128]
        r.segcol[8 + k * 128 : 8 + (k + 1) * 128] = jnp.broadcast_to(row, (128, 128)).T
    r.segloc[...] = r.segcol[pl.ds(pl.multiple_of(c * T, 8), T + 16)]
    for o in range(1, 5):
        same = r.segloc[0 : T + 8] == r.segloc[o : T + 8 + o]
        r.mext[o - 1, 0 : T + 8] = jnp.where(same, 1.0, 0.0)

    def mask(o, start, rows):
        if o > 0:
            return r.mext[o - 1, 8 + start : 8 + start + rows]
        return r.mext[-o - 1, 8 + start + o : 8 + start + o + rows]

    small_local.wait()
    for t in range(1, n):
        small_arrived(t).wait_recv()
    for grp in range(n // plan.nr):
        got = r.smallbuf[grp * plan.nr].astype(F32)[0:8, 0 : plan.nw]
        for k in range(1, plan.nr):
            got = got + r.smallbuf[grp * plan.nr + k].astype(F32)[0:8, 0 : plan.nw]
        r.nrm[:, grp * plan.nw : (grp + 1) * plan.nw] = got
    for s in range(n):
        r.midp[:, s * plan.FFn : (s + 1) * plan.FFn] = r.smallbuf[s].astype(F32)[8:24]

    def ln_out(k, v):
        unit, _ = normed(v)
        return (unit * r.nrm[k : k + 1] + r.nrm[4 + k : 5 + k]).astype(BF16)

    def ln_back(k, e, v):
        unit, rs = normed(v)
        eg = e * r.nrm[k : k + 1]
        m1 = jnp.mean(eg, axis=-1, keepdims=True)
        m2 = jnp.mean(eg * unit, axis=-1, keepdims=True)
        cols = slice(k * D, (k + 1) * D)
        r.g8[11:12, cols] += jnp.sum(e * unit, axis=0, keepdims=True)
        r.g8[12:13, cols] += jnp.sum(e, axis=0, keepdims=True)
        return rs * (eg - m1 - unit * m2)

    g1(GLU)
    g0(LEFT)
    g2(GLU)
    g1(CONV)
    tokens_in_done(r.xin, 0)
    g3(GLU)

    def glu(i):
        rows = rows_of(i)
        x = r.xin[rows].astype(F32)
        a1 = ln_out(0, x)
        r.a1[rows] = a1
        value = mm(a1, r.w[GLU][:, 0:D])
        gate = sigmoid(mm(a1, r.w[GLU][:, D : 2 * D]))
        r.sg[rows, 0:D] = gate.astype(BF16)
        r.sg[rows, D : 2 * D] = (value * gate * (1.0 - gate)).astype(BF16)
        y1 = x + value * gate
        r.y1[rows] = y1
        r.a2[rows] = ln_out(1, y1)

    loop(NB, glu)
    g0(POINT)
    g2(CONV)
    g1(LEFT)
    g3(CONV)

    def conv(i):
        a2 = r.a2[rows_of(i)]
        for o in range(3):
            r.pext[o, rows_of(i, RB, 8)] = mm(a2, r.w[CONV][o])

    loop(NB, conv)
    edge_send(0, r.pext[0, T : T + 8], r.pext[2, 8:16])
    g0(QKV)
    g2(LEFT)
    g1(POINT)
    top, bottom = edge_take(0)
    r.pext[0, 0:8] = top
    r.pext[2, T + 8 : T + 16] = bottom
    for k in range(T // 128):
        lo = k * 128
        before = mask(-1, lo, 128)
        after = mask(1, lo, 128)
        pre = (
            r.pext[0, lo + 7 : lo + 135] * jnp.concatenate([before] * (H // 128), axis=1)
            + r.pext[1, lo + 8 : lo + 136]
            + r.pext[2, lo + 9 : lo + 137] * jnp.concatenate([after] * (H // 128), axis=1)
        )
        value, slope = gelu_both(pre)
        r.pext[1, lo + 8 : lo + 136] = value
        r.dgr[lo : lo + 128] = slope.astype(BF16)
    g3(LEFT)

    CH = 512
    RM = 128

    def left(i):
        rows, erows = rows_of(i, RM), rows_of(i, RM, 8)
        a2 = r.a2[rows]
        for k in range(FF // CH):
            value, slope = gelu_both(mm(a2, r.w[LEFT][:, k * CH : (k + 1) * CH]))
            r.dgl[rows, k * CH : (k + 1) * CH] = slope.astype(BF16)
            r.big[erows, k * CH : (k + 1) * CH] = value
        r.big[erows, 0:H] += r.pext[1, erows]
        unit, rs = normed(r.big[erows])
        r.nm[rows] = unit.astype(BF16)
        r.rm[rows] = rs
        r.big[erows] = (unit * r.midp[0:1] + r.midp[1:2]).astype(BF16).astype(F32)

    loop(T // RM, left)
    edge_send(1, r.big[T : T + 8], r.big[8:16])
    g0(OUT)
    g2(POINT)
    g1(QKV)
    top, bottom = edge_take(1)
    r.big[0:8] = top
    r.big[T + 8 : T + 16] = bottom

    RC = 64

    def depthwise(j):
        cols = pl.ds(pl.multiple_of(j * 128, 128), 128)
        for k in range(T // RC):
            lo = k * RC
            total = r.big[lo + 8 : lo + 8 + RC, cols] * r.midp[6:7, cols]
            for o in (-4, -3, -2, -1, 1, 2, 3, 4):
                cells = r.big[lo + 8 + o : lo + 8 + o + RC, cols]
                total = total + cells * mask(o, lo, RC) * r.midp[6 + o : 7 + o, cols]
            r.sep[lo : lo + RC, cols] = total.astype(BF16)

    loop(FF // 128, depthwise)
    g0(FIN)
    g2(QKV)
    g1(OUT)
    g3(POINT)

    def point(i):
        rows = rows_of(i)
        y2 = r.y1[rows] + mm(r.sep[rows], r.w[POINT][...])
        r.y2[rows] = y2
        r.a4[rows] = ln_out(2, y2)

    loop(NB, point)
    g0(FOUT)
    g2(OUT)
    g1(FIN)
    g3(QKV)
    scale = 1.0 / math.sqrt(D // HEADS)

    def qkv(i):
        rows = rows_of(i)
        a4 = r.a4[rows]
        r.qb[rows] = (mm(a4, r.w[QKV][:, 0:D]) * scale).astype(BF16)
        r.kvb[c, rows, 0:D] = mm(a4, r.w[QKV][:, D : 2 * D]).astype(BF16)
        r.kvb[c, rows, D : 2 * D] = mm(a4, r.w[QKV][:, 2 * D : 3 * D]).astype(BF16)

    loop(NB, qkv)

    def kv_copy():
        blk = r.kvb.at[c]
        return remote(blk, blk, r.s_ks.at[0], r.s_kr.at[0], sibling)

    kv_copy().start()
    tokens_in(r.ct, r.cot, 1)
    lane = lax.broadcasted_iota(jnp.int32, (1, 128), 1)
    heads_lanes = [lane < 64, lane >= 64]
    g2(FIN)
    g1(FOUT)
    kv_copy().wait()

    def pair_cols(j, base=0):
        return pl.ds(pl.multiple_of(j * 128 + base, 128), 128)

    def one_head(q2, part, mine, key_row):
        def scores(keys, segs):
            raw = mm_t(q2, keys)
            same = jnp.concatenate([mine] * (T // 128), axis=1) == segs
            return jnp.where(same, raw, NEG)

        s0 = scores(part[0], key_row[:, 0:T])
        s1 = scores(part[1], key_row[:, T : 2 * T])
        most = jnp.maximum(
            jnp.max(s0, axis=-1, keepdims=True), jnp.max(s1, axis=-1, keepdims=True)
        )
        e0, e1 = jnp.exp(s0 - most), jnp.exp(s1 - most)
        total = jnp.sum(e0, axis=-1, keepdims=True) + jnp.sum(e1, axis=-1, keepdims=True)
        got = mm(e0.astype(BF16), part[2]) + mm(e1.astype(BF16), part[3])
        return got / total, most + jnp.log(total)

    def attend(j):
        cols, vcols = pair_cols(j), pair_cols(j, D)
        part = [r.kvb[0, :, cols], r.kvb[1, :, cols], r.kvb[0, :, vcols], r.kvb[1, :, vcols]]
        key_row = r.segrow[0:1]
        for k in range(T // RB):
            rows = slice(k * RB, (k + 1) * RB)
            q2 = r.qb[rows, cols]
            mine = r.segloc[8 + k * RB : 8 + (k + 1) * RB]
            got = []
            for e in range(2):
                context, lse = one_head(
                    jnp.where(heads_lanes[e], q2, jnp.zeros_like(q2)), part, mine, key_row
                )
                got.append(context)
                r.lse[rows] = jnp.where(lane == 2 * j + e, lse, r.lse[rows])
            r.ctx[rows, cols] = jnp.where(heads_lanes[0], got[0], got[1]).astype(BF16)

    r.lse[...] = jnp.zeros((T, 128), F32)
    loop(HEADS // 2, attend)
    turned = r.lse[...].T
    for j in range(HEADS // 2):
        r.lset[j, 0:2] = turned[2 * j : 2 * j + 2]
    g2(FOUT)
    g3(OUT)

    def out(i):
        rows = rows_of(i)
        y3 = r.y2[rows] + mm(r.ctx[rows], r.w[OUT][...])
        r.y3[rows] = y3
        r.a5[rows] = ln_out(3, y3)

    loop(NB, out)
    g3(FIN)

    def ffn_in(i):
        rows = rows_of(i)
        a5 = r.a5[rows]
        for k in range(FF // CH):
            value, slope = gelu_both(mm(a5, r.w[FIN][:, k * CH : (k + 1) * CH]))
            r.hid[rows, k * CH : (k + 1) * CH] = value.astype(BF16)
            r.dg[rows, k * CH : (k + 1) * CH] = slope.astype(BF16)

    loop(NB, ffn_in)
    g3(FOUT)

    def ffn_out(i):
        rows = rows_of(i)
        r.osend[rows] = (r.y3[rows] + mm(r.hid[rows], r.w[FOUT][...])).astype(BF16)

    loop(NB, ffn_out)
    tokens_out(r.osend, r.o_out, 2)
    for w in range(WEIGHTS):
        gather_sent(w)

    tokens_in_done(r.cot, 1)

    def ffn_back(i):
        rows = rows_of(i)
        f4 = r.cot[rows]
        for k in range(FF // CH):
            cols = slice(k * CH, (k + 1) * CH)
            up = mm_t(f4, r.w[FOUT][cols])
            r.dg[rows, cols] = (up * r.dg[rows, cols].astype(F32)).astype(BF16)
        e = mm_t(r.dg[rows], r.w[FIN][...])
        r.gs[rows] = f4.astype(F32) + ln_back(3, e, r.y3[rows])

    loop(NB, ffn_back)
    GC = 256

    def grad_outer(k):
        cols = rows_of(k, GC)
        r.w[FOUT][cols] = mm_tn(r.hid[:, cols], r.cot[...]).astype(BF16)

    loop(FF // GC, grad_outer)
    reduce_start(FOUT)
    r.tr[...] = r.a5[...].T

    def grad_inner(k):
        cols = rows_of(k, GC)
        r.w[FIN][:, cols] = mm(r.tr[...], r.dg[:, cols]).astype(BF16)

    loop(FF // GC, grad_inner)
    reduce_start(FIN)
    pump()

    def out_back(i):
        rows = rows_of(i)
        f3 = r.gs[rows].astype(BF16)
        r.a5[rows] = f3
        r.hid[rows, 3 * D : 4 * D] = mm_t(f3, r.w[OUT][...]).astype(BF16)

    loop(NB, out_back)
    r.w[OUT][...] = mm_tn(r.ctx[...], r.a5[...]).astype(BF16)
    reduce_start(OUT)
    pump()

    QB = 256

    def attend_back(j):
        cols, vcols = pair_cols(j), pair_cols(j, D)
        for k in range(T // QB):
            rows = slice(k * QB, (k + 1) * QB)
            q2 = r.qb[rows, cols]
            d2 = r.hid[rows, pair_cols(j, 3 * D)]
            dq = jnp.zeros((QB, 128), F32)
            for e in range(2):
                qe = jnp.where(heads_lanes[e], q2, jnp.zeros_like(q2))
                de = jnp.where(heads_lanes[e], d2, jnp.zeros_like(d2))
                lse = r.lset[j, e : e + 1, rows]
                probs, dprobs = [], []
                for kk in range(2):
                    keys = r.kvb[kk, :, cols]
                    values = r.kvb[kk, :, vcols]
                    segs = r.segcol[8 + kk * T : 8 + (kk + 1) * T]
                    same = jnp.concatenate([segs] * (QB // 128), axis=1) == r.segq[0:1, rows]
                    probs.append(jnp.where(same, jnp.exp(mm_t(keys, qe) - lse), 0.0))
                    dprobs.append(mm_t(values, de))
                delta = jnp.sum(probs[0] * dprobs[0], axis=0, keepdims=True) + jnp.sum(
                    probs[1] * dprobs[1], axis=0, keepdims=True
                )
                for kk in range(2):
                    keys = r.kvb[kk, :, cols]
                    ds = (probs[kk] * (dprobs[kk] - delta)).astype(BF16)
                    span_k = slice(kk * T, (kk + 1) * T)
                    dk = mm(ds, qe)
                    dv = mm(probs[kk].astype(BF16), de)
                    if k == 0 and e == 0:
                        r.acc[0, span_k] = dk
                        r.acc[1, span_k] = dv
                    else:
                        r.acc[0, span_k] += dk
                        r.acc[1, span_k] += dv
                    ke = jnp.where(heads_lanes[e], keys, jnp.zeros_like(keys))
                    dq = dq + mm_tn(ds, ke)
            r.hid[rows, cols] = (dq * scale).astype(BF16)
        own = pl.ds(pl.multiple_of(c * T, T), T)
        other = pl.ds(pl.multiple_of(oc * T, T), T)
        r.big[0:T, cols] = r.acc[0, own]
        r.big[0:T, vcols] = r.acc[1, own]
        r.dg[:, cols] = r.acc[0, other].astype(BF16)
        r.dg[:, vcols] = r.acc[1, other].astype(BF16)

    for half in range(2):
        lax.fori_loop(half * 2, half * 2 + 2, lambda j, _: (attend_back(j), 0)[1], 0)
        pump(2)

    def dkv_copy():
        return remote(
            r.dg.at[:, pl.ds(0, 2 * D)], r.dkvr, r.s_ks.at[1], r.s_kr.at[1], sibling
        )

    dkv_copy().start()
    pump()
    dkv_copy().wait()

    def qkv_back(i):
        rows = rows_of(i)
        total = r.big[rows, 0 : 2 * D] + r.dkvr[rows].astype(F32)
        r.hid[rows, D : 3 * D] = total.astype(BF16)
        e = mm_t(r.hid[rows, 0 : 3 * D], r.w[QKV][...])
        r.gs[rows] += ln_back(2, e, r.y2[rows])

    loop(NB, qkv_back)
    r.tr[...] = r.a4[...].T

    def grad_qkv(k):
        cols = rows_of(k, GC)
        r.w[QKV][:, cols] = mm(r.tr[...], r.hid[:, cols]).astype(BF16)

    loop(3 * D // GC, grad_qkv)
    reduce_start(QKV)
    pump()

    def point_back(i):
        rows = rows_of(i)
        f2 = r.gs[rows].astype(BF16)
        r.a4[rows] = f2
        for k in range(FF // CH):
            cols = slice(k * CH, (k + 1) * CH)
            d = mm_t(f2, r.w[POINT][cols])
            r.big[rows_of(i, RB, 8), cols] = d.astype(BF16).astype(F32)

    loop(NB, point_back)
    edge_send(2, r.big[T : T + 8], r.big[8:16])

    def grad_point(k):
        cols = rows_of(k, GC)
        r.w[POINT][cols] = mm_tn(r.sep[:, cols], r.a4[...]).astype(BF16)

    loop(FF // GC, grad_point)
    reduce_start(POINT)
    pump()
    top, bottom = edge_take(2)
    r.big[0:8] = top
    r.big[T + 8 : T + 16] = bottom

    def depth_back(j):
        cols = pl.ds(pl.multiple_of(j * 128, 128), 128)
        gain, shift = r.midp[0:1, cols], r.midp[1:2, cols]
        sums = [jnp.zeros((8, 128), F32) for _ in range(9)]
        for k in range(T // RC):
            lo = k * RC
            a3 = r.nm[lo : lo + RC, cols].astype(F32) * gain + shift
            total = jnp.zeros((RC, 128), F32)
            for o in range(-4, 5):
                moved = r.big[lo + 8 - o : lo + 8 - o + RC, cols]
                if o:
                    moved = moved * mask(-o, lo, RC)
                total = total + moved * r.midp[6 + o : 7 + o, cols]
                part = moved * a3
                for b in range(RC // 8):
                    sums[o + 4] = sums[o + 4] + part[b * 8 : (b + 1) * 8]
            r.col[lo : lo + RC] = total
        for o in range(9):
            r.g8[2 + o : 3 + o, cols] = jnp.sum(sums[o], axis=0, keepdims=True)
        r.big[8 : T + 8, cols] = r.col[...]

    loop(FF // 128, depth_back)
    pump()

    def mid_back(i):
        rows, erows = rows_of(i, RM), rows_of(i, RM, 8)
        e = r.big[erows]
        unit = r.nm[rows].astype(F32)
        eg = e * r.midp[0:1]
        m1 = jnp.mean(eg, axis=-1, keepdims=True)
        m2 = jnp.mean(eg * unit, axis=-1, keepdims=True)
        r.g8[0:1] += jnp.sum(e * unit, axis=0, keepdims=True)
        r.g8[1:2] += jnp.sum(e, axis=0, keepdims=True)
        dmid = r.rm[rows] * (eg - m1 - unit * m2)
        r.dgl[rows] = (dmid * r.dgl[rows].astype(F32)).astype(BF16)
        right = dmid[:, 0:H] * r.dgr[rows].astype(F32)
        r.pext[0, erows] = right.astype(BF16).astype(F32)

    loop(T // RM, mid_back)
    edge_send(3, r.pext[0, T : T + 8], r.pext[0, 8:16])
    pump()
    top, bottom = edge_take(3)
    r.pext[0, 0:8] = top
    r.pext[0, T + 8 : T + 16] = bottom
    for k in range(T // 128):
        lo = k * 128
        for o in (-1, 0, 1):
            moved = r.pext[0, lo + 8 - o : lo + 136 - o]
            if o:
                moved = moved * jnp.concatenate([mask(-o, lo, 128)] * (H // 128), axis=1)
            r.hid[lo : lo + 128, (o + 1) * H : (o + 2) * H] = moved.astype(BF16)

    def branch_back(i):
        rows = rows_of(i)
        e = mm_t(r.dgl[rows], r.w[LEFT][...])
        for o in range(3):
            e = e + mm_t(r.hid[rows, o * H : (o + 1) * H], r.w[CONV][o])
        r.gs[rows] += ln_back(1, e, r.y1[rows])

    loop(NB, branch_back)
    r.tr[...] = r.a2[...].T

    def grad_left(k):
        cols = rows_of(k, GC)
        r.w[LEFT][:, cols] = mm(r.tr[...], r.dgl[:, cols]).astype(BF16)

    loop(FF // GC, grad_left)
    reduce_start(LEFT)
    for o in range(3):
        r.w[CONV][o] = mm(r.tr[...], r.hid[:, o * H : (o + 1) * H]).astype(BF16)
    reduce_start(CONV)
    pump()

    def glu_back(i):
        rows = rows_of(i)
        g = r.gs[rows]
        r.sg[rows, 0:D] = (g * r.sg[rows, 0:D].astype(F32)).astype(BF16)
        r.sg[rows, D : 2 * D] = (g * r.sg[rows, D : 2 * D].astype(F32)).astype(BF16)
        e = mm_t(r.sg[rows], r.w[GLU][...])
        total = g + ln_back(0, e, r.xin[rows].astype(F32))
        r.a5[rows] = total.astype(BF16)

    loop(NB, glu_back)
    tokens_out(r.a5, r.o_ig, 3)
    r.tr[...] = r.a1[...].T

    def grad_glu(k):
        cols = rows_of(k, GC)
        r.w[GLU][:, cols] = mm(r.tr[...], r.sg[:, cols]).astype(BF16)

    loop(2 * D // GC, grad_glu)
    reduce_start(GLU)
    reduce_start(SMALL)
    while any(steps for _, steps in active):
        pump()

    for w in range(WEIGHTS + 1):
        red_end(w)
    tokens_out_done(r.osend, r.o_out, 2)
    tokens_out_done(r.a5, r.o_ig, 3)
    tokens_in_sent(r.x, r.xin, 0)
    tokens_in_sent(r.ct, r.cot, 1)
    seg_sent()
    for t in range(1, n):
        small_copy(t).wait_send()


def local(
    inputs,
    segment_ids,
    cotangent,
    norm_gain,
    norm_bias,
    glu_weight,
    left_weight,
    conv_weight,
    mid_gain,
    mid_bias,
    depth_weight,
    point_weight,
    qkv_weight,
    out_weight,
    ffn_in,
    ffn_out,
):
    seqs, span, width = inputs.shape
    n = lax.axis_size("seq")
    plan = Plan(
        lax.axis_size("dp"), n, seqs, span, width, ffn_in.shape[1], conv_weight.shape[2]
    )
    q = lax.axis_index("seq")

    def placed(piece, repeats):
        if repeats == 1:
            return piece
        size = piece.shape[-1]
        tiled = jnp.tile(piece, (1,) * (piece.ndim - 1) + (repeats,))
        at = lax.broadcasted_iota(jnp.int32, tiled.shape, tiled.ndim - 1) // size
        return jnp.where(at == q % repeats, tiled, jnp.zeros_like(tiled))

    segs = placed(segment_ids.astype(F32), plan.sr)
    segs = jnp.broadcast_to(segs[:, None, :], (seqs, 8, plan.sw))
    norms = placed(jnp.concatenate([norm_gain, norm_bias], 0), plan.nr)
    norms = jnp.pad(norms, ((0, 0), (0, plan.FFn - plan.nw)))
    small = jnp.concatenate([norms, mid_gain[None], mid_bias[None], depth_weight], 0)
    small = jnp.pad(small, ((0, 32 - small.shape[0]), (0, 0)))
    weights = [None] * WEIGHTS
    weights[GLU], weights[CONV], weights[LEFT] = glu_weight, conv_weight, left_weight
    weights[POINT], weights[QKV], weights[OUT] = point_weight, qkv_weight, out_weight
    weights[FIN], weights[FOUT] = ffn_in, ffn_out

    shapes = []
    plan.buffers(shapes.append)
    out_shape = [jax.ShapeDtypeStruct(inputs.shape, BF16)] * 2
    out_shape += [jax.ShapeDtypeStruct(w.shape, BF16) for w in weights]
    out_shape += [jax.ShapeDtypeStruct((16, plan.FF), F32)]
    hbm = pl.BlockSpec(memory_space=pl.ANY)
    got = pl.pallas_call(
        lambda *refs: kernel(plan, *refs),
        out_shape=out_shape,
        in_specs=[hbm] * INPUTS,
        out_specs=[hbm] * OUTPUTS,
        scratch_shapes=shapes,
        compiler_params=pltpu.CompilerParams(
            collective_id=0, has_side_effects=True, vmem_limit_bytes=64 << 20
        ),
        name="cell",
    )(inputs, segs, cotangent, small, *weights)
    output, input_grad = got[0].astype(F32), got[1].astype(F32)
    grads = [g.astype(F32) for g in got[2 : 2 + WEIGHTS]]
    rest = got[2 + WEIGHTS]
    mids = lax.dynamic_slice_in_dim(rest[0:11], q * plan.FFn, plan.FFn, 1)
    dn = width // n
    g_gain = lax.dynamic_slice_in_dim(rest[11].reshape(4, width), q * dn, dn, 1)
    g_bias = lax.dynamic_slice_in_dim(rest[12].reshape(4, width), q * dn, dn, 1)
    return (
        output,
        input_grad,
        g_gain,
        g_bias,
        grads[GLU],
        grads[LEFT],
        grads[CONV],
        mids[0],
        mids[1],
        mids[2:11],
        grads[POINT],
        grads[QKV],
        grads[OUT],
        grads[FIN],
        grads[FOUT],
    )


def solution(mesh):
    in_specs = (
        P("dp", "seq", None),
        P("dp", "seq"),
        P("dp", "seq", None),
        P(None, "seq"),
        P(None, "seq"),
        P("seq", None),
        P("seq", None),
        P(None, "seq", None),
        P("seq"),
        P("seq"),
        P(None, "seq"),
        P("seq", None),
        P("seq", None),
        P("seq", None),
        P("seq", None),
        P("seq", None),
    )
    out_specs = (
        P("dp", "seq", None),
        P("dp", "seq", None),
        P(None, "seq"),
        P(None, "seq"),
        P("seq", None),
        P("seq", None),
        P(None, "seq", None),
        P("seq"),
        P("seq"),
        P(None, "seq"),
        P("seq", None),
        P("seq", None),
        P("seq", None),
        P("seq", None),
        P("seq", None),
    )
    return jax.shard_map(local, mesh=mesh, in_specs=in_specs, out_specs=out_specs, check_vma=False)
```

time: 858 us -> 294 us (0.34)
  waiting for transfers between devices: 399 us -> 0 us
  Pallas kernels: 0 us -> 273 us
  matrix products: 124 us -> 0 us
  blocking collectives: 115 us -> 0 us
  other arithmetic: 108 us -> 13 us
  local copies, waits for them, and re-layouts: 62.3 us -> 6.24 us
  starting transfers between devices: 24.6 us -> 0 us
  between operations: 17.1 us -> 0.71 us
    pallas_call x0 -> x1, Pallas kernels: none -> 273 us  [local(): pl.pallas_call(lambda *refs: kernel(plan, *refs), out_shape=out_shape, in...]
    reduce_scatter x11 -> x0, waiting for transfers between devices: 224 us -> none  [the longest x1 38.3 us: local(): lax.psum_scatter(g_left.astype(jnp.bfloat16), 'seq', scatter_dimension=0,...]
    dot_general x36 -> x0, matrix products: 124 us -> none  [the longest x10 29.3 us: product(): return jnp.dot(left, right, preferred_element_type=jnp.float32)]
    all_gather x7 -> x0, waiting for transfers between devices: 80.4 us -> none  [the longest x1 42.8 us: attend(): whole_kv = lax.all_gather(kv_part, 'seq', axis=1, tiled=True)]
    all_gather x8 -> x0, blocking collectives: 76.8 us -> none  [the longest x1 14.2 us: local(): lax.all_gather(out_weight, 'seq', axis=0, tiled=True)]
    psum x1 -> x0, waiting for transfers between devices: 49.8 us -> none  [local(): lax.psum(owned[2].astype(jnp.bfloat16), 'dp').astype(jnp.float32)]
    reduce_sum x17 -> x0, other arithmetic: 46.5 us -> none  [the longest x3 21.7 us: layer_norm(): return centred * lax.rsqrt(spread + EPS) * gain + bias]
    unnamed x23 -> x0, waiting for transfers between devices: 40.1 us -> none
  transfers between devices with their start and end apart: 29 -> 0, of which waited for: 17 -> 0; matrix products, arithmetic and copies ran while one was open for 27% -> 0% of each run, Pallas kernels for 0% -> 0%
where the time goes in v1:
time: 294 us; the launch traced here: 293 us
  Pallas kernels  273 us (93%)
  other arithmetic  13 us (4%)
  local copies, waits for them, and re-layouts  6.24 us (2%)
    pallas_call x1, Pallas kernels, local(): pl.pallas_call(lambda *refs: kernel(plan, *refs), out_shape=out_shape, in...  273 us
    convert_element_type x8, other arithmetic, local(): grads = [g.astype(F32) for g in got[2:2 + WEIGHTS]]  7.64 us

profile of v1, /device:TPU:0, one launch (start us, length us, event | category | flops | bytes accessed | tf_op | source)
XLA Modules:
  0.0 293.1 jit_solution(16593739980070429167)
XLA Ops:
  0.6 0.0 copy-start.10
  0.7 0.7 fusion.9
  1.4 0.0 copy-done.10
  1.4 0.0 copy-start.11
  1.4 0.7 copy-done.11
  2.1 0.0 copy-start.9
  2.1 1.4 fusion.6.refs_3_
  3.4 0.0 copy-done.9
  3.4 0.6 broadcast_in_dim.12.refs_1_
  4.0 273.1 %cell.1 = (bf16[2,256,512]{2,1,0:T(8,128)(2,1)}, bf16[2,256,512]{2,1,0:T(8,128)(2,1)}, bf16[128,1024]{1,0:T(8,128)(2,1)}, bf16[3,128,256]{2,1,0:T(8,128)(2,1)}, ...) custom-call(bf16[2,256,512]{2,1,0:T(8,128)(2,1)} %refs_0_.1, ...), custom_call_target="tpu_custom_call" | custom-call | tf_op jit(solution)/shard_map/cell/pallas_call | solution.py:1218
  277.2 1.0 slice_reduce_fusion
  278.2 0.6 constant_dynamic-slice_fusion.1
  278.7 1.4 fusion.10
  280.2 1.5 dynamic-slice.2
  281.6 0.0 copy-start.4
  281.6 2.2 convert_element_type.38
  283.8 0.0 copy-done.4
  283.8 0.0 copy-start.3
  283.9 1.1 convert_element_type.39
  284.9 0.0 copy-done.3
  285.0 0.0 copy-start.2
  285.0 1.1 convert_element_type.41
  286.0 0.1 copy-done.2
  286.1 0.0 copy-start.1
  286.1 1.1 convert_element_type.43
  287.2 0.0 copy-done.1
  287.2 0.0 copy-start
  287.2 1.1 convert_element_type.46
  288.3 0.1 copy-done
  288.3 0.0 copy-start.5
  288.3 1.1 convert_element_type.47
  289.4 0.0 copy-done.5
  289.4 0.0 copy-start.6
  289.4 1.0 convert_element_type.44
  290.4 0.0 copy-done.6
  290.4 0.0 copy-start.7
  290.4 0.8 convert_element_type.40
  291.2 0.2 copy-done.7
  291.4 0.0 copy-start.8
  291.4 0.8 convert_element_type.42
  292.2 0.2 copy-done.8
  292.3 0.7 convert_element_type.45
  (5 shorter events, 0.0 us)
Async XLA Ops:
  0.6 0.7 copy-start.10
  1.4 0.7 copy-start.11
  2.1 1.4 copy-start.9
  281.6 2.2 copy-start.4
  283.8 1.1 copy-start.3
  285.0 1.1 copy-start.2
  286.1 1.1 copy-start.1
  287.2 1.1 copy-start
  288.3 1.1 copy-start.5
  289.4 1.0 copy-start.6
  290.4 1.0 copy-start.7
  291.4 1.0 copy-start.8

commit v2 on v1

--- a/solution.py
+++ b/solution.py
@@ -16,7 +16,10 @@
 
 GLU, CONV, LEFT, POINT, QKV, OUT, FIN, FOUT = range(8)
 WEIGHTS = 8
-SMALL = 8
+(U_GLU0, U_GLU1, U_CONV, U_LEFT0, U_LEFT1, U_POINT0, U_POINT1, U_QKV, U_OUT, U_FIN, U_FOUT, SMALL) = range(12)
+UNITS = 12
+UNIT_WEIGHT = (GLU, GLU, CONV, LEFT, LEFT, POINT, POINT, QKV, OUT, FIN, FOUT, WEIGHTS)
+UNIT_PART = (0, 1, None, 0, 1, 0, 1, None, None, None, None, None)
 
 
 def mm(a, b):
@@ -111,8 +114,10 @@
         parts = [(self.piece(w, self.hr(w)), BF16) for w in every] + [((8, FF), F32)]
         r.w = [vm(self.whole(w), BF16) for w in every]
         r.g8 = vm((16, FF), F32)
-        r.g = r.w + [r.g8]
-        r.r = [vm(self.piece(w, n * self.hr(w)), BF16) for w in every] + [vm((8, FF), F32)]
+        r.r = [None] * WEIGHTS + [vm((8, FF), F32)]
+        for w in (CONV, QKV, OUT, FIN, FOUT):
+            r.r[w] = vm(self.piece(w, n * self.hr(w)), BF16)
+        r.r[LEFT], r.r[POINT], r.r[GLU] = r.r[FIN], r.r[FOUT], r.r[QKV]
         r.p = [vm((n - 1,) + shape, dtype) for shape, dtype in parts]
         if self.Z > 1:
             r.u = [vm(shape, dtype) for shape, dtype in parts]
@@ -166,15 +171,15 @@
         r.s_br = sem(WEIGHTS, self.A * self.B)
         r.s_ds = sem(WEIGHTS, n)
         r.s_dr = sem(WEIGHTS, n)
-        r.s_rs = sem(WEIGHTS + 1, n)
-        r.s_rr = sem(WEIGHTS + 1, n)
-        r.s_ps = sem(WEIGHTS + 1, n)
-        r.s_pr = sem(WEIGHTS + 1, n)
-        r.s_zs = sem(WEIGHTS + 1, 2)
-        r.s_zr = sem(WEIGHTS + 1, 2)
-        r.s_fs = sem(WEIGHTS + 1)
-        r.s_fr = sem(WEIGHTS + 1)
-        r.s_fl = sem(WEIGHTS + 1)
+        r.s_rs = sem(UNITS, n)
+        r.s_rr = sem(UNITS, n)
+        r.s_ps = sem(UNITS, n)
+        r.s_pr = sem(UNITS, n)
+        r.s_zs = sem(UNITS, 2)
+        r.s_zr = sem(UNITS, 2)
+        r.s_fs = sem(UNITS)
+        r.s_fr = sem(UNITS)
+        r.s_fl = sem(UNITS)
         r.s_xs = sem(4, self.S)
         r.s_xr = sem(4, max(self.PH, self.S))
         r.s_gs = sem(2 * self.S)
@@ -479,171 +484,199 @@
         got = r.er[i][...]
         return jnp.where(c == 1, got, 0.0), jnp.where(c == 0, got, 0.0)
 
-    def gpiece(w, shard, half):
-        if w == SMALL:
+    def columns(u):
+        half = UNIT_PART[u]
+        if half is None:
+            return None
+        size = plan.dims[UNIT_WEIGHT[u]][1] // 2
+        return pl.ds(half * size, size)
+
+    def urows(ref, u, row0, rows):
+        cols = columns(u)
+        if cols is None:
+            return vrows(ref, UNIT_WEIGHT[u], row0, rows)
+        return ref.at[pl.ds(aligned(row0), rows), cols]
+
+    def gpiece(u, shard, half):
+        if u == SMALL:
             return r.g8.at[pl.ds(pl.multiple_of(half * 8, 8), 8)]
-        return vrows(r.w[w], w, shard * plan.kr(w) + half * plan.hr(w), plan.hr(w))
-
-    def rpiece(w, shard):
-        if w == SMALL:
-            return r.r[SMALL]
-        return vrows(r.r[w], w, shard * plan.hr(w), plan.hr(w))
-
-    def copy_r(w, s):
+        w = UNIT_WEIGHT[u]
+        row0 = shard * plan.kr(w) + half * plan.hr(w)
+        if w == GLU:
+            size = plan.D
+            cols = pl.ds(2 * D + UNIT_PART[u] * size, size)
+            return r.hid.at[pl.ds(aligned(row0), plan.hr(w)), cols]
+        return urows(r.dg if w == LEFT else r.w[w], u, row0, plan.hr(w))
+
+    def rpiece(u, shard):
+        w = UNIT_WEIGHT[u]
+        if u == SMALL:
+            return r.r[w]
+        return urows(r.r[w], u, shard * plan.hr(w), plan.hr(w))
+
+    def ppiece(u, slot):
+        cols = columns(u)
+        buf = r.p[UNIT_WEIGHT[u]]
+        return buf.at[slot] if cols is None else buf.at[slot, :, cols]
+
+    def zpiece(u, way):
+        cols = columns(u)
+        buf = (r.u, r.d)[way][UNIT_WEIGHT[u]]
+        return buf if cols is None else buf.at[:, cols]
+
+    def copy_r(u, s):
         return remote(
-            gpiece(w, s, oc), rpiece(w, s), r.s_rs.at[w, s], r.s_rr.at[w, s], sibling
+            gpiece(u, s, oc), rpiece(u, s), r.s_rs.at[u, s], r.s_rr.at[u, s], sibling
         )
 
-    def copy_p(w, t):
+    def copy_p(u, t):
         chip = lax.rem(q + t, n)
         return remote(
-            gpiece(w, chip, c),
-            r.p[w].at[t - 1],
-            r.s_ps.at[w, t],
-            r.s_pr.at[w, t],
+            gpiece(u, chip, c),
+            ppiece(u, t - 1),
+            r.s_ps.at[u, t],
+            r.s_pr.at[u, t],
             dev(c, chip),
         )
 
-    def shards(w):
-        return 1 if w == SMALL else n
-
-    def red0(w):
-        for s in range(shards(w)):
-            copy_r(w, s).start()
-
-    def add_core(w, s):
-        copy_r(w, s).wait_recv()
-        mine = gpiece(w, s, c)
-        total = mine[...].astype(F32) + rpiece(w, s)[...].astype(F32)
+    def shards(u):
+        return 1 if u == SMALL else n
+
+    def red0(u):
+        for s in range(shards(u)):
+            copy_r(u, s).start()
+
+    def plus(a, b):
+        return a[...].astype(F32) + b[...].astype(F32)
+
+    def add_core(u, s):
+        copy_r(u, s).wait_recv()
+        mine = gpiece(u, s, c)
+        mine[...] = plus(mine, rpiece(u, s)).astype(mine.dtype)
+
+    def red1(u):
+        if u == SMALL:
+            add_core(u, 0)
+
+        def one(t, _):
+            if u != SMALL:
+                add_core(u, lax.rem(q + t, n))
+            copy_p(u, t).start()
+            return 0
+
+        lax.fori_loop(1, n, one, 0)
+        if u != SMALL:
+            add_core(u, q)
+
+    def red2(u):
+        total = gpiece(u, q, c)[...].astype(F32)
+        for t in range(1, n):
+            copy_p(u, t).wait_recv()
+            total = total + ppiece(u, t - 1)[...].astype(F32)
+        mine = ppiece(u, 0)
         mine[...] = total.astype(mine.dtype)
 
-    def red1(w):
-        if w == SMALL:
-            add_core(w, 0)
-
-        def one(t, _):
-            if w != SMALL:
-                add_core(w, lax.rem(q + t, n))
-            copy_p(w, t).start()
-            return 0
-
-        lax.fori_loop(1, n, one, 0)
-        if w != SMALL:
-            add_core(w, q)
-
-    def red2(w):
-        buf = r.p[w]
-        mine = gpiece(w, q, c)
-        total = mine[...].astype(F32)
-        for t in range(1, n):
-            copy_p(w, t).wait_recv()
-            total = total + buf[t - 1].astype(F32)
-        buf[0] = total.astype(buf.dtype)
-
-    def copy_z(w, way):
-        plane = z + 1 if way == 0 else z - 1
+    def copy_z(u, way):
         return remote(
-            r.p[w].at[1 + way],
-            (r.u, r.d)[way][w],
-            r.s_zs.at[w, way],
-            r.s_zr.at[w, way],
-            dev(c, q, plane),
+            ppiece(u, 1 + way),
+            zpiece(u, way),
+            r.s_zs.at[u, way],
+            r.s_zr.at[u, way],
+            dev(c, q, z + 1 if way == 0 else z - 1),
         )
 
-    def red_hop(w, h):
-        buf = r.p[w]
+    def red_hop(u, h):
+        own, up, down = ppiece(u, 0), ppiece(u, 1), ppiece(u, 2)
 
         @pl.when(z == h)
         def _():
             if h == 0:
-                buf[1] = buf[0]
+                up[...] = own[...]
             else:
-                copy_z(w, 0).wait_recv()
-                buf[1] = (buf[0].astype(F32) + r.u[w][...].astype(F32)).astype(buf.dtype)
+                copy_z(u, 0).wait_recv()
+                up[...] = plus(own, zpiece(u, 0)).astype(up.dtype)
             if h < Z - 1:
-                copy_z(w, 0).start()
+                copy_z(u, 0).start()
 
         @pl.when(z == Z - 1 - h)
         def _():
             if h == 0:
-                buf[2] = buf[0]
+                down[...] = own[...]
             else:
-                copy_z(w, 1).wait_recv()
+                copy_z(u, 1).wait_recv()
                 if h < Z - 1:
-                    buf[2] = (buf[0].astype(F32) + r.d[w][...].astype(F32)).astype(buf.dtype)
+                    down[...] = plus(own, zpiece(u, 1)).astype(down.dtype)
             if h < Z - 1:
-                copy_z(w, 1).start()
-
-    def final_rows(w, ref):
-        if w == SMALL:
-            return ref.at[pl.ds(pl.multiple_of(c * 8, 8), 8)]
-        return vrows(ref, w, c * plan.hr(w), plan.hr(w))
-
-    def final_local(w):
-        return pltpu.make_async_copy(
-            r.p[w].at[0], final_rows(w, r.o[w]), r.s_fl.at[w]
-        )
-
-    def final_remote(w):
-        return remote(
-            r.p[w].at[0],
-            final_rows(w, r.o[w]),
-            r.s_fs.at[w],
-            r.s_fr.at[w],
-            sibling,
-        )
-
-    def red_final(w):
-        buf = r.p[w]
+                copy_z(u, 1).start()
+
+    def final_rows(u):
+        w = UNIT_WEIGHT[u]
+        if u == SMALL:
+            return r.o[w].at[pl.ds(pl.multiple_of(c * 8, 8), 8)]
+        return urows(r.o[w], u, c * plan.hr(w), plan.hr(w))
+
+    def final_local(u):
+        return pltpu.make_async_copy(ppiece(u, 0), final_rows(u), r.s_fl.at[u])
+
+    def final_remote(u):
+        return remote(ppiece(u, 0), final_rows(u), r.s_fs.at[u], r.s_fr.at[u], sibling)
+
+    def red_final(u):
         if Z > 1:
+            own, up = ppiece(u, 0), ppiece(u, 1)
 
             @pl.when(z == Z - 1)
             def _():
-                buf[0] = buf[1]
+                own[...] = up[...]
 
             @pl.when(z < Z - 1)
             def _():
-                buf[0] = (buf[1].astype(F32) + r.d[w][...].astype(F32)).astype(buf.dtype)
-
-        final_local(w).start()
-        final_remote(w).start()
-
-    def red_end(w):
-        final_local(w).wait()
-        final_remote(w).wait()
-        for s in range(shards(w)):
-            copy_r(w, s).wait_send()
+                own[...] = plus(up, zpiece(u, 1)).astype(own.dtype)
+
+        final_local(u).start()
+        final_remote(u).start()
+
+    def red_end(u):
+        final_local(u).wait()
+        final_remote(u).wait()
+        for s in range(shards(u)):
+            copy_r(u, s).wait_send()
         for t in range(1, n):
-            copy_p(w, t).wait_send()
+            copy_p(u, t).wait_send()
         if Z > 1:
 
             @pl.when(z < Z - 1)
             def _():
-                copy_z(w, 0).wait_send()
+                copy_z(u, 0).wait_send()
 
             @pl.when(z > 0)
             def _():
-                copy_z(w, 1).wait_send()
-
-    active = []
-
-    def reduce_start(w):
-        red0(w)
-        steps = [red1, red2]
-        if Z > 1:
-            steps += [lambda k, h=h: red_hop(k, h) for h in range(Z)]
-        steps.append(red_final)
-        active.append((w, steps))
-
-    def pump(times=1):
-        for _ in range(times):
-            for w, steps in active:
-                if steps:
-                    steps.pop(0)(w)
-
-    def loop(count, body):
+                copy_z(u, 1).wait_send()
+
+    ahead = {}
+
+    def last_hop(u):
+        red_hop(u, Z - 1)
+        red_final(u)
+
+    def reduce_start(*units):
+        for u in units:
+            red0(u)
+            ahead[u] = [red1, red2]
+            if Z > 1:
+                ahead[u] += [lambda k, h=h: red_hop(k, h) for h in range(Z - 1)]
+            ahead[u].append(last_hop if Z > 1 else red_final)
+
+    def move(*units):
+        for u in units:
+            if ahead[u]:
+                ahead[u].pop(0)(u)
+
+    def loop(count, body, after=()):
         def step(i, _):
             body(i)
+            for k, act in after:
+                pl.when(i == k)(act)
             return 0
 
         lax.fori_loop(0, count, step, 0)
@@ -734,9 +767,9 @@
         r.a2[rows] = ln_out(1, y1)
 
     loop(NB, glu)
-    g0(POINT)
     g2(CONV)
     g1(LEFT)
+    g0(POINT)
     g3(CONV)
 
     def conv(i):
@@ -746,9 +779,9 @@
 
     loop(NB, conv)
     edge_send(0, r.pext[0, T : T + 8], r.pext[2, 8:16])
-    g0(QKV)
     g2(LEFT)
     g1(POINT)
+    g0(QKV)
     top, bottom = edge_take(0)
     r.pext[0, 0:8] = top
     r.pext[2, T + 8 : T + 16] = bottom
@@ -784,9 +817,9 @@
 
     loop(T // RM, left)
     edge_send(1, r.big[T : T + 8], r.big[8:16])
-    g0(OUT)
     g2(POINT)
     g1(QKV)
+    g0(OUT)
     top, bottom = edge_take(1)
     r.big[0:8] = top
     r.big[T + 8 : T + 16] = bottom
@@ -803,10 +836,13 @@
                 total = total + cells * mask(o, lo, RC) * r.midp[6 + o : 7 + o, cols]
             r.sep[lo : lo + RC, cols] = total.astype(BF16)
 
-    loop(FF // 128, depthwise)
-    g0(FIN)
-    g2(QKV)
-    g1(OUT)
+    def ahead_qkv():
+        g2(QKV)
+        g1(OUT)
+        g0(FIN)
+
+    loop(FF // 128, depthwise, [(7, ahead_qkv)])
+    g2(OUT)
     g3(POINT)
 
     def point(i):
@@ -816,9 +852,6 @@
         r.a4[rows] = ln_out(2, y2)
 
     loop(NB, point)
-    g0(FOUT)
-    g2(OUT)
-    g1(FIN)
     g3(QKV)
     scale = 1.0 / math.sqrt(D // HEADS)
 
@@ -839,8 +872,8 @@
     tokens_in(r.ct, r.cot, 1)
     lane = lax.broadcasted_iota(jnp.int32, (1, 128), 1)
     heads_lanes = [lane < 64, lane >= 64]
-    g2(FIN)
-    g1(FOUT)
+    g1(FIN)
+    g0(FOUT)
     kv_copy().wait()
 
     def pair_cols(j, base=0):
@@ -880,7 +913,11 @@
             r.ctx[rows, cols] = jnp.where(heads_lanes[0], got[0], got[1]).astype(BF16)
 
     r.lse[...] = jnp.zeros((T, 128), F32)
-    loop(HEADS // 2, attend)
+    def ahead_fin():
+        g2(FIN)
+        g1(FOUT)
+
+    loop(HEADS // 2, attend, [(1, ahead_fin)])
     turned = r.lse[...].T
     for j in range(HEADS // 2):
         r.lset[j, 0:2] = turned[2 * j : 2 * j + 2]
@@ -936,7 +973,7 @@
         r.w[FOUT][cols] = mm_tn(r.hid[:, cols], r.cot[...]).astype(BF16)
 
     loop(FF // GC, grad_outer)
-    reduce_start(FOUT)
+    reduce_start(U_FOUT)
     r.tr[...] = r.a5[...].T
 
     def grad_inner(k):
@@ -944,8 +981,8 @@
         r.w[FIN][:, cols] = mm(r.tr[...], r.dg[:, cols]).astype(BF16)
 
     loop(FF // GC, grad_inner)
-    reduce_start(FIN)
-    pump()
+    reduce_start(U_FIN)
+    move(U_FOUT)
 
     def out_back(i):
         rows = rows_of(i)
@@ -955,8 +992,7 @@
 
     loop(NB, out_back)
     r.w[OUT][...] = mm_tn(r.ctx[...], r.a5[...]).astype(BF16)
-    reduce_start(OUT)
-    pump()
+    reduce_start(U_OUT)
 
     QB = 256
 
@@ -1004,9 +1040,15 @@
         r.dg[:, cols] = r.acc[0, other].astype(BF16)
         r.dg[:, vcols] = r.acc[1, other].astype(BF16)
 
-    for half in range(2):
-        lax.fori_loop(half * 2, half * 2 + 2, lambda j, _: (attend_back(j), 0)[1], 0)
-        pump(2)
+    loop(
+        HEADS // 2,
+        attend_back,
+        [
+            (1, lambda: move(U_FIN)),
+            (2, lambda: move(U_FOUT, U_FOUT)),
+            (3, lambda: move(U_OUT)),
+        ],
+    )
 
     def dkv_copy():
         return remote(
@@ -1014,7 +1056,6 @@
         )
 
     dkv_copy().start()
-    pump()
     dkv_copy().wait()
 
     def qkv_back(i):
@@ -1032,8 +1073,7 @@
         r.w[QKV][:, cols] = mm(r.tr[...], r.hid[:, cols]).astype(BF16)
 
     loop(3 * D // GC, grad_qkv)
-    reduce_start(QKV)
-    pump()
+    reduce_start(U_QKV)
 
     def point_back(i):
         rows = rows_of(i)
@@ -1046,14 +1086,15 @@
 
     loop(NB, point_back)
     edge_send(2, r.big[T : T + 8], r.big[8:16])
+    move(U_FIN, U_FOUT, U_FIN, U_QKV)
 
     def grad_point(k):
         cols = rows_of(k, GC)
         r.w[POINT][cols] = mm_tn(r.sep[:, cols], r.a4[...]).astype(BF16)
 
     loop(FF // GC, grad_point)
-    reduce_start(POINT)
-    pump()
+    reduce_start(U_POINT0, U_POINT1)
+    move(U_OUT, U_OUT)
     top, bottom = edge_take(2)
     r.big[0:8] = top
     r.big[T + 8 : T + 16] = bottom
@@ -1079,8 +1120,16 @@
             r.g8[2 + o : 3 + o, cols] = jnp.sum(sums[o], axis=0, keepdims=True)
         r.big[8 : T + 8, cols] = r.col[...]
 
-    loop(FF // 128, depth_back)
-    pump()
+    loop(
+        FF // 128,
+        depth_back,
+        [
+            (3, lambda: move(U_POINT0, U_POINT1)),
+            (7, lambda: move(U_FOUT, U_FIN, U_OUT, U_QKV, U_QKV)),
+            (13, lambda: move(U_FOUT, U_FIN, U_OUT, U_QKV)),
+        ],
+    )
+    move(U_POINT0, U_POINT0)
 
     def mid_back(i):
         rows, erows = rows_of(i, RM), rows_of(i, RM, 8)
@@ -1098,7 +1147,19 @@
 
     loop(T // RM, mid_back)
     edge_send(3, r.pext[0, T : T + 8], r.pext[0, 8:16])
-    pump()
+    move(U_POINT1, U_POINT1, U_QKV)
+    r.tr[...] = r.a2[...].T
+
+    def grad_left(k):
+        cols = rows_of(k, GC)
+        r.dg[:, cols] = mm(r.tr[...], r.dgl[:, cols]).astype(BF16)
+
+    for half in range(2):
+        lax.fori_loop(
+            half * (FF // GC // 2), (half + 1) * (FF // GC // 2), lambda k, _: (grad_left(k), 0)[1], 0
+        )
+        reduce_start((U_LEFT0, U_LEFT1)[half])
+    move(U_POINT0, U_FIN, U_OUT)
     top, bottom = edge_take(3)
     r.pext[0, 0:8] = top
     r.pext[0, T + 8 : T + 16] = bottom
@@ -1117,45 +1178,49 @@
             e = e + mm_t(r.hid[rows, o * H : (o + 1) * H], r.w[CONV][o])
         r.gs[rows] += ln_back(1, e, r.y1[rows])
 
-    loop(NB, branch_back)
-    r.tr[...] = r.a2[...].T
-
-    def grad_left(k):
-        cols = rows_of(k, GC)
-        r.w[LEFT][:, cols] = mm(r.tr[...], r.dgl[:, cols]).astype(BF16)
-
-    loop(FF // GC, grad_left)
-    reduce_start(LEFT)
+    loop(NB, branch_back, [(0, lambda: move(U_LEFT0))])
+    move(U_LEFT1, U_QKV, U_POINT1)
     for o in range(3):
         r.w[CONV][o] = mm(r.tr[...], r.hid[:, o * H : (o + 1) * H]).astype(BF16)
-    reduce_start(CONV)
-    pump()
-
-    def glu_back(i):
+    reduce_start(U_CONV)
+    move(U_POINT0)
+
+    def gate_back(i):
         rows = rows_of(i)
         g = r.gs[rows]
         r.sg[rows, 0:D] = (g * r.sg[rows, 0:D].astype(F32)).astype(BF16)
         r.sg[rows, D : 2 * D] = (g * r.sg[rows, D : 2 * D].astype(F32)).astype(BF16)
-        e = mm_t(r.sg[rows], r.w[GLU][...])
-        total = g + ln_back(0, e, r.xin[rows].astype(F32))
-        r.a5[rows] = total.astype(BF16)
-
-    loop(NB, glu_back)
-    tokens_out(r.a5, r.o_ig, 3)
+
+    loop(NB, gate_back)
     r.tr[...] = r.a1[...].T
 
     def grad_glu(k):
         cols = rows_of(k, GC)
-        r.w[GLU][:, cols] = mm(r.tr[...], r.sg[:, cols]).astype(BF16)
+        to = pl.ds(pl.multiple_of(k * GC + 2 * D, GC), GC)
+        r.hid[:, to] = mm(r.tr[...], r.sg[:, cols]).astype(BF16)
 
     loop(2 * D // GC, grad_glu)
-    reduce_start(GLU)
+    move(U_CONV)
+    reduce_start(U_GLU0, U_GLU1)
+
+    def glu_back(i):
+        rows = rows_of(i)
+        e = mm_t(r.sg[rows], r.w[GLU][...])
+        total = r.gs[rows] + ln_back(0, e, r.xin[rows].astype(F32))
+        r.a5[rows] = total.astype(BF16)
+
+    loop(NB, glu_back)
     reduce_start(SMALL)
-    while any(steps for _, steps in active):
-        pump()
-
-    for w in range(WEIGHTS + 1):
-        red_end(w)
+    move(U_POINT1, U_LEFT0, U_LEFT0, U_GLU0, U_GLU1, SMALL)
+    tokens_out(r.a5, r.o_ig, 3)
+    move(U_POINT0, U_LEFT1, U_LEFT1, U_LEFT0, U_POINT1, U_CONV, U_CONV, U_LEFT1, U_LEFT0)
+    move(U_CONV, U_GLU0, U_GLU0, U_LEFT1, U_GLU1, U_GLU1, SMALL, SMALL, U_LEFT0, U_CONV)
+    move(U_GLU0, U_LEFT1, U_GLU1, SMALL, U_CONV, U_GLU0, U_GLU1, SMALL, U_GLU0, U_GLU1, SMALL)
+    while any(ahead.values()):
+        move(*range(UNITS))
+
+    for u in range(UNITS):
+        red_end(u)
     tokens_out_done(r.osend, r.o_out, 2)
     tokens_out_done(r.a5, r.o_ig, 3)
     tokens_in_sent(r.x, r.xin, 0)
@@ -1226,30 +1291,76 @@
         ),
         name="cell",
     )(inputs, segs, cotangent, small, *weights)
-    output, input_grad = got[0].astype(F32), got[1].astype(F32)
-    grads = [g.astype(F32) for g in got[2 : 2 + WEIGHTS]]
-    rest = got[2 + WEIGHTS]
-    mids = lax.dynamic_slice_in_dim(rest[0:11], q * plan.FFn, plan.FFn, 1)
-    dn = width // n
-    g_gain = lax.dynamic_slice_in_dim(rest[11].reshape(4, width), q * dn, dn, 1)
-    g_bias = lax.dynamic_slice_in_dim(rest[12].reshape(4, width), q * dn, dn, 1)
+    out = unpacked(plan, got)
     return (
-        output,
-        input_grad,
-        g_gain,
-        g_bias,
-        grads[GLU],
-        grads[LEFT],
-        grads[CONV],
-        mids[0],
-        mids[1],
-        mids[2:11],
-        grads[POINT],
-        grads[QKV],
-        grads[OUT],
-        grads[FIN],
-        grads[FOUT],
+        out[0],
+        out[1],
+        out[2 + WEIGHTS],
+        out[3 + WEIGHTS],
+        out[2 + GLU],
+        out[2 + LEFT],
+        out[2 + CONV],
+        out[4 + WEIGHTS].reshape(-1),
+        out[5 + WEIGHTS].reshape(-1),
+        out[6 + WEIGHTS],
+        out[2 + POINT],
+        out[2 + QKV],
+        out[2 + OUT],
+        out[2 + FIN],
+        out[2 + FOUT],
     )
+
+
+def unpacked(plan, parts):
+    count = 2 + WEIGHTS
+    dn = plan.D // plan.n
+    wide = [jax.ShapeDtypeStruct(p.shape, F32) for p in parts[:count]]
+    tiny = [(4, dn), (4, dn), (1, plan.FFn), (1, plan.FFn), (9, plan.FFn)]
+    out_shape = wide + [jax.ShapeDtypeStruct(shape, F32) for shape in tiny]
+
+    def body(*refs):
+        ins, outs = refs[:count], refs[count + 1 : 2 * count + 1]
+        sums, tinies = refs[count], refs[2 * count + 1 : 2 * count + 6]
+        near, far = refs[2 * count + 6 : 3 * count + 6], refs[3 * count + 6 : 4 * count + 6]
+        came, went = refs[4 * count + 6], refs[4 * count + 7]
+
+        def arrive(i):
+            return pltpu.make_async_copy(ins[i], near[i], came.at[i])
+
+        def leave(i):
+            return pltpu.make_async_copy(far[i], outs[i], went.at[i])
+
+        for i in range(count):
+            arrive(i).start()
+        q = lax.axis_index("seq")
+        rolled = pltpu.roll(sums[...], (plan.FF - q * plan.FFn) % plan.FF, 1)[:, 0 : plan.FFn]
+        tinies[2][...] = rolled[0:1]
+        tinies[3][...] = rolled[1:2]
+        tinies[4][...] = rolled[2:11]
+        for k in range(2):
+            row = sums[11 + k : 12 + k]
+            rows = [row[:, i * plan.D : (i + 1) * plan.D] for i in range(4)]
+            both = jnp.concatenate(rows + rows, axis=0)
+            tinies[k][...] = pltpu.roll(both, (plan.D - q * dn) % plan.D, 1)[0:4, 0:dn]
+        for i in range(count):
+            arrive(i).wait()
+            far[i][...] = near[i][...].astype(F32)
+            leave(i).start()
+        for i in range(count):
+            leave(i).wait()
+
+    hbm = pl.BlockSpec(memory_space=pl.ANY)
+    vmem = pl.BlockSpec(memory_space=pltpu.VMEM)
+    return pl.pallas_call(
+        body,
+        out_shape=out_shape,
+        in_specs=[hbm] * count + [vmem],
+        out_specs=[hbm] * count + [vmem] * len(tiny),
+        scratch_shapes=[pltpu.VMEM(p.shape, BF16) for p in parts[:count]]
+        + [pltpu.VMEM(p.shape, F32) for p in parts[:count]]
+        + [pltpu.SemaphoreType.DMA((count,))] * 2,
+        compiler_params=pltpu.CompilerParams(vmem_limit_bytes=64 << 20),
+    )(*parts)
 
 
 def solution(mesh):

time: 294 us -> 198 us (0.67)
  Pallas kernels: 273 us -> 194 us
  other arithmetic: 13 us -> 1.33 us
  local copies, waits for them, and re-layouts: 6.24 us -> 1.38 us
    pallas_call x1, Pallas kernels: 273 us -> 188 us  [local(): pl.pallas_call(lambda *refs: kernel(plan, *refs), out_shape=out_shape, in...]
    convert_element_type x10 -> x0, other arithmetic: 10.9 us -> none  [the longest x8 7.64 us: local(): grads = [g.astype(F32) for g in got[2:2 + WEIGHTS]]]
    pallas_call x0 -> x1, Pallas kernels: none -> 6.13 us  [unpacked(): pl.pallas_call(body, out_shape=out_shape, in_specs=[hbm] * count + [vmem]...]
    slice x3 -> x0, local copies, waits for them, and re-layouts: 3.86 us -> none  [the longest x1 1.45 us: local(): mids[2:11]]
where the time goes in v2:
time: 198 us
  Pallas kernels  194 us (98%)
    pallas_call x1, Pallas kernels, local(): pl.pallas_call(lambda *refs: kernel(plan, *refs), out_shape=out_shape, in...  188 us
    pallas_call x1, Pallas kernels, unpacked(): pl.pallas_call(body, out_shape=out_shape, in_specs=[hbm] * count + [vmem]...  6.13 us

profile of v2, /device:TPU:0, one launch (start us, length us, event | category | flops | bytes accessed | tf_op | source)
XLA Modules:
  0.0 197.8 jit_solution(15325986460530904505)
XLA Ops:
  0.6 0.0 copy-start.1
  0.7 0.7 convert_element_type.7
  1.3 0.0 copy-done.1
  1.3 0.0 copy-start.2
  1.4 0.0 copy-start.3
  1.4 0.0 copy-start.4
  1.4 0.7 copy-done.2
  2.0 0.0 copy-start
  2.0 0.0 copy-done.3
  2.0 0.0 copy-done.4
  2.1 0.6 broadcast_in_dim.12.refs_1_
  2.7 0.1 copy-done
  2.7 0.6 fusion.6.refs_3_
  3.4 188.1 %cell.1 = (bf16[2,256,512]{2,1,0:T(8,128)(2,1)}, bf16[2,256,512]{2,1,0:T(8,128)(2,1)}, bf16[128,1024]{1,0:T(8,128)(2,1)}, bf16[3,128,256]{2,1,0:T(8,128)(2,1)}, ...) custom-call(bf16[2,256,512]{2,1,0:T(8,128)(2,1)} %refs_0_.1, ...), custom_call_target="tpu_custom_call" | custom-call | tf_op jit(solution)/shard_map/cell/pallas_call | solution.py:1283
  191.5 6.1 %shard_map.271 = (f32[2,256,512]{2,1,0:T(8,128)}, f32[2,256,512]{2,1,0:T(8,128)}, f32[128,1024]{1,0:T(8,128)}, f32[3,128,256]{2,1,0:T(8,128)}, f32[128,2048]{1,0...) custom-call(bf16[2,256,512]{2,1,0:T(8,128)(2,1)} %get-tuple-element., ...), custom_call_target="tpu_custom_call" | custom-call | tf_op jit(solution)/shard_map/pallas_call | solution.py:1354
  (3 shorter events, 0.0 us)
Async XLA Ops:
  0.6 0.7 copy-start.1
  1.3 0.7 copy-start.2
  1.4 0.7 copy-start.3
  1.4 0.7 copy-start.4
  2.0 0.7 copy-start

commit v3 on v2

--- a/solution.py
+++ b/solution.py
@@ -9,7 +9,6 @@
 
 HEADS = 8
 EPS = 1e-06
-NEG = -1000000000.0
 MESH = pl.DeviceIdType.MESH
 F32 = jnp.float32
 BF16 = jnp.bfloat16
@@ -18,6 +17,9 @@
 WEIGHTS = 8
 (U_GLU0, U_GLU1, U_CONV, U_LEFT0, U_LEFT1, U_POINT0, U_POINT1, U_QKV, U_OUT, U_FIN, U_FOUT, SMALL) = range(12)
 UNITS = 12
+
+MB, MW = 128, 256
+FAR = -(2.0**30)
 UNIT_WEIGHT = (GLU, GLU, CONV, LEFT, LEFT, POINT, POINT, QKV, OUT, FIN, FOUT, WEIGHTS)
 UNIT_PART = (0, 1, None, 0, 1, 0, 1, None, None, None, None, None)
 
@@ -69,6 +71,7 @@
         self.B = math.isqrt(n)
         self.A = n // self.B
         assert self.A == self.B and n == 2 * seqs and dp % 2 == 0
+        self.shared = (LEFT, POINT, FIN, FOUT) if self.Z % 2 == 0 else ()
         self.sw = max(span, 128)
         self.sr = self.sw // span
         dn = width // n
@@ -124,10 +127,12 @@
             r.d = [vm(shape, dtype) for shape, dtype in parts]
         r.segbuf = vm((n, 8, self.sw), F32)
         r.segrow = vm((8, self.LEN), F32)
-        r.segq = vm((8, T), F32)
         r.segcol = vm((self.LEN + 16, 128), F32)
         r.segloc = vm((T + 16, 128), F32)
-        r.mext = vm((4, T + 16, 128), F32)
+        r.mext = vm((T + 16, 128), F32)
+        r.ms = vm((T // MB, 9 * MB, MW), BF16)
+        r.qenc = vm((T, 128), BF16)
+        r.kenc = vm((self.LEN, 128), BF16)
         r.smallbuf = vm((n, 32, self.FFn), BF16)
         r.nrm = vm((8, D), F32)
         r.midp = vm((16, FF), F32)
@@ -147,36 +152,36 @@
         r.y2 = vm((T, D), F32)
         r.a4 = vm((T, D), BF16)
         r.qb = vm((T, D), BF16)
-        r.kvb = vm((2, T, 2 * D), BF16)
+        r.kvb = vm((self.LEN, 2 * D), BF16)
         r.lse = vm((T, 128), F32)
-        r.lset = vm((HEADS // 2, 8, T), F32)
         r.ctx = vm((T, D), BF16)
         r.y3 = vm((T, D), F32)
         r.a5 = vm((T, D), BF16)
-        r.hid = vm((T, FF), BF16)
+        r.hid = vm((T + 32, FF), BF16)
         r.dg = vm((T, FF), BF16)
         r.osend = vm((T, D), BF16)
-        r.gs = vm((T, D), F32)
+        r.gs = r.y3
         r.dkvr = vm((T, 2 * D), BF16)
-        r.acc = vm((2, self.LEN, 128), F32)
         r.tr = vm((D, T), BF16)
-        r.col = vm((T, 128), F32)
-        wides = (H, FF, FF, H)
-        r.es = [vm((8, wide), F32) for wide in wides]
-        r.er = [vm((8, wide), F32) for wide in wides]
+        edges = (((8, H), F32), ((16, FF), BF16), ((16, FF), BF16), ((8, H), F32))
+        r.es = [vm(shape, dtype) for shape, dtype in edges]
+        r.er = [vm(shape, dtype) for shape, dtype in edges]
         r.s_loc = sem(WEIGHTS)
-        r.s_as = sem(WEIGHTS, self.B)
-        r.s_ar = sem(WEIGHTS, self.B)
-        r.s_bs = sem(WEIGHTS, self.A * self.B)
-        r.s_br = sem(WEIGHTS, self.A * self.B)
-        r.s_ds = sem(WEIGHTS, n)
-        r.s_dr = sem(WEIGHTS, n)
-        r.s_rs = sem(UNITS, n)
-        r.s_rr = sem(UNITS, n)
-        r.s_ps = sem(UNITS, n)
-        r.s_pr = sem(UNITS, n)
-        r.s_zs = sem(UNITS, 2)
-        r.s_zr = sem(UNITS, 2)
+        r.s_as = sem(WEIGHTS)
+        r.s_ar = sem(WEIGHTS, self.B - 1)
+        r.s_br = sem(WEIGHTS, (self.A - 1) * self.B)
+        r.s_ds = sem(WEIGHTS)
+        r.s_dr = sem(WEIGHTS)
+        if self.shared:
+            r.s_hs = sem(WEIGHTS)
+            r.s_hr = sem(WEIGHTS)
+        r.s_rs = sem(UNITS)
+        r.s_rr = sem(UNITS)
+        r.s_ps = sem(UNITS, 2)
+        r.s_pr = sem(UNITS, 2)
+        if self.Z > 1:
+            r.s_zs = sem(UNITS, 2)
+            r.s_zr = sem(UNITS, 2)
         r.s_fs = sem(UNITS)
         r.s_fr = sem(UNITS)
         r.s_fl = sem(UNITS)
@@ -251,8 +256,8 @@
         ds = pl.ds(aligned(row0), rows)
         return ref.at[:, ds] if w == CONV else ref.at[ds]
 
-    def wblock(w, shard, half):
-        return vrows(r.w[w], w, shard * plan.kr(w) + half * plan.hr(w), plan.hr(w))
+    def bytes_of(view, semaphore):
+        return pltpu.make_async_copy(view, view, semaphore)
 
     def qof(core, f, g):
         f, g = f % B, g % B
@@ -260,51 +265,40 @@
 
     b_, a_ = q % B, q // B
     f_, g_ = c * a_ + oc * b_, c * b_ + oc * a_
-    of_, og_ = oc * a_ + c * b_, oc * b_ + c * a_
+    par = z % 2
+    partner = dev(c, q, z + 1 - 2 * par)
+
+    def wrows(ref, w, row0, rows, side):
+        if w not in plan.shared:
+            return vrows(ref, w, row0, rows)
+        size = plan.dims[w][1] // 2
+        cols = pl.ds(pl.multiple_of(side * size, 128), size)
+        return ref.at[pl.ds(aligned(row0), rows), cols]
+
+    def wblock(w, shard, side=par):
+        return wrows(r.w[w], w, shard * plan.kr(w) + c * plan.hr(w), plan.hr(w), side)
+
+    def own_block(w):
+        return wrows(r.h[w], w, c * plan.hr(w), plan.hr(w), par)
 
     def copy_a(w, t):
-        src = vrows(r.h[w], w, c * plan.hr(w), plan.hr(w))
-        return remote(
-            src,
-            wblock(w, q, c),
-            r.s_as.at[w, t],
-            r.s_ar.at[w, t],
-            dev(c, qof(c, f_ + t, g_)),
-        )
-
-    def arrived_a(w, t):
-        blk = wblock(w, qof(c, f_ + B - t, g_), c)
-        return remote(blk, blk, r.s_as.at[w, t], r.s_ar.at[w, t], sibling)
+        to = dev(c, qof(c, f_ + t, g_))
+        return remote(own_block(w), wblock(w, q), r.s_as.at[w], r.s_ar.at[w, t - 1], to)
 
     def copy_b(w, u, t):
-        shard = qof(c, f_ + B - t, g_)
-        if t == 0:
-            src = vrows(r.h[w], w, c * plan.hr(w), plan.hr(w))
-        else:
-            src = wblock(w, shard, c)
-        i = u * B + t
-        return remote(
-            src,
-            wblock(w, shard, c),
-            r.s_bs.at[w, i],
-            r.s_br.at[w, i],
-            dev(c, qof(c, f_, g_ + u)),
-        )
-
-    def arrived_b(w, u, t):
-        blk = wblock(w, qof(c, f_ + B - t, g_ + B - u), c)
-        i = u * B + t
-        return remote(blk, blk, r.s_bs.at[w, i], r.s_br.at[w, i], sibling)
-
-    def copy_d(w, u, t):
-        blk = wblock(w, qof(c, f_ + B - t, g_ + B - u), c)
-        i = u * B + t
-        return remote(blk, blk, r.s_ds.at[w, i], r.s_dr.at[w, i], sibling)
-
-    def arrived_d(w, u, t):
-        blk = wblock(w, qof(oc, of_ + B - t, og_ + B - u), oc)
-        i = u * B + t
-        return remote(blk, blk, r.s_ds.at[w, i], r.s_dr.at[w, i], sibling)
+        blk = wblock(w, qof(c, f_ + B - t, g_))
+        src = own_block(w) if t == 0 else blk
+        to = dev(c, qof(c, f_, g_ + u))
+        return remote(src, blk, r.s_as.at[w], r.s_br.at[w, (u - 1) * B + t], to)
+
+    def shard_from(u, t):
+        return qof(c, f_ + B - t, g_ + B - u)
+
+    def pass_on(w, u, t):
+        blk = wblock(w, shard_from(u, t))
+        remote(blk, blk, r.s_ds.at[w], r.s_dr.at[w], sibling).start()
+        if w in plan.shared:
+            remote(blk, blk, r.s_hs.at[w], r.s_hr.at[w], partner).start()
 
     def local_shard(w):
         dst = vrows(r.w[w], w, q * plan.kr(w), plan.kr(w))
@@ -319,33 +313,39 @@
 
     def g1(w):
         for t in range(1, B):
-            arrived_a(w, t).wait_recv()
+            bytes_of(wblock(w, shard_from(0, t)), r.s_ar.at[w, t - 1]).wait()
             for u in range(1, A):
                 copy_b(w, u, t).start()
-            copy_d(w, 0, t).start()
+            pass_on(w, 0, t)
 
     def g2(w):
         for u in range(1, A):
             for t in range(B):
-                arrived_b(w, u, t).wait_recv()
-                copy_d(w, u, t).start()
-
-    def g3(w):
-        local_shard(w).wait()
+                bytes_of(wblock(w, shard_from(u, t)), r.s_br.at[w, (u - 1) * B + t]).wait()
+                pass_on(w, u, t)
+
+    def others(w):
+        return wrows(r.w[w], w, 0, (n - 1) * plan.hr(w), 0)
+
+    def gz(w):
+        if w not in plan.shared:
+            return
+        bytes_of(others(w), r.s_hr.at[w]).wait()
         for u in range(A):
             for t in range(B):
                 if (u, t) != (0, 0):
-                    arrived_d(w, u, t).wait_recv()
+                    blk = wblock(w, shard_from(u, t), 1 - par)
+                    remote(blk, blk, r.s_ds.at[w], r.s_dr.at[w], sibling).start()
+
+    def g3(w):
+        local_shard(w).wait()
+        bytes_of(vrows(r.w[w], w, 0, (n - 1) * plan.hr(w)), r.s_dr.at[w]).wait()
 
     def gather_sent(w):
-        for t in range(1, B):
-            copy_a(w, t).wait_send()
-        for u in range(A):
-            for t in range(B):
-                if u > 0:
-                    copy_b(w, u, t).wait_send()
-                if (u, t) != (0, 0):
-                    copy_d(w, u, t).wait_send()
+        bytes_of(others(w), r.s_as.at[w]).wait()
+        bytes_of(vrows(r.w[w], w, 0, (n - 1) * plan.hr(w)), r.s_ds.at[w]).wait()
+        if w in plan.shared:
+            bytes_of(others(w), r.s_hs.at[w]).wait()
 
     def token_rows(ref, slot):
         return ref.at[pl.ds(aligned(slot * span), span)]
@@ -482,7 +482,8 @@
     def edge_take(i):
         edge_copy(i).wait()
         got = r.er[i][...]
-        return jnp.where(c == 1, got, 0.0), jnp.where(c == 0, got, 0.0)
+        none = jnp.zeros_like(got)
+        return jnp.where(c == 1, got, none), jnp.where(c == 0, got, none)
 
     def columns(u):
         half = UNIT_PART[u]
@@ -525,19 +526,12 @@
         return buf if cols is None else buf.at[:, cols]
 
     def copy_r(u, s):
-        return remote(
-            gpiece(u, s, oc), rpiece(u, s), r.s_rs.at[u, s], r.s_rr.at[u, s], sibling
-        )
-
-    def copy_p(u, t):
-        chip = lax.rem(q + t, n)
-        return remote(
-            gpiece(u, chip, c),
-            ppiece(u, t - 1),
-            r.s_ps.at[u, t],
-            r.s_pr.at[u, t],
-            dev(c, chip),
-        )
+        return remote(gpiece(u, s, oc), rpiece(u, s), r.s_rs.at[u], r.s_rr.at[u], sibling)
+
+    def all_r(u, semaphore):
+        w = UNIT_WEIGHT[u]
+        view = r.r[w] if u == SMALL else urows(r.r[w], u, 0, n * plan.hr(w))
+        return bytes_of(view, semaphore.at[u])
 
     def shards(u):
         return 1 if u == SMALL else n
@@ -550,29 +544,89 @@
         return a[...].astype(F32) + b[...].astype(F32)
 
     def add_core(u, s):
-        copy_r(u, s).wait_recv()
         mine = gpiece(u, s, c)
         mine[...] = plus(mine, rpiece(u, s)).astype(mine.dtype)
 
+    def slot1(u, t):
+        return (u - 1) * B + t
+
+    def slot2(t):
+        return (A - 1) * B + t - 1
+
+    def copy_p1(u, k, t):
+        return remote(
+            gpiece(u, qof(c, f_ + t, g_ + k), c),
+            ppiece(u, slot1(k, t)),
+            r.s_ps.at[u, 0],
+            r.s_pr.at[u, 0],
+            dev(c, qof(c, f_, g_ + k)),
+        )
+
+    def copy_p2(u, t):
+        to = qof(c, f_ + t, g_)
+        return remote(
+            r.r[WEIGHTS] if u == SMALL else gpiece(u, to, c),
+            ppiece(u, slot2(t)),
+            r.s_ps.at[u, 1],
+            r.s_pr.at[u, 1],
+            dev(c, to),
+        )
+
+    def all_p(u, step, semaphore):
+        count = B - 1 if step else A - 1 if u == SMALL else (A - 1) * B
+        cols = columns(u)
+        buf = r.p[UNIT_WEIGHT[u]]
+        view = buf.at[pl.ds(0, count)] if cols is None else buf.at[pl.ds(0, count), :, cols]
+        return bytes_of(view, semaphore.at[u, step])
+
     def red1(u):
+        all_r(u, r.s_rr).wait()
         if u == SMALL:
             add_core(u, 0)
-
-        def one(t, _):
+            for k in range(1, A):
+                copy_p1(u, k, 0).start()
+            return
+
+        def send(i, _):
+            k, t = i // B + 1, i % B
+            add_core(u, qof(c, f_ + t, g_ + k))
+            copy_p1(u, k, t).start()
+            return 0
+
+        lax.fori_loop(0, (A - 1) * B, send, 0)
+        lax.fori_loop(0, B, lambda t, _: (add_core(u, qof(c, f_ + t, g_)), 0)[1], 0)
+
+    def red1b(u):
+        all_p(u, 0, r.s_pr).wait()
+
+        def send(t, _):
+            if u == SMALL:
+                total, to = r.g8[pl.ds(pl.multiple_of(c * 8, 8), 8)], r.r[WEIGHTS]
+            else:
+                to = gpiece(u, qof(c, f_ + t, g_), c)
+                total = to[...].astype(F32)
+            for k in range(1, A):
+                total = total + ppiece(u, slot1(k, 0 if u == SMALL else t))[...].astype(F32)
+            to[...] = total.astype(to.dtype)
             if u != SMALL:
-                add_core(u, lax.rem(q + t, n))
-            copy_p(u, t).start()
+                copy_p2(u, t).start()
             return 0
 
-        lax.fori_loop(1, n, one, 0)
+        if u == SMALL:
+            send(0, 0)
+            for t in range(1, B):
+                copy_p2(u, t).start()
+        else:
+            lax.fori_loop(1, B, send, 0)
+
+    def red2(u):
+        all_p(u, 1, r.s_pr).wait()
+        total = (r.r[WEIGHTS] if u == SMALL else gpiece(u, q, c))[...].astype(F32)
         if u != SMALL:
-            add_core(u, q)
-
-    def red2(u):
-        total = gpiece(u, q, c)[...].astype(F32)
-        for t in range(1, n):
-            copy_p(u, t).wait_recv()
-            total = total + ppiece(u, t - 1)[...].astype(F32)
+            for k in range(1, A):
+                total = total + ppiece(u, slot1(k, 0))[...].astype(F32)
+        for t in range(1, B):
+            total = total + ppiece(u, slot2(t))[...].astype(F32)
         mine = ppiece(u, 0)
         mine[...] = total.astype(mine.dtype)
 
@@ -639,10 +693,9 @@
     def red_end(u):
         final_local(u).wait()
         final_remote(u).wait()
-        for s in range(shards(u)):
-            copy_r(u, s).wait_send()
-        for t in range(1, n):
-            copy_p(u, t).wait_send()
+        all_r(u, r.s_rs).wait()
+        all_p(u, 0, r.s_ps).wait()
+        all_p(u, 1, r.s_ps).wait()
         if Z > 1:
 
             @pl.when(z < Z - 1)
@@ -662,7 +715,7 @@
     def reduce_start(*units):
         for u in units:
             red0(u)
-            ahead[u] = [red1, red2]
+            ahead[u] = [red1, red1b, red2]
             if Z > 1:
                 ahead[u] += [lambda k, h=h: red_hop(k, h) for h in range(Z - 1)]
             ahead[u].append(last_hop if Z > 1 else red_final)
@@ -685,17 +738,17 @@
     NB = T // RB
 
     def rows_of(i, size=RB, base=0):
-        return pl.ds(pl.multiple_of(i * size + base, 8 if base else size), size)
-
+        return pl.ds(pl.multiple_of(i * size + base, base or size), size)
+
+    g0(GLU)
+    seg_send()
     small_local = pltpu.make_async_copy(r.small, r.smallbuf.at[q], r.s_mr.at[0])
     small_local.start()
     for t in range(1, n):
         small_copy(t).start()
-    seg_send()
     tokens_in(r.x, r.xin, 0)
-    g0(GLU)
-    g0(CONV)
     r.g8[...] = jnp.zeros((16, FF), F32)
+    g1(GLU)
 
     for s in range(n):
         blk = r.segbuf.at[s]
@@ -705,21 +758,17 @@
         for k in range(1, plan.sr):
             got = got + r.segbuf[grp * plan.sr + k]
         r.segrow[:, grp * plan.sw : (grp + 1) * plan.sw] = got
-    r.segq[...] = r.segrow[:, pl.ds(pl.multiple_of(c * T, 128), T)]
     r.segcol[0:8] = jnp.full((8, 128), -1.0, F32)
     r.segcol[plan.LEN + 8 : plan.LEN + 16] = jnp.full((8, 128), -1.0, F32)
     for k in range(plan.LEN // 128):
         row = r.segrow[0:1, k * 128 : (k + 1) * 128]
         r.segcol[8 + k * 128 : 8 + (k + 1) * 128] = jnp.broadcast_to(row, (128, 128)).T
     r.segloc[...] = r.segcol[pl.ds(pl.multiple_of(c * T, 8), T + 16)]
-    for o in range(1, 5):
-        same = r.segloc[0 : T + 8] == r.segloc[o : T + 8 + o]
-        r.mext[o - 1, 0 : T + 8] = jnp.where(same, 1.0, 0.0)
+    r.mext[0 : T + 8] = jnp.where(r.segloc[0 : T + 8] == r.segloc[1 : T + 9], 1.0, 0.0)
 
     def mask(o, start, rows):
-        if o > 0:
-            return r.mext[o - 1, 8 + start : 8 + start + rows]
-        return r.mext[-o - 1, 8 + start + o : 8 + start + o + rows]
+        first = 8 + start + (0 if o > 0 else o)
+        return r.mext[first : first + rows]
 
     small_local.wait()
     for t in range(1, n):
@@ -746,12 +795,38 @@
         r.g8[12:13, cols] += jnp.sum(e, axis=0, keepdims=True)
         return rs * (eg - m1 - unit * m2)
 
-    g1(GLU)
     g0(LEFT)
     g2(GLU)
-    g1(CONV)
+    g0(CONV)
+
+    def window(b):
+        return min(max(b * MB - (MW - MB) // 2 + 16, 0), T + 32 - MW)
+
+    ahead_of = lax.broadcasted_iota(jnp.int32, (MB, MW), 1) - lax.broadcasted_iota(
+        jnp.int32, (MB, MW), 0
+    )
+    for b in range(T // MB):
+        home = r.segloc[8 + b * MB : 8 + (b + 1) * MB]
+        for o in range(-4, 5):
+            there = r.segloc[8 + b * MB + o : 8 + (b + 1) * MB + o]
+            same = jnp.where(home == there, 1.0, 0.0)
+            hit = ahead_of == b * MB + 16 - window(b) + o
+            tap = jnp.where(hit, jnp.concatenate([same] * (MW // 128), axis=1), 0.0)
+            r.ms[b, (o + 4) * MB : (o + 5) * MB] = tap.astype(BF16)
+
+    lane = lax.broadcasted_iota(jnp.int32, (1, 128), 1)
+    lane_f = lane.astype(F32)
+    own_doc = r.segloc[8 : T + 8] == lane_f
+    r.qenc[...] = jnp.where(jnp.logical_and(lane < 4, jnp.logical_not(own_doc)), FAR, 0.0).astype(BF16)
+    ones = jnp.logical_and(lane >= 4, lane < 7)
+    r.kenc[...] = jnp.where(
+        jnp.logical_or(r.segcol[8 : plan.LEN + 8] == lane_f, ones), 1.0, 0.0
+    ).astype(BF16)
+
     tokens_in_done(r.xin, 0)
     g3(GLU)
+    g1(LEFT)
+    g0(POINT)
 
     def glu(i):
         rows = rows_of(i)
@@ -766,10 +841,9 @@
         r.y1[rows] = y1
         r.a2[rows] = ln_out(1, y1)
 
-    loop(NB, glu)
+    loop(NB, glu, [(0, lambda: g1(CONV))])
+    g2(LEFT)
     g2(CONV)
-    g1(LEFT)
-    g0(POINT)
     g3(CONV)
 
     def conv(i):
@@ -779,7 +853,6 @@
 
     loop(NB, conv)
     edge_send(0, r.pext[0, T : T + 8], r.pext[2, 8:16])
-    g2(LEFT)
     g1(POINT)
     g0(QKV)
     top, bottom = edge_take(0)
@@ -797,6 +870,7 @@
         value, slope = gelu_both(pre)
         r.pext[1, lo + 8 : lo + 136] = value
         r.dgr[lo : lo + 128] = slope.astype(BF16)
+    gz(LEFT)
     g3(LEFT)
 
     CH = 512
@@ -813,36 +887,39 @@
         unit, rs = normed(r.big[erows])
         r.nm[rows] = unit.astype(BF16)
         r.rm[rows] = rs
-        r.big[erows] = (unit * r.midp[0:1] + r.midp[1:2]).astype(BF16).astype(F32)
-
-    loop(T // RM, left)
-    edge_send(1, r.big[T : T + 8], r.big[8:16])
-    g2(POINT)
-    g1(QKV)
-    g0(OUT)
-    top, bottom = edge_take(1)
-    r.big[0:8] = top
-    r.big[T + 8 : T + 16] = bottom
-
-    RC = 64
+        r.hid[rows_of(i, RM, 16)] = (unit * r.midp[0:1] + r.midp[1:2]).astype(BF16)
+
+    def ahead_point():
+        g2(POINT)
+        g1(QKV)
+        g0(OUT)
+
+    loop(T // RM, left, [(1, ahead_point)])
+    edge_send(1, r.hid[T : T + 16], r.hid[16:32])
+    gz(POINT)
+    r.hid[0:16], r.hid[T + 16 : T + 32] = edge_take(1)
 
     def depthwise(j):
-        cols = pl.ds(pl.multiple_of(j * 128, 128), 128)
-        for k in range(T // RC):
-            lo = k * RC
-            total = r.big[lo + 8 : lo + 8 + RC, cols] * r.midp[6:7, cols]
-            for o in (-4, -3, -2, -1, 1, 2, 3, 4):
-                cells = r.big[lo + 8 + o : lo + 8 + o + RC, cols]
-                total = total + cells * mask(o, lo, RC) * r.midp[6 + o : 7 + o, cols]
-            r.sep[lo : lo + RC, cols] = total.astype(BF16)
+        cols = pl.ds(pl.multiple_of(j * 256, 256), 256)
+        for b in range(T // MB):
+            near = r.hid[window(b) : window(b) + MW, cols]
+            taps = mm(r.ms[b], near)
+            total = taps[0:MB] * r.midp[2:3, cols]
+            for o in range(1, 9):
+                total = total + taps[o * MB : (o + 1) * MB] * r.midp[2 + o : 3 + o, cols]
+            r.sep[b * MB : (b + 1) * MB, cols] = total.astype(BF16)
 
     def ahead_qkv():
         g2(QKV)
         g1(OUT)
         g0(FIN)
 
-    loop(FF // 128, depthwise, [(7, ahead_qkv)])
-    g2(OUT)
+    def ahead_out():
+        g2(OUT)
+        g1(FIN)
+        g0(FOUT)
+
+    loop(FF // 256, depthwise, [(1, ahead_qkv), (5, ahead_out)])
     g3(POINT)
 
     def point(i):
@@ -859,69 +936,52 @@
         rows = rows_of(i)
         a4 = r.a4[rows]
         r.qb[rows] = (mm(a4, r.w[QKV][:, 0:D]) * scale).astype(BF16)
-        r.kvb[c, rows, 0:D] = mm(a4, r.w[QKV][:, D : 2 * D]).astype(BF16)
-        r.kvb[c, rows, D : 2 * D] = mm(a4, r.w[QKV][:, 2 * D : 3 * D]).astype(BF16)
+        here = pl.ds(pl.multiple_of(c * T + i * RB, RB), RB)
+        r.kvb[here, 0:D] = mm(a4, r.w[QKV][:, D : 2 * D]).astype(BF16)
+        r.kvb[here, D : 2 * D] = mm(a4, r.w[QKV][:, 2 * D : 3 * D]).astype(BF16)
 
     loop(NB, qkv)
 
     def kv_copy():
-        blk = r.kvb.at[c]
+        blk = r.kvb.at[pl.ds(aligned(c * T), T)]
         return remote(blk, blk, r.s_ks.at[0], r.s_kr.at[0], sibling)
 
     kv_copy().start()
     tokens_in(r.ct, r.cot, 1)
-    lane = lax.broadcasted_iota(jnp.int32, (1, 128), 1)
     heads_lanes = [lane < 64, lane >= 64]
-    g1(FIN)
-    g0(FOUT)
+    g2(FIN)
     kv_copy().wait()
 
     def pair_cols(j, base=0):
         return pl.ds(pl.multiple_of(j * 128 + base, 128), 128)
 
-    def one_head(q2, part, mine, key_row):
-        def scores(keys, segs):
-            raw = mm_t(q2, keys)
-            same = jnp.concatenate([mine] * (T // 128), axis=1) == segs
-            return jnp.where(same, raw, NEG)
-
-        s0 = scores(part[0], key_row[:, 0:T])
-        s1 = scores(part[1], key_row[:, T : 2 * T])
-        most = jnp.maximum(
-            jnp.max(s0, axis=-1, keepdims=True), jnp.max(s1, axis=-1, keepdims=True)
-        )
-        e0, e1 = jnp.exp(s0 - most), jnp.exp(s1 - most)
-        total = jnp.sum(e0, axis=-1, keepdims=True) + jnp.sum(e1, axis=-1, keepdims=True)
-        got = mm(e0.astype(BF16), part[2]) + mm(e1.astype(BF16), part[3])
-        return got / total, most + jnp.log(total)
+    def head_lanes(e, v):
+        return jnp.where(heads_lanes[e], v, jnp.zeros_like(v))
 
     def attend(j):
         cols, vcols = pair_cols(j), pair_cols(j, D)
-        part = [r.kvb[0, :, cols], r.kvb[1, :, cols], r.kvb[0, :, vcols], r.kvb[1, :, vcols]]
-        key_row = r.segrow[0:1]
+        keys = jnp.concatenate([r.kvb[:, cols], r.kenc[...]], axis=1)
         for k in range(T // RB):
             rows = slice(k * RB, (k + 1) * RB)
             q2 = r.qb[rows, cols]
-            mine = r.segloc[8 + k * RB : 8 + (k + 1) * RB]
             got = []
             for e in range(2):
-                context, lse = one_head(
-                    jnp.where(heads_lanes[e], q2, jnp.zeros_like(q2)), part, mine, key_row
-                )
-                got.append(context)
+                score = mm_t(jnp.concatenate([head_lanes(e, q2), r.qenc[rows]], axis=1), keys)
+                most = jnp.max(score, axis=-1, keepdims=True)
+                power = jnp.exp(score - most)
+                total = jnp.sum(power, axis=-1, keepdims=True)
+                got.append(mm(power.astype(BF16), r.kvb[:, vcols]) / total)
+                lse = most + jnp.log(total)
                 r.lse[rows] = jnp.where(lane == 2 * j + e, lse, r.lse[rows])
             r.ctx[rows, cols] = jnp.where(heads_lanes[0], got[0], got[1]).astype(BF16)
 
     r.lse[...] = jnp.zeros((T, 128), F32)
-    def ahead_fin():
-        g2(FIN)
-        g1(FOUT)
-
-    loop(HEADS // 2, attend, [(1, ahead_fin)])
-    turned = r.lse[...].T
-    for j in range(HEADS // 2):
-        r.lset[j, 0:2] = turned[2 * j : 2 * j + 2]
-    g2(FOUT)
+
+    loop(
+        HEADS // 2,
+        attend,
+        [(0, lambda: g1(FOUT)), (1, lambda: gz(FIN)), (2, lambda: g2(FOUT))],
+    )
     g3(OUT)
 
     def out(i):
@@ -941,7 +1001,7 @@
             r.hid[rows, k * CH : (k + 1) * CH] = value.astype(BF16)
             r.dg[rows, k * CH : (k + 1) * CH] = slope.astype(BF16)
 
-    loop(NB, ffn_in)
+    loop(NB, ffn_in, [(0, lambda: gz(FOUT))])
     g3(FOUT)
 
     def ffn_out(i):
@@ -970,7 +1030,7 @@
 
     def grad_outer(k):
         cols = rows_of(k, GC)
-        r.w[FOUT][cols] = mm_tn(r.hid[:, cols], r.cot[...]).astype(BF16)
+        r.w[FOUT][cols] = mm_tn(r.hid[0:T, cols], r.cot[...]).astype(BF16)
 
     loop(FF // GC, grad_outer)
     reduce_start(U_FOUT)
@@ -996,57 +1056,66 @@
 
     QB = 256
 
+    def with_terms(extra, v):
+        high = v.astype(BF16).astype(F32)
+        mid = (v - high).astype(BF16).astype(F32)
+        low = v - high - mid
+        terms = jnp.where(lane == 4, high, jnp.where(lane == 5, mid, jnp.where(lane == 6, low, 0.0)))
+        return extra - terms.astype(BF16)
+
     def attend_back(j):
         cols, vcols = pair_cols(j), pair_cols(j, D)
+        k2 = r.kvb[:, cols]
+        keys = jnp.concatenate([k2, r.kenc[...]], axis=1)
+        values = jnp.concatenate([r.kvb[:, vcols], r.kenc[...]], axis=1)
         for k in range(T // QB):
             rows = slice(k * QB, (k + 1) * QB)
             q2 = r.qb[rows, cols]
             d2 = r.hid[rows, pair_cols(j, 3 * D)]
+            inner = d2.astype(F32) * r.ctx[rows, cols].astype(F32)
             dq = jnp.zeros((QB, 128), F32)
             for e in range(2):
-                qe = jnp.where(heads_lanes[e], q2, jnp.zeros_like(q2))
-                de = jnp.where(heads_lanes[e], d2, jnp.zeros_like(d2))
-                lse = r.lset[j, e : e + 1, rows]
-                probs, dprobs = [], []
+                qe, de = head_lanes(e, q2), head_lanes(e, d2)
+                lse = jnp.sum(
+                    jnp.where(lane == 2 * j + e, r.lse[rows], 0.0), axis=-1, keepdims=True
+                )
+                delta = jnp.sum(head_lanes(e, inner), axis=-1, keepdims=True)
+                shifted = mm_t(keys, jnp.concatenate([qe, with_terms(r.qenc[rows], lse)], axis=1))
+                probs = jnp.exp(shifted)
+                none = jnp.zeros((QB, 128), BF16)
+                moved = mm_t(values, jnp.concatenate([de, with_terms(none, delta)], axis=1))
+                ds = (probs * moved).astype(BF16)
+                dk = mm(ds, qe)
+                dv = mm(probs.astype(BF16), de)
                 for kk in range(2):
-                    keys = r.kvb[kk, :, cols]
-                    values = r.kvb[kk, :, vcols]
-                    segs = r.segcol[8 + kk * T : 8 + (kk + 1) * T]
-                    same = jnp.concatenate([segs] * (QB // 128), axis=1) == r.segq[0:1, rows]
-                    probs.append(jnp.where(same, jnp.exp(mm_t(keys, qe) - lse), 0.0))
-                    dprobs.append(mm_t(values, de))
-                delta = jnp.sum(probs[0] * dprobs[0], axis=0, keepdims=True) + jnp.sum(
-                    probs[1] * dprobs[1], axis=0, keepdims=True
-                )
-                for kk in range(2):
-                    keys = r.kvb[kk, :, cols]
-                    ds = (probs[kk] * (dprobs[kk] - delta)).astype(BF16)
-                    span_k = slice(kk * T, (kk + 1) * T)
-                    dk = mm(ds, qe)
-                    dv = mm(probs[kk].astype(BF16), de)
+                    half = slice(kk * T, (kk + 1) * T)
+                    at = 2 * D + kk * 128
                     if k == 0 and e == 0:
-                        r.acc[0, span_k] = dk
-                        r.acc[1, span_k] = dv
+                        r.big[0:T, at : at + 128] = dk[half]
+                        r.big[0:T, at + 256 : at + 384] = dv[half]
                     else:
-                        r.acc[0, span_k] += dk
-                        r.acc[1, span_k] += dv
-                    ke = jnp.where(heads_lanes[e], keys, jnp.zeros_like(keys))
-                    dq = dq + mm_tn(ds, ke)
+                        r.big[0:T, at : at + 128] += dk[half]
+                        r.big[0:T, at + 256 : at + 384] += dv[half]
+                dq = dq + mm_tn(ds, head_lanes(e, k2))
             r.hid[rows, cols] = (dq * scale).astype(BF16)
-        own = pl.ds(pl.multiple_of(c * T, T), T)
-        other = pl.ds(pl.multiple_of(oc * T, T), T)
-        r.big[0:T, cols] = r.acc[0, own]
-        r.big[0:T, vcols] = r.acc[1, own]
-        r.dg[:, cols] = r.acc[0, other].astype(BF16)
-        r.dg[:, vcols] = r.acc[1, other].astype(BF16)
+
+        def part(core, what):
+            at = pl.multiple_of(2 * D + core * 128 + what * 256, 128)
+            return r.big[0:T, pl.ds(at, 128)]
+
+        r.big[0:T, cols] = part(c, 0)
+        r.big[0:T, vcols] = part(c, 1)
+        r.dg[:, cols] = part(oc, 0).astype(BF16)
+        r.dg[:, vcols] = part(oc, 1).astype(BF16)
 
     loop(
         HEADS // 2,
         attend_back,
         [
-            (1, lambda: move(U_FIN)),
-            (2, lambda: move(U_FOUT, U_FOUT)),
-            (3, lambda: move(U_OUT)),
+            (0, lambda: move(U_FIN)),
+            (1, lambda: move(U_FOUT)),
+            (2, lambda: move(U_OUT)),
+            (3, lambda: move(U_FOUT, U_FOUT, U_FIN)),
         ],
     )
 
@@ -1057,6 +1126,7 @@
 
     dkv_copy().start()
     dkv_copy().wait()
+    move(U_OUT)
 
     def qkv_back(i):
         rows = rows_of(i)
@@ -1070,7 +1140,7 @@
 
     def grad_qkv(k):
         cols = rows_of(k, GC)
-        r.w[QKV][:, cols] = mm(r.tr[...], r.hid[:, cols]).astype(BF16)
+        r.w[QKV][:, cols] = mm(r.tr[...], r.hid[0:T, cols]).astype(BF16)
 
     loop(3 * D // GC, grad_qkv)
     reduce_start(U_QKV)
@@ -1082,11 +1152,11 @@
         for k in range(FF // CH):
             cols = slice(k * CH, (k + 1) * CH)
             d = mm_t(f2, r.w[POINT][cols])
-            r.big[rows_of(i, RB, 8), cols] = d.astype(BF16).astype(F32)
+            r.hid[rows_of(i, RB, 16), cols] = d.astype(BF16)
 
     loop(NB, point_back)
-    edge_send(2, r.big[T : T + 8], r.big[8:16])
-    move(U_FIN, U_FOUT, U_FIN, U_QKV)
+    edge_send(2, r.hid[T : T + 16], r.hid[16:32])
+    move(U_FIN, U_FIN, U_QKV)
 
     def grad_point(k):
         cols = rows_of(k, GC)
@@ -1094,42 +1164,40 @@
 
     loop(FF // GC, grad_point)
     reduce_start(U_POINT0, U_POINT1)
-    move(U_OUT, U_OUT)
-    top, bottom = edge_take(2)
-    r.big[0:8] = top
-    r.big[T + 8 : T + 16] = bottom
+    move(U_FOUT, U_OUT, U_OUT)
+    r.hid[0:16], r.hid[T + 16 : T + 32] = edge_take(2)
 
     def depth_back(j):
-        cols = pl.ds(pl.multiple_of(j * 128, 128), 128)
+        cols = pl.ds(pl.multiple_of(j * 256, 256), 256)
         gain, shift = r.midp[0:1, cols], r.midp[1:2, cols]
-        sums = [jnp.zeros((8, 128), F32) for _ in range(9)]
-        for k in range(T // RC):
-            lo = k * RC
-            a3 = r.nm[lo : lo + RC, cols].astype(F32) * gain + shift
-            total = jnp.zeros((RC, 128), F32)
-            for o in range(-4, 5):
-                moved = r.big[lo + 8 - o : lo + 8 - o + RC, cols]
-                if o:
-                    moved = moved * mask(-o, lo, RC)
-                total = total + moved * r.midp[6 + o : 7 + o, cols]
+        sums = [jnp.zeros((8, 256), F32) for _ in range(9)]
+        for b in range(T // MB):
+            lo = b * MB
+            taps = mm(r.ms[b], r.hid[window(b) : window(b) + MW, cols])
+            a3 = r.nm[lo : lo + MB, cols].astype(F32) * gain + shift
+            total = jnp.zeros((MB, 256), F32)
+            for o in range(9):
+                moved = taps[(8 - o) * MB : (9 - o) * MB]
+                total = total + moved * r.midp[2 + o : 3 + o, cols]
                 part = moved * a3
-                for b in range(RC // 8):
-                    sums[o + 4] = sums[o + 4] + part[b * 8 : (b + 1) * 8]
-            r.col[lo : lo + RC] = total
+                for g in range(MB // 8):
+                    sums[o] = sums[o] + part[g * 8 : (g + 1) * 8]
+            r.big[lo + 8 : lo + 8 + MB, cols] = total
         for o in range(9):
             r.g8[2 + o : 3 + o, cols] = jnp.sum(sums[o], axis=0, keepdims=True)
-        r.big[8 : T + 8, cols] = r.col[...]
 
     loop(
-        FF // 128,
+        FF // 256,
         depth_back,
         [
-            (3, lambda: move(U_POINT0, U_POINT1)),
-            (7, lambda: move(U_FOUT, U_FIN, U_OUT, U_QKV, U_QKV)),
-            (13, lambda: move(U_FOUT, U_FIN, U_OUT, U_QKV)),
+            (1, lambda: move(U_POINT0)),
+            (2, lambda: move(U_POINT1)),
+            (3, lambda: move(U_OUT)),
+            (4, lambda: move(U_QKV, U_FOUT)),
+            (6, lambda: move(U_FIN)),
+            (7, lambda: move(U_POINT0, U_OUT)),
         ],
     )
-    move(U_POINT0, U_POINT0)
 
     def mid_back(i):
         rows, erows = rows_of(i, RM), rows_of(i, RM, 8)
@@ -1147,7 +1215,7 @@
 
     loop(T // RM, mid_back)
     edge_send(3, r.pext[0, T : T + 8], r.pext[0, 8:16])
-    move(U_POINT1, U_POINT1, U_QKV)
+    move(U_QKV, U_QKV, U_POINT1)
     r.tr[...] = r.a2[...].T
 
     def grad_left(k):
@@ -1159,7 +1227,8 @@
             half * (FF // GC // 2), (half + 1) * (FF // GC // 2), lambda k, _: (grad_left(k), 0)[1], 0
         )
         reduce_start((U_LEFT0, U_LEFT1)[half])
-    move(U_POINT0, U_FIN, U_OUT)
+        move((U_FIN, U_FOUT)[half])
+    move(U_LEFT0, U_POINT0, U_POINT0, U_OUT)
     top, bottom = edge_take(3)
     r.pext[0, 0:8] = top
     r.pext[0, T + 8 : T + 16] = bottom
@@ -1178,12 +1247,10 @@
             e = e + mm_t(r.hid[rows, o * H : (o + 1) * H], r.w[CONV][o])
         r.gs[rows] += ln_back(1, e, r.y1[rows])
 
-    loop(NB, branch_back, [(0, lambda: move(U_LEFT0))])
-    move(U_LEFT1, U_QKV, U_POINT1)
+    loop(NB, branch_back, [(0, lambda: move(U_LEFT1)), (1, lambda: move(U_LEFT0, U_POINT1, U_POINT1))])
     for o in range(3):
-        r.w[CONV][o] = mm(r.tr[...], r.hid[:, o * H : (o + 1) * H]).astype(BF16)
+        r.w[CONV][o] = mm(r.tr[...], r.hid[0:T, o * H : (o + 1) * H]).astype(BF16)
     reduce_start(U_CONV)
-    move(U_POINT0)
 
     def gate_back(i):
         rows = rows_of(i)
@@ -1197,11 +1264,12 @@
     def grad_glu(k):
         cols = rows_of(k, GC)
         to = pl.ds(pl.multiple_of(k * GC + 2 * D, GC), GC)
-        r.hid[:, to] = mm(r.tr[...], r.sg[:, cols]).astype(BF16)
+        r.hid[0:T, to] = mm(r.tr[...], r.sg[:, cols]).astype(BF16)
 
     loop(2 * D // GC, grad_glu)
     move(U_CONV)
     reduce_start(U_GLU0, U_GLU1)
+    move(U_QKV)
 
     def glu_back(i):
         rows = rows_of(i)
@@ -1211,11 +1279,12 @@
 
     loop(NB, glu_back)
     reduce_start(SMALL)
-    move(U_POINT1, U_LEFT0, U_LEFT0, U_GLU0, U_GLU1, SMALL)
+    move(U_GLU0, U_GLU1, SMALL, U_LEFT0, U_LEFT0, U_LEFT1, U_POINT0, U_POINT1, U_CONV)
+    move(U_LEFT1, U_LEFT1, U_GLU0, U_GLU1, SMALL, U_QKV, U_LEFT0, U_POINT0, U_CONV, U_CONV)
+    move(U_POINT1, U_GLU0, U_GLU0, U_LEFT1, U_GLU1, U_GLU1, SMALL, SMALL, U_LEFT0, U_CONV)
     tokens_out(r.a5, r.o_ig, 3)
-    move(U_POINT0, U_LEFT1, U_LEFT1, U_LEFT0, U_POINT1, U_CONV, U_CONV, U_LEFT1, U_LEFT0)
-    move(U_CONV, U_GLU0, U_GLU0, U_LEFT1, U_GLU1, U_GLU1, SMALL, SMALL, U_LEFT0, U_CONV)
-    move(U_GLU0, U_LEFT1, U_GLU1, SMALL, U_CONV, U_GLU0, U_GLU1, SMALL, U_GLU0, U_GLU1, SMALL)
+    move(U_GLU0, U_LEFT1, U_GLU1, SMALL, U_CONV, U_GLU0, U_GLU1, SMALL)
+    move(U_FIN, U_QKV, U_POINT0, U_POINT1, U_LEFT0, U_LEFT1, U_CONV, U_GLU0, U_GLU1, SMALL)
     while any(ahead.values()):
         move(*range(UNITS))
 

time: 198 us -> 186 us (0.939)
  Pallas kernels: 194 us -> 182 us
    pallas_call x1, Pallas kernels: 188 us -> 176 us  [local(): pl.pallas_call(lambda *refs: kernel(plan, *refs), out_shape=out_shape, in...]
where the time goes in v3:
time: 186 us
  Pallas kernels  182 us (98%)
    pallas_call x1, Pallas kernels, local(): pl.pallas_call(lambda *refs: kernel(plan, *refs), out_shape=out_shape, in...  176 us
    pallas_call x1, Pallas kernels, unpacked(): pl.pallas_call(body, out_shape=out_shape, in_specs=[hbm] * count + [vmem]...  6.13 us

profile of v3, /device:TPU:0, one launch (start us, length us, event | category | flops | bytes accessed | tf_op | source)
XLA Modules:
  0.0 186.0 jit_solution(2644694602464177863)
XLA Ops:
  0.6 0.0 copy-start.1
  0.7 0.7 convert_element_type.7
  1.3 0.0 copy-done.1
  1.3 0.0 copy-start.2
  1.4 0.0 copy-start.3
  1.4 0.0 copy-start.4
  1.4 0.7 copy-done.2
  2.0 0.0 copy-start
  2.0 0.0 copy-done.3
  2.0 0.0 copy-done.4
  2.1 0.6 broadcast_in_dim.12.refs_1_
  2.7 0.1 copy-done
  2.7 0.6 fusion.6.refs_3_
  3.4 176.3 %cell.1 = (bf16[2,256,512]{2,1,0:T(8,128)(2,1)}, bf16[2,256,512]{2,1,0:T(8,128)(2,1)}, bf16[128,1024]{1,0:T(8,128)(2,1)}, bf16[3,128,256]{2,1,0:T(8,128)(2,1)}, ...) custom-call(bf16[2,256,512]{2,1,0:T(8,128)(2,1)} %refs_0_.1, ...), custom_call_target="tpu_custom_call" | custom-call | tf_op jit(solution)/shard_map/cell/pallas_call | solution.py:1352
  179.7 6.1 %shard_map.271 = (f32[2,256,512]{2,1,0:T(8,128)}, f32[2,256,512]{2,1,0:T(8,128)}, f32[128,1024]{1,0:T(8,128)}, f32[3,128,256]{2,1,0:T(8,128)}, f32[128,2048]{1,0...) custom-call(bf16[2,256,512]{2,1,0:T(8,128)(2,1)} %get-tuple-element., ...), custom_call_target="tpu_custom_call" | custom-call | tf_op jit(solution)/shard_map/pallas_call | solution.py:1423
  (3 shorter events, 0.0 us)
Async XLA Ops:
  0.6 0.7 copy-start.1
  1.3 0.7 copy-start.2
  1.4 0.7 copy-start.3
  1.4 0.7 copy-start.4
  2.0 0.7 copy-start

commit v4 on v3

--- a/solution.py
+++ b/solution.py
@@ -15,13 +15,51 @@
 
 GLU, CONV, LEFT, POINT, QKV, OUT, FIN, FOUT = range(8)
 WEIGHTS = 8
-(U_GLU0, U_GLU1, U_CONV, U_LEFT0, U_LEFT1, U_POINT0, U_POINT1, U_QKV, U_OUT, U_FIN, U_FOUT, SMALL) = range(12)
-UNITS = 12
+(U_GLU0, U_GLU1, U_CONV, U_LEFT0, U_LEFT1, U_POINT0, U_POINT1, U_QKV0, U_QKV1, U_OUT, U_FIN, U_FOUT, SMALL) = range(13)
+UNITS = 13
+UNIT_WEIGHT = (GLU, GLU, CONV, LEFT, LEFT, POINT, POINT, QKV, QKV, OUT, FIN, FOUT, WEIGHTS)
+UNIT_PART = (0, 1, None, 0, 1, 0, 1, 0, 1, None, None, None, None)
+
+SCHEDULE = (
+    (),
+    (),
+    (U_FOUT,),
+    (U_FIN, U_OUT,),
+    (U_FOUT,),
+    (),
+    (U_FOUT, U_FIN, U_OUT,),
+    (U_QKV0,),
+    (U_QKV1, U_FIN,),
+    (U_OUT, U_FOUT, U_QKV0,),
+    (),
+    (U_QKV1, U_POINT0,),
+    (U_QKV0, U_POINT1,),
+    (U_FIN,),
+    (U_QKV1, U_OUT,),
+    (),
+    (U_FOUT, U_QKV0, U_POINT0,),
+    (),
+    (),
+    (U_QKV1, U_POINT1,),
+    (),
+    (U_POINT0,),
+    (U_FIN,),
+    (U_OUT, U_POINT1,),
+    (U_QKV0, U_LEFT0,),
+    (U_POINT0, U_LEFT1,),
+    (U_QKV1, U_CONV,),
+    (U_POINT1,),
+    (),
+    (U_LEFT0,),
+    (U_POINT0, U_GLU0, U_GLU1,),
+)
+TAIL = (
+    (SMALL, U_LEFT1, U_POINT1, U_CONV, U_LEFT0, U_GLU0, U_GLU1, SMALL),
+    (U_LEFT1, U_LEFT0, U_CONV, U_GLU0, U_GLU1, SMALL, U_LEFT1, U_LEFT0, U_CONV, U_GLU0, U_GLU1, U_LEFT1, SMALL, U_CONV, U_GLU0, U_GLU1, SMALL, U_FOUT, U_FIN, U_OUT, U_QKV0, U_QKV1, U_POINT0, U_POINT1, U_LEFT0, U_LEFT1, U_CONV, U_GLU0, U_GLU1, SMALL),
+)
 
 MB, MW = 128, 256
 FAR = -(2.0**30)
-UNIT_WEIGHT = (GLU, GLU, CONV, LEFT, LEFT, POINT, POINT, QKV, OUT, FIN, FOUT, WEIGHTS)
-UNIT_PART = (0, 1, None, 0, 1, 0, 1, None, None, None, None, None)
 
 
 def mm(a, b):
@@ -99,9 +137,11 @@
     def hr(self, w):
         return self.kr(w) // 2
 
+    def gcols(self, w):
+        return self.dims[w][1] * (3 if w == CONV else 1)
+
     def piece(self, w, rows):
-        cols = self.dims[w][1]
-        return (3, rows, cols) if w == CONV else (rows, cols)
+        return (rows, self.gcols(w))
 
     def buffers(self, take):
         T, D, FF, H, n = self.T, self.D, self.FF, self.HALF, self.n
@@ -114,10 +154,11 @@
             return take(pltpu.SemaphoreType.DMA(shape))
 
         every = range(WEIGHTS)
-        parts = [(self.piece(w, self.hr(w)), BF16) for w in every] + [((8, FF), F32)]
+        parts = [(self.piece(w, self.hr(w)), BF16) for w in every] + [((16, FF // 2), BF16)]
         r.w = [vm(self.whole(w), BF16) for w in every]
         r.g8 = vm((16, FF), F32)
-        r.r = [None] * WEIGHTS + [vm((8, FF), F32)]
+        r.gsm = vm((32, FF // 2), BF16)
+        r.r = [None] * WEIGHTS + [vm((16, FF // 2), BF16)]
         for w in (CONV, QKV, OUT, FIN, FOUT):
             r.r[w] = vm(self.piece(w, n * self.hr(w)), BF16)
         r.r[LEFT], r.r[POINT], r.r[GLU] = r.r[FIN], r.r[FOUT], r.r[QKV]
@@ -193,8 +234,10 @@
         r.s_mr = sem(n)
         r.s_es = sem(4)
         r.s_er = sem(4)
-        r.s_ks = sem(2)
-        r.s_kr = sem(2)
+        r.s_ks = sem(1)
+        r.s_kr = sem(1)
+        r.s_js = sem(HEADS // 2)
+        r.s_jr = sem(HEADS // 2)
         return r
 
 
@@ -486,28 +529,22 @@
         return jnp.where(c == 1, got, none), jnp.where(c == 0, got, none)
 
     def columns(u):
-        half = UNIT_PART[u]
-        if half is None:
-            return None
-        size = plan.dims[UNIT_WEIGHT[u]][1] // 2
-        return pl.ds(half * size, size)
-
-    def urows(ref, u, row0, rows):
-        cols = columns(u)
-        if cols is None:
-            return vrows(ref, UNIT_WEIGHT[u], row0, rows)
-        return ref.at[pl.ds(aligned(row0), rows), cols]
+        w, half = UNIT_WEIGHT[u], UNIT_PART[u]
+        size = plan.gcols(w)
+        return (0, size) if half is None else (half * (size // 2), size // 2)
+
+    def urows(ref, u, row0, rows, shift=0):
+        col0, size = columns(u)
+        return ref.at[pl.ds(aligned(row0), rows), pl.ds(col0 + shift, size)]
+
+    grad_home = {GLU: (r.hid, 2 * D), CONV: (r.dkvr, 0), LEFT: (r.sep, 0), QKV: (r.dg, 0)}
 
     def gpiece(u, shard, half):
         if u == SMALL:
-            return r.g8.at[pl.ds(pl.multiple_of(half * 8, 8), 8)]
+            return r.gsm.at[pl.ds(pl.multiple_of(half * 16, 16), 16)]
         w = UNIT_WEIGHT[u]
-        row0 = shard * plan.kr(w) + half * plan.hr(w)
-        if w == GLU:
-            size = plan.D
-            cols = pl.ds(2 * D + UNIT_PART[u] * size, size)
-            return r.hid.at[pl.ds(aligned(row0), plan.hr(w)), cols]
-        return urows(r.dg if w == LEFT else r.w[w], u, row0, plan.hr(w))
+        ref, shift = grad_home.get(w, (r.w[w] if w < WEIGHTS else None, 0))
+        return urows(ref, u, shard * plan.kr(w) + half * plan.hr(w), plan.hr(w), shift)
 
     def rpiece(u, shard):
         w = UNIT_WEIGHT[u]
@@ -515,15 +552,26 @@
             return r.r[w]
         return urows(r.r[w], u, shard * plan.hr(w), plan.hr(w))
 
+    def slots(u, first, count):
+        buf = r.p[UNIT_WEIGHT[u]]
+        if u == SMALL:
+            return buf.at[pl.ds(first, count)]
+        col0, size = columns(u)
+        return buf.at[pl.ds(first, count), :, pl.ds(col0, size)]
+
     def ppiece(u, slot):
-        cols = columns(u)
         buf = r.p[UNIT_WEIGHT[u]]
-        return buf.at[slot] if cols is None else buf.at[slot, :, cols]
+        if u == SMALL:
+            return buf.at[slot]
+        col0, size = columns(u)
+        return buf.at[slot, :, pl.ds(col0, size)]
 
     def zpiece(u, way):
-        cols = columns(u)
         buf = (r.u, r.d)[way][UNIT_WEIGHT[u]]
-        return buf if cols is None else buf.at[:, cols]
+        if u == SMALL:
+            return buf
+        col0, size = columns(u)
+        return buf.at[:, pl.ds(col0, size)]
 
     def copy_r(u, s):
         return remote(gpiece(u, s, oc), rpiece(u, s), r.s_rs.at[u], r.s_rr.at[u], sibling)
@@ -574,10 +622,7 @@
 
     def all_p(u, step, semaphore):
         count = B - 1 if step else A - 1 if u == SMALL else (A - 1) * B
-        cols = columns(u)
-        buf = r.p[UNIT_WEIGHT[u]]
-        view = buf.at[pl.ds(0, count)] if cols is None else buf.at[pl.ds(0, count), :, cols]
-        return bytes_of(view, semaphore.at[u, step])
+        return bytes_of(slots(u, 0, count), semaphore.at[u, step])
 
     def red1(u):
         all_r(u, r.s_rr).wait()
@@ -601,7 +646,7 @@
 
         def send(t, _):
             if u == SMALL:
-                total, to = r.g8[pl.ds(pl.multiple_of(c * 8, 8), 8)], r.r[WEIGHTS]
+                total, to = gpiece(u, 0, c)[...].astype(F32), r.r[WEIGHTS]
             else:
                 to = gpiece(u, qof(c, f_ + t, g_), c)
                 total = to[...].astype(F32)
@@ -666,7 +711,7 @@
     def final_rows(u):
         w = UNIT_WEIGHT[u]
         if u == SMALL:
-            return r.o[w].at[pl.ds(pl.multiple_of(c * 8, 8), 8)]
+            return r.o[w].at[pl.ds(pl.multiple_of(c * 16, 16), 16)]
         return urows(r.o[w], u, c * plan.hr(w), plan.hr(w))
 
     def final_local(u):
@@ -706,30 +751,50 @@
             def _():
                 copy_z(u, 1).wait_send()
 
-    ahead = {}
+    def red2_hop(u):
+        red2(u)
+        red_hop(u, 0)
 
     def last_hop(u):
         red_hop(u, Z - 1)
         red_final(u)
 
+    ahead = {}
+    turns = iter(SCHEDULE)
+
     def reduce_start(*units):
         for u in units:
             red0(u)
-            ahead[u] = [red1, red1b, red2]
             if Z > 1:
-                ahead[u] += [lambda k, h=h: red_hop(k, h) for h in range(Z - 1)]
-            ahead[u].append(last_hop if Z > 1 else red_final)
-
-    def move(*units):
-        for u in units:
-            if ahead[u]:
-                ahead[u].pop(0)(u)
+                ahead[u] = [red1, red1b, red2_hop]
+                ahead[u] += [lambda k, h=h: red_hop(k, h) for h in range(1, Z - 1)]
+                ahead[u].append(last_hop)
+            else:
+                ahead[u] = [red1, red1b, red2, red_final]
+
+    def steps_of(units):
+        return [(ahead[u].pop(0), u) for u in units if ahead[u]]
+
+    def move(units):
+        for step, u in steps_of(units):
+            step(u)
+
+    def turn():
+        move(next(turns))
+
+    def turns_of(count):
+        acts = []
+        for k in range(count):
+            steps = steps_of(next(turns))
+            if steps:
+                acts.append((k, lambda steps=steps: [step(u) for step, u in steps][:0]))
+        return acts
 
     def loop(count, body, after=()):
         def step(i, _):
             body(i)
             for k, act in after:
-                pl.when(i == k)(act)
+                pl.when(i == k)(lambda act=act: (act(), None)[1])
             return 0
 
         lax.fori_loop(0, count, step, 0)
@@ -891,12 +956,14 @@
 
     def ahead_point():
         g2(POINT)
+        g0(OUT)
+
+    def ahead_qkv():
         g1(QKV)
-        g0(OUT)
-
-    loop(T // RM, left, [(1, ahead_point)])
+        g0(FIN)
+
+    loop(T // RM, left, [(0, ahead_point), (1, ahead_qkv)])
     edge_send(1, r.hid[T : T + 16], r.hid[16:32])
-    gz(POINT)
     r.hid[0:16], r.hid[T + 16 : T + 32] = edge_take(1)
 
     def depthwise(j):
@@ -909,17 +976,20 @@
                 total = total + taps[o * MB : (o + 1) * MB] * r.midp[2 + o : 3 + o, cols]
             r.sep[b * MB : (b + 1) * MB, cols] = total.astype(BF16)
 
-    def ahead_qkv():
+    def ahead_out():
         g2(QKV)
         g1(OUT)
-        g0(FIN)
-
-    def ahead_out():
+        g0(FOUT)
+
+    def ahead_fin():
         g2(OUT)
         g1(FIN)
-        g0(FOUT)
-
-    loop(FF // 256, depthwise, [(1, ahead_qkv), (5, ahead_out)])
+
+    loop(
+        FF // 256,
+        depthwise,
+        [(0, ahead_out), (2, ahead_fin), (4, lambda: gz(POINT)), (7, lambda: g2(FIN))],
+    )
     g3(POINT)
 
     def point(i):
@@ -949,7 +1019,7 @@
     kv_copy().start()
     tokens_in(r.ct, r.cot, 1)
     heads_lanes = [lane < 64, lane >= 64]
-    g2(FIN)
+    g1(FOUT)
     kv_copy().wait()
 
     def pair_cols(j, base=0):
@@ -980,7 +1050,7 @@
     loop(
         HEADS // 2,
         attend,
-        [(0, lambda: g1(FOUT)), (1, lambda: gz(FIN)), (2, lambda: g2(FOUT))],
+        [(0, lambda: gz(FIN)), (1, lambda: g2(FOUT)), (3, lambda: gz(FOUT))],
     )
     g3(OUT)
 
@@ -1001,7 +1071,7 @@
             r.hid[rows, k * CH : (k + 1) * CH] = value.astype(BF16)
             r.dg[rows, k * CH : (k + 1) * CH] = slope.astype(BF16)
 
-    loop(NB, ffn_in, [(0, lambda: gz(FOUT))])
+    loop(NB, ffn_in)
     g3(FOUT)
 
     def ffn_out(i):
@@ -1034,6 +1104,7 @@
 
     loop(FF // GC, grad_outer)
     reduce_start(U_FOUT)
+    turn()
     r.tr[...] = r.a5[...].T
 
     def grad_inner(k):
@@ -1042,7 +1113,7 @@
 
     loop(FF // GC, grad_inner)
     reduce_start(U_FIN)
-    move(U_FOUT)
+    turn()
 
     def out_back(i):
         rows = rows_of(i)
@@ -1053,6 +1124,8 @@
     loop(NB, out_back)
     r.w[OUT][...] = mm_tn(r.ctx[...], r.a5[...]).astype(BF16)
     reduce_start(U_OUT)
+    turn()
+    r.tr[...] = r.a4[...].T
 
     QB = 256
 
@@ -1103,47 +1176,60 @@
             at = pl.multiple_of(2 * D + core * 128 + what * 256, 128)
             return r.big[0:T, pl.ds(at, 128)]
 
-        r.big[0:T, cols] = part(c, 0)
-        r.big[0:T, vcols] = part(c, 1)
-        r.dg[:, cols] = part(oc, 0).astype(BF16)
-        r.dg[:, vcols] = part(oc, 1).astype(BF16)
-
-    loop(
-        HEADS // 2,
-        attend_back,
-        [
-            (0, lambda: move(U_FIN)),
-            (1, lambda: move(U_FOUT)),
-            (2, lambda: move(U_OUT)),
-            (3, lambda: move(U_FOUT, U_FOUT, U_FIN)),
-        ],
-    )
-
-    def dkv_copy():
+        for what in range(2):
+            mine = pl.ds(pl.multiple_of(j * 256 + what * 128, 128), 128)
+            r.big[0:T, mine] = part(c, what)
+            r.cot[:, pl.ds(pl.multiple_of(lax.rem(j, 2) * 256 + what * 128, 128), 128)] = part(
+                oc, what
+            ).astype(BF16)
+        dkv_copy(j).start()
+
+        @pl.when(j > 0)
+        def _():
+            pair_back(j - 1)
+
+    def dkv_copy(j):
+        slot = lax.rem(j, 2)
         return remote(
-            r.dg.at[:, pl.ds(0, 2 * D)], r.dkvr, r.s_ks.at[1], r.s_kr.at[1], sibling
+            r.cot.at[:, pl.ds(pl.multiple_of(slot * 256, 128), 256)],
+            r.dkvr.at[:, pl.ds(pl.multiple_of(j * 256, 128), 256)],
+            r.s_js.at[j],
+            r.s_jr.at[j],
+            sibling,
         )
 
-    dkv_copy().start()
-    dkv_copy().wait()
-    move(U_OUT)
+    def pair_back(j):
+        dkv_copy(j).wait()
+        both = pl.ds(pl.multiple_of(j * 256, 256), 256)
+        dkv = (r.big[0:T, both] + r.dkvr[:, both].astype(F32)).astype(BF16)
+        pair = jnp.concatenate([r.hid[0:T, pair_cols(j)], dkv], axis=1)
+        weight = jnp.concatenate([r.w[QKV][:, pair_cols(j, base)] for base in (0, D, 2 * D)], axis=1)
+        share = mm_t(pair, weight)
+
+        @pl.when(j == 0)
+        def _():
+            r.big[0:T, 3 * D : 4 * D] = share
+
+        @pl.when(j > 0)
+        def _():
+            r.big[0:T, 3 * D : 4 * D] += share
+
+        grad = mm(r.tr[...], pair)
+        r.dg[:, pl.ds(pl.multiple_of(j * 384, 128), 384)] = grad.astype(BF16)
+
+    loop(3, attend_back, turns_of(3))
+    reduce_start(U_QKV0)
+    attend_back(3)
+    turn()
+    pair_back(3)
+    reduce_start(U_QKV1)
+    turn()
 
     def qkv_back(i):
         rows = rows_of(i)
-        total = r.big[rows, 0 : 2 * D] + r.dkvr[rows].astype(F32)
-        r.hid[rows, D : 3 * D] = total.astype(BF16)
-        e = mm_t(r.hid[rows, 0 : 3 * D], r.w[QKV][...])
-        r.gs[rows] += ln_back(2, e, r.y2[rows])
+        r.gs[rows] += ln_back(2, r.big[rows, 3 * D : 4 * D], r.y2[rows])
 
     loop(NB, qkv_back)
-    r.tr[...] = r.a4[...].T
-
-    def grad_qkv(k):
-        cols = rows_of(k, GC)
-        r.w[QKV][:, cols] = mm(r.tr[...], r.hid[0:T, cols]).astype(BF16)
-
-    loop(3 * D // GC, grad_qkv)
-    reduce_start(U_QKV)
 
     def point_back(i):
         rows = rows_of(i)
@@ -1156,7 +1242,7 @@
 
     loop(NB, point_back)
     edge_send(2, r.hid[T : T + 16], r.hid[16:32])
-    move(U_FIN, U_FIN, U_QKV)
+    turn()
 
     def grad_point(k):
         cols = rows_of(k, GC)
@@ -1164,7 +1250,7 @@
 
     loop(FF // GC, grad_point)
     reduce_start(U_POINT0, U_POINT1)
-    move(U_FOUT, U_OUT, U_OUT)
+    turn()
     r.hid[0:16], r.hid[T + 16 : T + 32] = edge_take(2)
 
     def depth_back(j):
@@ -1186,18 +1272,7 @@
         for o in range(9):
             r.g8[2 + o : 3 + o, cols] = jnp.sum(sums[o], axis=0, keepdims=True)
 
-    loop(
-        FF // 256,
-        depth_back,
-        [
-            (1, lambda: move(U_POINT0)),
-            (2, lambda: move(U_POINT1)),
-            (3, lambda: move(U_OUT)),
-            (4, lambda: move(U_QKV, U_FOUT)),
-            (6, lambda: move(U_FIN)),
-            (7, lambda: move(U_POINT0, U_OUT)),
-        ],
-    )
+    loop(FF // 256, depth_back, turns_of(FF // 256))
 
     def mid_back(i):
         rows, erows = rows_of(i, RM), rows_of(i, RM, 8)
@@ -1213,22 +1288,21 @@
         right = dmid[:, 0:H] * r.dgr[rows].astype(F32)
         r.pext[0, erows] = right.astype(BF16).astype(F32)
 
-    loop(T // RM, mid_back)
+    loop(T // RM, mid_back, turns_of(T // RM))
     edge_send(3, r.pext[0, T : T + 8], r.pext[0, 8:16])
-    move(U_QKV, U_QKV, U_POINT1)
     r.tr[...] = r.a2[...].T
 
     def grad_left(k):
         cols = rows_of(k, GC)
-        r.dg[:, cols] = mm(r.tr[...], r.dgl[:, cols]).astype(BF16)
-
-    for half in range(2):
-        lax.fori_loop(
-            half * (FF // GC // 2), (half + 1) * (FF // GC // 2), lambda k, _: (grad_left(k), 0)[1], 0
-        )
-        reduce_start((U_LEFT0, U_LEFT1)[half])
-        move((U_FIN, U_FOUT)[half])
-    move(U_LEFT0, U_POINT0, U_POINT0, U_OUT)
+        r.sep[:, cols] = mm(r.tr[...], r.dgl[:, cols]).astype(BF16)
+
+    half = FF // GC // 2
+    lax.fori_loop(0, half, lambda k, _: (grad_left(k), 0)[1], 0)
+    reduce_start(U_LEFT0)
+    turn()
+    lax.fori_loop(half, 2 * half, lambda k, _: (grad_left(k), 0)[1], 0)
+    reduce_start(U_LEFT1)
+    turn()
     top, bottom = edge_take(3)
     r.pext[0, 0:8] = top
     r.pext[0, T + 8 : T + 16] = bottom
@@ -1239,6 +1313,11 @@
             if o:
                 moved = moved * jnp.concatenate([mask(-o, lo, 128)] * (H // 128), axis=1)
             r.hid[lo : lo + 128, (o + 1) * H : (o + 2) * H] = moved.astype(BF16)
+    for o in range(3):
+        cols = slice(o * H, (o + 1) * H)
+        r.dkvr[:, cols] = mm(r.tr[...], r.hid[0:T, cols]).astype(BF16)
+    reduce_start(U_CONV)
+    turn()
 
     def branch_back(i):
         rows = rows_of(i)
@@ -1247,10 +1326,7 @@
             e = e + mm_t(r.hid[rows, o * H : (o + 1) * H], r.w[CONV][o])
         r.gs[rows] += ln_back(1, e, r.y1[rows])
 
-    loop(NB, branch_back, [(0, lambda: move(U_LEFT1)), (1, lambda: move(U_LEFT0, U_POINT1, U_POINT1))])
-    for o in range(3):
-        r.w[CONV][o] = mm(r.tr[...], r.hid[0:T, o * H : (o + 1) * H]).astype(BF16)
-    reduce_start(U_CONV)
+    loop(NB, branch_back, turns_of(NB))
 
     def gate_back(i):
         rows = rows_of(i)
@@ -1266,10 +1342,12 @@
         to = pl.ds(pl.multiple_of(k * GC + 2 * D, GC), GC)
         r.hid[0:T, to] = mm(r.tr[...], r.sg[:, cols]).astype(BF16)
 
-    loop(2 * D // GC, grad_glu)
-    move(U_CONV)
-    reduce_start(U_GLU0, U_GLU1)
-    move(U_QKV)
+    lax.fori_loop(0, D // GC, lambda k, _: (grad_glu(k), 0)[1], 0)
+    reduce_start(U_GLU0)
+    turn()
+    lax.fori_loop(D // GC, 2 * D // GC, lambda k, _: (grad_glu(k), 0)[1], 0)
+    reduce_start(U_GLU1)
+    turn()
 
     def glu_back(i):
         rows = rows_of(i)
@@ -1277,16 +1355,15 @@
         total = r.gs[rows] + ln_back(0, e, r.xin[rows].astype(F32))
         r.a5[rows] = total.astype(BF16)
 
-    loop(NB, glu_back)
+    loop(NB, glu_back, turns_of(NB))
+    r.gsm[0:16] = r.g8[:, 0 : FF // 2].astype(BF16)
+    r.gsm[16:32] = r.g8[:, FF // 2 : FF].astype(BF16)
     reduce_start(SMALL)
-    move(U_GLU0, U_GLU1, SMALL, U_LEFT0, U_LEFT0, U_LEFT1, U_POINT0, U_POINT1, U_CONV)
-    move(U_LEFT1, U_LEFT1, U_GLU0, U_GLU1, SMALL, U_QKV, U_LEFT0, U_POINT0, U_CONV, U_CONV)
-    move(U_POINT1, U_GLU0, U_GLU0, U_LEFT1, U_GLU1, U_GLU1, SMALL, SMALL, U_LEFT0, U_CONV)
+    move(TAIL[0])
     tokens_out(r.a5, r.o_ig, 3)
-    move(U_GLU0, U_LEFT1, U_GLU1, SMALL, U_CONV, U_GLU0, U_GLU1, SMALL)
-    move(U_FIN, U_QKV, U_POINT0, U_POINT1, U_LEFT0, U_LEFT1, U_CONV, U_GLU0, U_GLU1, SMALL)
+    move(TAIL[1])
     while any(ahead.values()):
-        move(*range(UNITS))
+        move(range(UNITS))
 
     for u in range(UNITS):
         red_end(u)
@@ -1346,8 +1423,8 @@
     shapes = []
     plan.buffers(shapes.append)
     out_shape = [jax.ShapeDtypeStruct(inputs.shape, BF16)] * 2
-    out_shape += [jax.ShapeDtypeStruct(w.shape, BF16) for w in weights]
-    out_shape += [jax.ShapeDtypeStruct((16, plan.FF), F32)]
+    out_shape += [jax.ShapeDtypeStruct(plan.piece(w, plan.kr(w)), BF16) for w in range(WEIGHTS)]
+    out_shape += [jax.ShapeDtypeStruct((32, plan.FF // 2), BF16)]
     hbm = pl.BlockSpec(memory_space=pl.ANY)
     got = pl.pallas_call(
         lambda *refs: kernel(plan, *refs),
@@ -1384,6 +1461,8 @@
     count = 2 + WEIGHTS
     dn = plan.D // plan.n
     wide = [jax.ShapeDtypeStruct(p.shape, F32) for p in parts[:count]]
+    conv, qkv, H = 2 + CONV, 2 + QKV, plan.HALF
+    wide[conv] = jax.ShapeDtypeStruct((3, plan.kr(CONV), H), F32)
     tiny = [(4, dn), (4, dn), (1, plan.FFn), (1, plan.FFn), (9, plan.FFn)]
     out_shape = wide + [jax.ShapeDtypeStruct(shape, F32) for shape in tiny]
 
@@ -1402,18 +1481,27 @@
         for i in range(count):
             arrive(i).start()
         q = lax.axis_index("seq")
-        rolled = pltpu.roll(sums[...], (plan.FF - q * plan.FFn) % plan.FF, 1)[:, 0 : plan.FFn]
+        whole = jnp.concatenate([sums[0:16].astype(F32), sums[16:32].astype(F32)], axis=1)
+        rolled = pltpu.roll(whole, (plan.FF - q * plan.FFn) % plan.FF, 1)[:, 0 : plan.FFn]
         tinies[2][...] = rolled[0:1]
         tinies[3][...] = rolled[1:2]
         tinies[4][...] = rolled[2:11]
         for k in range(2):
-            row = sums[11 + k : 12 + k]
+            row = whole[11 + k : 12 + k]
             rows = [row[:, i * plan.D : (i + 1) * plan.D] for i in range(4)]
             both = jnp.concatenate(rows + rows, axis=0)
             tinies[k][...] = pltpu.roll(both, (plan.D - q * dn) % plan.D, 1)[0:4, 0:dn]
         for i in range(count):
             arrive(i).wait()
-            far[i][...] = near[i][...].astype(F32)
+            if i == conv:
+                for k in range(3):
+                    far[i][k] = near[i][:, k * H : (k + 1) * H].astype(F32)
+            elif i == qkv:
+                for k in range(12):
+                    to = (k % 3) * plan.D + k // 3 * 128
+                    far[i][:, to : to + 128] = near[i][:, k * 128 : (k + 1) * 128].astype(F32)
+            else:
+                far[i][...] = near[i][...].astype(F32)
             leave(i).start()
         for i in range(count):
             leave(i).wait()
@@ -1426,7 +1514,7 @@
         in_specs=[hbm] * count + [vmem],
         out_specs=[hbm] * count + [vmem] * len(tiny),
         scratch_shapes=[pltpu.VMEM(p.shape, BF16) for p in parts[:count]]
-        + [pltpu.VMEM(p.shape, F32) for p in parts[:count]]
+        + [pltpu.VMEM(shape.shape, F32) for shape in wide]
         + [pltpu.SemaphoreType.DMA((count,))] * 2,
         compiler_params=pltpu.CompilerParams(vmem_limit_bytes=64 << 20),
     )(*parts)

time: 186 us -> 182 us (0.978); the launches traced: 186 us -> 180 us
  Pallas kernels: 182 us -> 176 us
    pallas_call x1, Pallas kernels: 176 us -> 170 us  [local(): pl.pallas_call(lambda *refs: kernel(plan, *refs), out_shape=out_shape, in...]
where the time goes in v4:
time: 182 us; the launch traced here: 180 us
  Pallas kernels  176 us (97%)
    pallas_call x1, Pallas kernels, local(): pl.pallas_call(lambda *refs: kernel(plan, *refs), out_shape=out_shape, in...  170 us
    pallas_call x1, Pallas kernels, unpacked(): pl.pallas_call(body, out_shape=out_shape, in_specs=[hbm] * count + [vmem]...  6.07 us

profile of v4, /device:TPU:0, one launch (start us, length us, event | category | flops | bytes accessed | tf_op | source)
XLA Modules:
  0.0 179.9 jit_solution(3539464412264303270)
XLA Ops:
  0.6 0.0 copy-start.1
  0.7 0.7 convert_element_type.7
  1.3 0.0 copy-done.1
  1.3 0.0 copy-start.2
  1.4 0.0 copy-start.3
  1.4 0.0 copy-start.4
  1.4 0.7 copy-done.2
  2.0 0.0 copy-start
  2.0 0.0 copy-done.3
  2.0 0.0 copy-done.4
  2.1 0.6 broadcast_in_dim.12.refs_1_
  2.7 0.1 copy-done
  2.7 0.6 fusion.6.refs_3_
  3.4 170.3 %cell.1 = (bf16[2,256,512]{2,1,0:T(8,128)(2,1)}, bf16[2,256,512]{2,1,0:T(8,128)(2,1)}, bf16[128,1024]{1,0:T(8,128)(2,1)}, bf16[128,768]{1,0:T(8,128)(2,1)}, bf16...) custom-call(bf16[2,256,512]{2,1,0:T(8,128)(2,1)} %refs_0_.1, ...), custom_call_target="tpu_custom_call" | custom-call | tf_op jit(solution)/shard_map/cell/pallas_call | solution.py:1429
  173.7 6.1 %shard_map.271 = (f32[2,256,512]{2,1,0:T(8,128)}, f32[2,256,512]{2,1,0:T(8,128)}, f32[128,1024]{1,0:T(8,128)}, f32[3,128,256]{2,1,0:T(8,128)}, f32[128,2048]{1,0...) custom-call(bf16[2,256,512]{2,1,0:T(8,128)(2,1)} %get-tuple-element., ...), custom_call_target="tpu_custom_call" | custom-call | tf_op jit(solution)/shard_map/pallas_call | solution.py:1511
  (3 shorter events, 0.0 us)
Async XLA Ops:
  0.6 0.7 copy-start.1
  1.3 0.7 copy-start.2
  1.4 0.7 copy-start.3
  1.4 0.7 copy-start.4
  2.0 0.7 copy-start
